TPU v7x, 256 devices: a whole 4x4x8 slice. The times are simulated.
256 devices in a mesh: tm: 2 (over x_lo), inline: 4 (over x_hi, core), xline: 32 (over y, z).
Axes of the slice: x: 4 (x_hi: 2, x_lo: 2; x = x_hi * 2 + x_lo), y: 4, z: 8, core: 2. Of those that a mesh axis runs over, the one named last changes fastest.
Arguments:
- coef_fine: bfloat16 [2, 256, 512, 4096], P(None, 'tm', 'inline', 'xline'), may hold values from -6 to 6
- coef_coarse: bfloat16 [2, 128, 256, 2048], P(None, 'tm', 'inline', 'xline'), may hold values from -6 to 6
- kept: int32 [2, 4, 32, 6], P('tm', 'inline', 'xline'), may hold values from 0 to 15, all different within a row
- tile_offsets: int32 [2, 4, 32, 3], P('tm', 'inline', 'xline'), may hold values from 0 to 16
Outputs:
- field_block: float32 [128, 256, 2048], P('tm', 'inline', 'xline')
Inputs may be any that keep to these rules, and one draw needn't show every extreme that they name: The 6 wedges of one tile are distinct, and every wedge is kept by some tile.
All inputs are finite; a program needn't handle non-finite values.
Results may differ from a plain program's by a relative error of at most 0.0003.
Values sent between devices are 32-bit elements; how exact they have to be, the bound alone decides.
No kernel may reach another device: no remote copies, remote signals or barrier semaphores. Data moves between devices by JAX's collectives and lax.ppermute only.
A program may use at most 192 MiB of HBM per device.

v0:
```python
import math

import jax
import jax.numpy as jnp
import numpy as np
from jax import lax
from jax.experimental import pallas as pl
from jax.experimental.pallas import tpu as pltpu
from jax.sharding import PartitionSpec as P

B = 128
NW = 16
F32 = jnp.float32
BF16 = jnp.bfloat16
NTR = 104
VMEM = pltpu.VMEM
SMEM = pltpu.SMEM


def tables():
    f = np.where(np.arange(B) < B // 2, np.arange(B), np.arange(B) - B).astype(np.float64)
    theta = np.mod(np.arctan2(f[None, :], f[:, None]), np.pi)
    delta = np.pi / NW
    dist = np.mod(theta[None] - np.arange(NW)[:, None, None] * delta + np.pi / 2, np.pi) - np.pi / 2
    win = np.where(np.abs(dist) < delta, np.cos(0.5 * np.pi * dist / delta), 0.0)
    rows = np.concatenate([np.arange(0, 32), np.arange(96, 128)])
    radius = np.sqrt(np.arange(32.0)[:, None, None] ** 2 + f[rows][None, :, None] ** 2 + f[None, None, :] ** 2)
    ramp = np.clip((radius - 16.0) / 16.0, 0.0, 1.0)
    wf = np.where(ramp >= 1.0, 1.0, np.sin(0.5 * np.pi * ramp))
    wc = np.where(ramp >= 1.0, 0.0, np.cos(0.5 * np.pi * ramp))
    wf = wf.reshape(32, 4, 16, B).transpose(1, 0, 2, 3)
    wc = wc.reshape(32, 4, 16, B).transpose(1, 0, 2, 3)
    n = np.arange(B)
    p = np.where(n < 64, np.sin(np.pi * (n + 0.5) / B) ** 2, np.sin(np.pi * (B - n - 0.5) / B) ** 2)
    phase = 2 * np.pi * ((n[:, None] * n[None, :]) % B) / B
    c = np.cos(phase) * p[:, None] / math.sqrt(B)
    s = np.sin(phase) * p[:, None] / math.sqrt(B)
    e0 = np.stack([np.concatenate([c, -s], 1), np.concatenate([s, c], 1)])
    w2 = np.stack([np.concatenate([c, -s], 1).T, np.concatenate([s, c], 1).T])
    w1 = np.concatenate([c[:, :64], -s[:, :64]], 1)
    w1[:, 64] = c[:, 64]
    return [np.asarray(t, np.float32) for t in (win, wf, wc, e0, w2, w1)]


def split(x):
    hi = x.astype(BF16)
    return hi, (x - hi.astype(F32)).astype(BF16)


def dot(a, b):
    return lax.dot_general(a, b, (((1,), (0,)), ((), ())), preferred_element_type=F32)


def rows_of(table, offset):
    rolled = pltpu.roll(table, offset, 0)
    row = lax.broadcasted_iota(jnp.int32, (16, table.shape[1]), 0)
    shared = rolled[0:16]
    above = jnp.concatenate([rolled[104:128], jnp.where(row < offset, shared, 0.0)], axis=0)
    below = jnp.concatenate([jnp.where(row >= offset, shared, 0.0), rolled[16:40]], axis=0)
    return rolled[40:104], above, below


def transform_kernel(
    sc, fine, coarse, win, wf, wc, e0t, w2t, w1t, rim_out, rhs_out, wco_out,
    stage, xhi, xlo, pq, ang, e0, w2, wm,
):
    step = pl.program_id(0)
    o0, o1, o2, tm, odd = sc[0], sc[1], sc[2], sc[3], sc[4]

    @pl.when(step == 0)
    def _():
        total = win[sc[5]]
        for i in range(1, 6):
            total = total + win[sc[5 + i]]
        ang[...] = total
        parts = []
        for c in range(2):
            own, above, below = rows_of(e0t[c], o0)
            parts += [own, jnp.where(tm == 0, above, below)]
        hi, lo = split(jnp.concatenate(parts, axis=0))
        e0[0] = hi
        e0[1] = lo
        for c in range(2):
            hi, lo = split(pltpu.roll(w2t[c], o2 + 88, 1))
            w2[c] = jnp.concatenate([hi, lo], axis=1)
        own, above, below = rows_of(w1t[...], o1)
        mutual = jnp.where(odd == 0, above, below)
        outer = jnp.where(odd == 0, below, above)
        hi, lo = split(mutual)
        hi, lo = hi.astype(F32), lo.astype(F32)
        wm[...] = jnp.concatenate(
            [jnp.concatenate([hi, hi], axis=1), jnp.concatenate([lo, jnp.zeros_like(lo)], axis=1)], axis=0
        ).astype(BF16)
        hi, lo = split(jnp.concatenate([own, outer], axis=0))
        hi, lo = hi.astype(F32), lo.astype(F32)
        wco_out[...] = jnp.concatenate(
            [jnp.concatenate([hi, hi], axis=1), jnp.concatenate([lo, jnp.zeros_like(lo)], axis=1)], axis=0
        ).astype(BF16)

    inner = (step < 2) | ((step >= 6) & (step < 8))

    @pl.when(inner)
    def _():
        a = ang[pl.ds(pl.multiple_of(step * 16, 16), 16), :]
        row = lax.broadcasted_iota(jnp.int32, (16, B), 0)
        a = jnp.where((step == 6) & (row == 0), 1.0, a)

        def plane(k0, j0, radial, coarse_w):
            for c in range(2):
                small = coarse[c, j0].astype(F32)
                small = jnp.concatenate([small, small], axis=1)
                stage[c * B + k0] = (a * radial) * fine[c, k0].astype(F32) + coarse_w * small

        plane(0, 0, wf[0, 0], wc[0, 0])

        def low(q, _):
            radial = wf[0, q]
            coarse_w = wc[0, q]
            plane(q, q, radial, coarse_w)
            plane(B - q, 64 - q, radial, coarse_w)
            return 0

        lax.fori_loop(1, 32, low, 0)

        def high(k0, _):
            for c in range(2):
                stage[c * B + k0] = a * fine[c, k0].astype(F32)
            return 0

        lax.fori_loop(32, 97, high, 0)
        base = step * 16
        base_lo = jnp.where(step < 2, step * 16, step * 16 - 64)
        for r in range(16):
            hi, lo = split(stage[:, r, :])
            xhi[base + r] = hi
            xlo[base_lo + r] = lo

    @pl.when((step >= 2) & (step < 6))
    def _():
        def every(k0, _):
            for c in range(2):
                stage[c * B + k0] = fine[c, k0].astype(F32)
            return 0

        lax.fori_loop(0, B, every, 0)
        for r in range(16):
            xhi[step * 16 + r] = stage[:, r, :].astype(BF16)

    def along_xline(even, odd_part, j):
        for which, pair in ((0, even), (1, odd_part)):
            wide = [jnp.concatenate([g[:NTR], g[NTR:]], axis=1) for g in pair]
            hi, lo = split(jnp.concatenate(wide, axis=0))
            out = dot(hi, w2[which])
            out = out[:, :B] + out[:, B:] + dot(lo, w2[which, :, :B])
            pq[which * 64 + j] = out[:NTR]
            pq[which * 64 + j + 1] = out[NTR:]

    def first(k, kk, lo_pair):
        hi = jnp.concatenate([xhi[k], xhi[kk]], axis=1)
        out = dot(e0[0], hi) + dot(e0[1], hi)
        if lo_pair is not None:
            out = out + dot(e0[0], jnp.concatenate(lo_pair, axis=1))
        return out

    def inner_pair(j):
        out = first(j, B - j, (xlo[j], xlo[64 - j]))
        return out[:, :B] + out[:, B:], out[:, :B] - out[:, B:]

    @pl.when(step == 8)
    def _():
        out = first(0, 64, (xlo[0], jnp.zeros((256, B), BF16)))
        half = out[:, B:] * ang[64:65, :]
        even0 = out[:, :B]
        odd0 = jnp.concatenate([-half[NTR:], half[:NTR]], axis=0)
        even1, odd1 = inner_pair(1)
        along_xline((even0, even1), (odd0, odd1), 0)

        def near(i, _):
            ea, oa = inner_pair(2 * i)
            eb, ob = inner_pair(2 * i + 1)
            along_xline((ea, eb), (oa, ob), 2 * i)
            return 0

        lax.fori_loop(1, 16, near, 0)

        def outer_pair(j):
            out = first(j, B - j, None)
            a = out[:, :B] * ang[pl.ds(j, 1), :]
            b = out[:, B:] * ang[pl.ds(B - j, 1), :]
            return a + b, a - b

        def far(i, _):
            ea, oa = outer_pair(2 * i)
            eb, ob = outer_pair(2 * i + 1)
            along_xline((ea, eb), (oa, ob), 2 * i)
            return 0

        lax.fori_loop(16, 32, far, 0)
        rim_out[13 * 8 : 14 * 8] = jnp.full((8, 40, B), o2.astype(F32), F32)

    @pl.when(step >= 9)
    def _():
        n0 = (step - 9) * 8
        for pair in range(4):
            x = jnp.concatenate([pq[:, n0 + 2 * pair, :], pq[:, n0 + 2 * pair + 1, :]], axis=1)
            hi, lo = split(x)
            rhs = jnp.concatenate([hi, lo], axis=0)
            rhs_out[pair] = rhs
            out = dot(wm[...], rhs)
            out = out[:40] + out[40:]
            rim_out[n0 + 2 * pair] = out[:, :B]
            rim_out[n0 + 2 * pair + 1] = out[:, B:]


def transform(scalars, fine, coarse, tabs):
    def edge(s):
        return jnp.where(s < 2, s, jnp.clip(s - 4, 2, 3))

    whole = pl.BlockSpec(memory_space=VMEM)
    return pl.pallas_call(
        transform_kernel,
        grid=(22,),
        in_specs=[
            pl.BlockSpec(memory_space=SMEM),
            pl.BlockSpec((2, B, 16, B), lambda s: (0, 0, jnp.minimum(s, 7), 0)),
            pl.BlockSpec((2, 64, 16, 64), lambda s: (0, 0, edge(s), 0)),
            whole,
            pl.BlockSpec((1, 32, 16, B), lambda s: (edge(s), 0, 0, 0)),
            pl.BlockSpec((1, 32, 16, B), lambda s: (edge(s), 0, 0, 0)),
            whole,
            whole,
            whole,
        ],
        out_specs=[
            whole,
            pl.BlockSpec((4, 256, 256), lambda s: (jnp.maximum(s - 9, 0), 0, 0)),
            whole,
        ],
        out_shape=[
            jax.ShapeDtypeStruct((NTR + 8, 40, B), F32),
            jax.ShapeDtypeStruct((NTR // 2, 256, 256), BF16),
            jax.ShapeDtypeStruct((208, 256), BF16),
        ],
        scratch_shapes=[
            VMEM((256, 16, B), F32),
            VMEM((B, 256, B), BF16),
            VMEM((64, 256, B), BF16),
            VMEM((B, NTR, B), F32),
            VMEM((B, B), F32),
            VMEM((2, 208, 256), BF16),
            VMEM((2, 256, 256), BF16),
            VMEM((80, 256), BF16),
        ],
        compiler_params=pltpu.CompilerParams(
            dimension_semantics=("arbitrary",), vmem_limit_bytes=50 * 2**20
        ),
        cost_estimate=pl.CostEstimate(flops=2 * 10**10, bytes_accessed=30 * 10**6, transcendentals=0),
    )(scalars, fine, coarse, *tabs)


def own_rows_kernel(rhs, wco, out):
    for pair in range(4):
        x = dot(wco[...], rhs[pair])
        x = x[:NTR] + x[NTR:]
        out[2 * pair] = x[:, :B]
        out[2 * pair + 1] = x[:, B:]


def own_rows(rhs, wco):
    return pl.pallas_call(
        own_rows_kernel,
        grid=(13,),
        in_specs=[pl.BlockSpec((4, 256, 256), lambda s: (s, 0, 0)), pl.BlockSpec(memory_space=VMEM)],
        out_specs=pl.BlockSpec((8, NTR, B), lambda s: (s, 0, 0)),
        out_shape=jax.ShapeDtypeStruct((NTR, NTR, B), F32),
        compiler_params=pltpu.CompilerParams(dimension_semantics=("arbitrary",), vmem_limit_bytes=32 * 2**20),
        cost_estimate=pl.CostEstimate(flops=52 * 2 * 208 * 256 * 256, bytes_accessed=14 * 10**6, transcendentals=0),
    )(rhs, wco)


def lanes():
    return lax.broadcasted_iota(jnp.int32, (8, B), 1)


def two_sides(value, offset):
    lane = lanes()
    return jnp.where(lane < 88 + offset, value, 0.0), jnp.where(lane >= 88 + offset, value, 0.0)


def turn(value, shift):
    shift = shift % B
    return value if shift == 0 else pltpu.roll(value, shift, 1)


def pack3(pieces, start):
    lane = lanes()
    out = turn(pieces[0], -start)
    for i in range(1, len(pieces)):
        out = jnp.where(lane < 40 * i, out, turn(pieces[i], 40 * i - start))
    return out


def unpack3(packed, place, start):
    lane = lanes()
    value = turn(packed, start - 40 * place)
    return jnp.where((lane >= start) & (lane < start + 40), value, 0.0)


def merged(co, rim, t, b, sc):
    near, far = two_sides(co[t, 8 * b : 8 * b + 8, :], sc[2])
    if b < 8:
        shift = jnp.where(sc[4] == 0, 3, 0)
        place = b - shift
        valid = (place >= 0) & (place < 5)
        place = jnp.clip(place, 0, 4)
        other = rim[t, pl.ds(pl.multiple_of(place * 8, 8), 8), :]
        other = jnp.where(valid, other, 0.0)
        near2, far2 = two_sides(other, sc[11])
        near, far = near + near2, far + far2
    return near, far


def pack_many(pieces, out, start):
    for g in range(14):
        out[g] = pack3(pieces[3 * g : 3 * g + 3], start)


def pack_kernel(sc, co, rim, zhc, zlc, zho, zlo, tmsg):
    step = pl.program_id(0)
    outer_h, outer_l = [], []
    for t in range(8):
        parts = [merged(co, rim, t, b, sc) for b in range(3)]
        zhc[t] = pack3([x[0] for x in parts], 64)
        zlc[t] = pack3([x[1] for x in parts], 88)
        for b in range(8, 13):
            near, far = merged(co, rim, t, b, sc)
            outer_h.append(near)
            outer_l.append(far)
    pack_many(outer_h, zho, 64)
    pack_many(outer_l, zlo, 88)

    @pl.when(step >= 8)
    def _():
        lane = lanes()
        for t in range(8):
            extra = None
            for b in range(3, 8):
                near, far = merged(co, rim, t, b, sc)
                tmsg[t * 5 + b - 3] = jnp.where(lane < 104, near, far)
                moved = turn(far, 16 * (b - 3) - 88)
                extra = moved if extra is None else jnp.where(lane < 16 * (b - 3), extra, moved)
            tmsg[40 + t] = extra


def pack(sc, co, rim):
    return pl.pallas_call(
        pack_kernel,
        grid=(13,),
        in_specs=[
            pl.BlockSpec(memory_space=SMEM),
            pl.BlockSpec((8, NTR, B), lambda s: (s, 0, 0)),
            pl.BlockSpec((8, 40, B), lambda s: (s, 0, 0)),
        ],
        out_specs=[
            pl.BlockSpec((8, 8, B), lambda s: (s, 0, 0)),
            pl.BlockSpec((8, 8, B), lambda s: (s, 0, 0)),
            pl.BlockSpec((14, 8, B), lambda s: (s, 0, 0)),
            pl.BlockSpec((14, 8, B), lambda s: (s, 0, 0)),
            pl.BlockSpec((48, 8, B), lambda s: (jnp.maximum(s - 8, 0), 0, 0)),
        ],
        out_shape=[
            jax.ShapeDtypeStruct((NTR, 8, B), F32),
            jax.ShapeDtypeStruct((NTR, 8, B), F32),
            jax.ShapeDtypeStruct((13 * 14, 8, B), F32),
            jax.ShapeDtypeStruct((13 * 14, 8, B), F32),
            jax.ShapeDtypeStruct((5 * 48, 8, B), F32),
        ],
        compiler_params=pltpu.CompilerParams(dimension_semantics=("arbitrary",), vmem_limit_bytes=32 * 2**20),
        cost_estimate=pl.CostEstimate(flops=10**7, bytes_accessed=11 * 10**6, transcendentals=0),
    )(sc, co, rim)


def middle_kernel(sc, co, rim, zhc, zlc, zho, zlo, tmsg, own1, tmc, tmo, zh2, zl2, own2):
    step = pl.program_id(0)
    lane = lanes()

    def first_rows(t, b):
        near, _ = merged(co, rim, t, b, sc)
        if b < 3:
            low, high = unpack3(zhc[t], b, 0), unpack3(zlc[t], b, 24)
        else:
            q = t * 5 + b - 8
            low, high = unpack3(zho[q // 3], q % 3, 0), unpack3(zlo[q // 3], q % 3, 24)
        return near + low + high

    blocks = [0, 1, 2, 8, 9, 10, 11, 12]

    @pl.when(step >= 8)
    def _():
        for t in range(4):
            for i, b in enumerate(blocks):
                both = jnp.where(lane < 64, first_rows(t, b), turn(first_rows(t + 4, b), 64))
                if b < 3:
                    tmc[t * 3 + i] = both
                else:
                    tmo[t * 5 + i - 3] = both

    @pl.when(step < 8)
    def _():
        for t in range(8):
            for i, b in enumerate(blocks):
                own1[t, 8 * i : 8 * i + 8, :] = first_rows(t, b)
        place = step - jnp.where(sc[3] == 0, 3, 0)
        valid = (place >= 0) & (place < 5)
        base = jnp.clip(place, 0, 4) * 48
        ahead, behind = [], []
        for t in range(8):
            extra = tmsg[base + 40 + t]
            for b in range(3, 8):
                near, far = merged(co, rim, t, b, sc)
                main = tmsg[base + t * 5 + b - 3]
                moved = turn(extra, 88 - 16 * (b - 3))
                near = near + jnp.where(valid & (lane < 104), main, 0.0)
                far2 = jnp.where(lane >= 104, main, jnp.where(lane >= 88, moved, 0.0))
                far = far + jnp.where(valid, far2, 0.0)
                ahead.append(near)
                behind.append(far)
                own2[t, 8 * (b - 3) : 8 * (b - 3) + 8, :] = near
        pack_many(ahead, zh2, 64)
        pack_many(behind, zl2, 88)


def middle(sc, co, rim, zhc, zlc, zho, zlo, tmsg):
    def core(s):
        return (jnp.minimum(s, 7), 0, 0)

    def edge(s):
        return (jnp.maximum(s - 8, 0), 0, 0)

    def each(s):
        return (s, 0, 0)

    return pl.pallas_call(
        middle_kernel,
        grid=(13,),
        in_specs=[
            pl.BlockSpec(memory_space=SMEM),
            pl.BlockSpec((8, NTR, B), each),
            pl.BlockSpec((8, 40, B), each),
            pl.BlockSpec((8, 8, B), each),
            pl.BlockSpec((8, 8, B), each),
            pl.BlockSpec((14, 8, B), each),
            pl.BlockSpec((14, 8, B), each),
            pl.BlockSpec(memory_space=VMEM),
        ],
        out_specs=[
            pl.BlockSpec((8, 64, B), core),
            pl.BlockSpec((12, 8, B), edge),
            pl.BlockSpec((20, 8, B), edge),
            pl.BlockSpec((14, 8, B), core),
            pl.BlockSpec((14, 8, B), core),
            pl.BlockSpec((8, 40, B), core),
        ],
        out_shape=[
            jax.ShapeDtypeStruct((64, 64, B), F32),
            jax.ShapeDtypeStruct((60, 8, B), F32),
            jax.ShapeDtypeStruct((100, 8, B), F32),
            jax.ShapeDtypeStruct((8 * 14, 8, B), F32),
            jax.ShapeDtypeStruct((8 * 14, 8, B), F32),
            jax.ShapeDtypeStruct((64, 40, B), F32),
        ],
        compiler_params=pltpu.CompilerParams(dimension_semantics=("arbitrary",), vmem_limit_bytes=32 * 2**20),
        cost_estimate=pl.CostEstimate(flops=10**7, bytes_accessed=16 * 10**6, transcendentals=0),
    )(sc, co, rim, zhc, zlc, zho, zlo, tmsg)


def late_kernel(sc, own1, tmc, tmo, zh2, zl2, own2, block, dmsg):
    step = pl.program_id(0)
    lane = lanes()
    place = step - jnp.where(sc[3] == 0, 3, 0)
    valid = (place >= 0) & (place < 5)
    place = jnp.clip(place, 0, 4)

    def first_rows(t, i):
        index = place * 4 + t % 4
        both = tmc[index * 3 + i] if i < 3 else tmo[index * 5 + i - 3]
        both = both if t < 4 else turn(both, 64)
        return own1[t, 8 * i : 8 * i + 8, :] + jnp.where(valid, both, 0.0)

    for t in range(8):
        for i in range(3):
            block[t, 8 * i : 8 * i + 8, :] = first_rows(t, i)
        for i in range(5):
            q = t * 5 + i
            low, high = unpack3(zh2[q // 3], q % 3, 0), unpack3(zl2[q // 3], q % 3, 24)
            block[t, 24 + 8 * i : 32 + 8 * i, :] = own2[t, 8 * i : 8 * i + 8, :] + low + high
    for t in range(4):
        for i in range(3, 8):
            dmsg[t * 5 + i - 3] = jnp.where(lane < 64, first_rows(t, i), turn(first_rows(t + 4, i), 64))


def late(sc, own1, tmc, tmo, zh2, zl2, own2):
    def each(s):
        return (s, 0, 0)

    whole = pl.BlockSpec(memory_space=VMEM)
    return pl.pallas_call(
        late_kernel,
        grid=(8,),
        in_specs=[
            pl.BlockSpec(memory_space=SMEM),
            pl.BlockSpec((8, 64, B), each),
            whole,
            whole,
            pl.BlockSpec((14, 8, B), each),
            pl.BlockSpec((14, 8, B), each),
            pl.BlockSpec((8, 40, B), each),
        ],
        out_specs=[pl.BlockSpec((8, 64, B), each), pl.BlockSpec((20, 8, B), each)],
        out_shape=[
            jax.ShapeDtypeStruct((64, 64, B), F32),
            jax.ShapeDtypeStruct((160, 8, B), F32),
        ],
        compiler_params=pltpu.CompilerParams(dimension_semantics=("arbitrary",), vmem_limit_bytes=32 * 2**20),
        cost_estimate=pl.CostEstimate(flops=10**7, bytes_accessed=7 * 10**6, transcendentals=0),
    )(sc, own1, tmc, tmo, zh2, zl2, own2)


def last_kernel(sc, block, dmsg, out):
    shift = jnp.where(sc[4] == 0, 0, 3)
    for t in range(8):
        for b in range(8):
            place = b - shift
            valid = (place >= 0) & (place < 5)
            other = dmsg[(t % 4) * 5 + jnp.clip(place, 0, 4)]
            other = other if t < 4 else turn(other, 64)
            value = block[t, 8 * b : 8 * b + 8, :] + jnp.where(valid, other, 0.0)
            out[t, 8 * b : 8 * b + 8, :] = value[:, :64]


def last(sc, block, dmsg):
    def each(s):
        return (s, 0, 0)

    return pl.pallas_call(
        last_kernel,
        grid=(8,),
        in_specs=[
            pl.BlockSpec(memory_space=SMEM),
            pl.BlockSpec((8, 64, B), each),
            pl.BlockSpec((20, 8, B), each),
        ],
        out_specs=pl.BlockSpec((8, 64, 64), each),
        out_shape=jax.ShapeDtypeStruct((64, 64, 64), F32),
        compiler_params=pltpu.CompilerParams(dimension_semantics=("arbitrary",), vmem_limit_bytes=32 * 2**20),
        cost_estimate=pl.CostEstimate(flops=10**6, bytes_accessed=5 * 10**6, transcendentals=0),
    )(sc, block, dmsg)


def local(coef_fine, coef_coarse, kept, tile_offsets):
    tabs = [jnp.asarray(t) for t in tables()]
    n_tm, n_in, n_x = (lax.axis_size(a) for a in ("tm", "inline", "xline"))
    tm = lax.axis_index("tm").astype(jnp.int32)
    odd = (lax.axis_index("inline") % 2).astype(jnp.int32)
    sc = jnp.concatenate([tile_offsets.reshape(3), jnp.stack([tm, odd]), kept.reshape(6)])

    along = [(i, i + 1) for i in range(n_x - 1)]
    back = [(b, a) for a, b in along]
    inner = range(1, n_in - 1)
    along_o = [(i * n_x + a, i * n_x + b) for i in inner for a, b in along]
    back_o = [(b, a) for a, b in along_o]
    times = [(0, 1), (1, 0)]
    times_o = [(a * n_in + i, b * n_in + i) for i in inner for a, b in times]
    mates = [(i, i ^ 1) for i in range(n_in)]
    outer = [p for i in range(1, n_in - 1, 2) for p in ((i, i + 1), (i + 1, i))]

    rim, rhs, wco = transform(sc, coef_fine, coef_coarse, tabs)
    rim = lax.ppermute(rim, "inline", mates)
    co = own_rows(rhs, wco)
    other = rim[NTR, 0, 0].astype(jnp.int32)
    sc = jnp.concatenate([sc, other[None]])

    zhc, zlc, zho, zlo, tmsg = pack(sc, co, rim)
    tmsg = lax.ppermute(tmsg, "tm", times)
    zho = lax.ppermute(zho, ("inline", "xline"), along_o)
    zlo = lax.ppermute(zlo, ("inline", "xline"), back_o)
    zhc = lax.ppermute(zhc, "xline", along)
    zlc = lax.ppermute(zlc, "xline", back)
    own1, tmc, tmo, zh2, zl2, own2 = middle(sc, co, rim, zhc, zlc, zho, zlo, tmsg)
    tmo = lax.ppermute(tmo, ("tm", "inline"), times_o)
    tmc = lax.ppermute(tmc, "tm", times)
    zh2 = lax.ppermute(zh2, "xline", along)
    zl2 = lax.ppermute(zl2, "xline", back)
    block, dmsg = late(sc, own1, tmc, tmo, zh2, zl2, own2)
    dmsg = lax.ppermute(dmsg, "inline", outer)
    return last(sc, block, dmsg)


def solution(mesh):
    in_specs = (
        P(None, "tm", "inline", "xline"),
        P(None, "tm", "inline", "xline"),
        P("tm", "inline", "xline", None),
        P("tm", "inline", "xline", None),
    )
    out_specs = P("tm", "inline", "xline")
    return jax.shard_map(local, mesh=mesh, in_specs=in_specs, out_specs=out_specs, check_vma=False)
```

profile of v0, /device:TPU:27, one launch (start us, length us, event | category | flops | bytes accessed | tf_op | source)
XLA Modules:
  0.0 173.5 jit_solution(9075166209027861654)
XLA Ops:
  0.0 0.7 pad_add_fusion.sc
  0.8 1.2 copy-done.3
  2.0 1.2 copy-done.4
  3.2 1.2 copy-done.5
  4.4 0.9 copy-done.6
  5.4 0.9 copy-done.7
  6.3 0.8 copy-done.8
  7.2 74.7 %shard_map.100 = (f32[112,40,128]{2,1,0:T(8,128)}, bf16[52,256,256]{2,1,0:T(8,128)(2,1)}, bf16[208,256]{1,0:T(8,128)(2,1)S(1)}) custom-call(s32[11]{0:T(128)S(1)} %pad_add_fusion.sc, bf16[2,128,128,128]{3,2,1,0:T(8,128)(2,1)} %fine.1, bf16[2,64,64,64]{3,2,1,0:T(8,128)(2,1)} %coarse.1, f32[16,128,128]{2,1,0:T(8,128)S(1)} %copy-done.5, ...), custom_call_target="tpu_custom_call" | custom-call | flops 20000000000 | bytes 30000000 | tf_op jit(solution)/shard_map/pallas_call | solution.py:220
  81.9 0.7 collective-permute-start
  82.6 2.9 %copy-done.2 = bf16[52,256,256]{2,1,0:T(8,128)(2,1)S(1)} copy-done((bf16[52,256,256]{2,1,0:T(8,128)(2,1)S(1)}, bf16[52,256,256]{2,1,0:T(8,128)(2,1)}, u32[]{:S(2)}) %copy-start.2) | copy-done | bytes 6815768
  85.5 3.8 %shard_map.101.co = f32[104,104,128]{2,1,0:T(8,128)S(1)} custom-call(bf16[52,256,256]{2,1,0:T(8,128)(2,1)S(1)} %copy-done.2, bf16[208,256]{1,0:T(8,128)(2,1)S(1)} %get-tuple-element.23.wco), custom_call_target="tpu_custom_call" | custom-call | flops 1417674752 | bytes 14000000 | tf_op jit(solution)/shard_map/pallas_call | solution.py:270
  89.3 2.4 %copy-done = f32[104,104,128]{2,1,0:T(8,128)} copy-done((f32[104,104,128]{2,1,0:T(8,128)}, f32[104,104,128]{2,1,0:T(8,128)S(1)}, u32[]{:S(2)}) %copy-start) | copy-done | bytes 5537816
  91.7 0.5 slice.4
  92.9 2.6 %copy-done.1 = f32[104,104,128]{2,1,0:T(8,128)S(1)} copy-done((f32[104,104,128]{2,1,0:T(8,128)S(1)}, f32[104,104,128]{2,1,0:T(8,128)}, u32[]{:S(2)}) %copy-start.1) | copy-done | bytes 5537816
  95.4 4.2 %shard_map.102 = (f32[104,8,128]{2,1,0:T(8,128)S(1)}, f32[104,8,128]{2,1,0:T(8,128)S(1)}, f32[182,8,128]{2,1,0:T(8,128)S(1)}, f32[182,8,128]{2,1,0:T(8,128)S(1)}, f32[240,8,128]{2,1,0:T(8,128)S(1)}) custom-call(s32[12]{0:T(128)S(1)} %concatenate.8.sc, f32[104,104,128]{2,1,0:T(8,128)S(1)} %copy-done.1, f32[112,40,128]{2,1,0:T(8,128)S(1)} %collective-permute-done.rim), custom_call_target="tpu_custom_call" | custom-call | flops 10000000 | bytes 11000000 | tf_op jit(solution)/shard_map/pallas_call | solution.py:356
  99.7 0.3 collective-permute-start.5
  100.0 3.5 %collective-permute-start.3 = (f32[182,8,128]{2,1,0:T(8,128)S(1)}, f32[182,8,128]{2,1,0:T(8,128)S(1)}, u32[]{:S(2)}, u32[]{:S(2)}) collective-permute-start(f32[182,8,128]{2,1,0:T(8,128)S(1)} %get-tuple-element.26), channel_id=1, source_target_pairs={{32,33},{33,34},{34,35},{35,36},{36,37},{37,38},{38,39},{39,40},{4... | collective-permute-start | bytes 2236424 | tf_op jit(solution)/shard_map/ppermute | solution.py:585
  103.5 6.0 %collective-permute-start.4 = (f32[182,8,128]{2,1,0:T(8,128)S(1)}, f32[182,8,128]{2,1,0:T(8,128)S(1)}, u32[]{:S(2)}, u32[]{:S(2)}) collective-permute-start(f32[182,8,128]{2,1,0:T(8,128)S(1)} %get-tuple-element.27), channel_id=1, source_target_pairs={{33,32},{34,33},{35,34},{36,35},{37,36},{38,37},{39,38},{40,39},{4... | collective-permute-start | bytes 2236424 | tf_op jit(solution)/shard_map/ppermute | solution.py:586
  109.6 1.9 %collective-permute-start.1 = (f32[104,8,128]{2,1,0:T(8,128)S(1)}, f32[104,8,128]{2,1,0:T(8,128)S(1)}, u32[]{:S(2)}, u32[]{:S(2)}) collective-permute-start(f32[104,8,128]{2,1,0:T(8,128)S(1)} %get-tuple-element.24), channel_id=1, source_target_pairs={{0,1},{1,2},{2,3},{3,4},{4,5},{5,6},{6,7},{7,8},{8,9},{9,10},{10,1... | collective-permute-start | bytes 1277960 | tf_op jit(solution)/shard_map/ppermute | solution.py:587
  111.5 5.5 %collective-permute-start.2 = (f32[104,8,128]{2,1,0:T(8,128)S(1)}, f32[104,8,128]{2,1,0:T(8,128)S(1)}, u32[]{:S(2)}, u32[]{:S(2)}) collective-permute-start(f32[104,8,128]{2,1,0:T(8,128)S(1)} %get-tuple-element.25), channel_id=1, source_target_pairs={{1,0},{2,1},{3,2},{4,3},{5,4},{6,5},{7,6},{8,7},{9,8},{10,9},{11,1... | collective-permute-start | bytes 1277960 | tf_op jit(solution)/shard_map/ppermute | solution.py:588
  117.0 8.7 %collective-permute-done.1.zhc = f32[104,8,128]{2,1,0:T(8,128)S(1)} collective-permute-done((f32[104,8,128]{2,1,0:T(8,128)S(1)}, f32[104,8,128]{2,1,0:T(8,128)S(1)}, u32[]{:S(2)}, u32[]{:S(2)}) %collective-permute-start.1) | collective-permute-done | bytes 426016 | tf_op jit(solution)/shard_map/ppermute | solution.py:587
  125.7 1.5 collective-permute-done.2.zlc
  127.2 5.7 %shard_map.103 = (f32[64,64,128]{2,1,0:T(8,128)S(1)}, f32[60,8,128]{2,1,0:T(8,128)S(1)}, f32[100,8,128]{2,1,0:T(8,128)S(1)}, f32[112,8,128]{2,1,0:T(8,128)S(1)},...) custom-call(s32[12]{0:T(128)S(1)} %concatenate.8.sc, f32[104,104,128]{2,1,0:T(8,128)S(1)} %copy-done.1, ...), custom_call_target="tpu_custom_call" | custom-call | flops 10000000 | bytes 16000000 | tf_op jit(solution)/shard_map/pallas_call | solution.py:443
  132.9 1.9 %collective-permute-start.8 = (f32[112,8,128]{2,1,0:T(8,128)S(1)}, f32[112,8,128]{2,1,0:T(8,128)S(1)}, u32[]{:S(2)}, u32[]{:S(2)}) collective-permute-start(f32[112,8,128]{2,1,0:T(8,128)S(1)} %get-tuple-element.32), channel_id=1, source_target_pairs={{0,1},{1,2},{2,3},{3,4},{4,5},{5,6},{6,7},{7,8},{8,9},{9,10},{10,1... | collective-permute-start | bytes 1376264 | tf_op jit(solution)/shard_map/ppermute | solution.py:592
  134.8 5.9 %collective-permute-start.9 = (f32[112,8,128]{2,1,0:T(8,128)S(1)}, f32[112,8,128]{2,1,0:T(8,128)S(1)}, u32[]{:S(2)}, u32[]{:S(2)}) collective-permute-start(f32[112,8,128]{2,1,0:T(8,128)S(1)} %get-tuple-element.33), channel_id=1, source_target_pairs={{1,0},{2,1},{3,2},{4,3},{5,4},{6,5},{7,6},{8,7},{9,8},{10,9},{11,1... | collective-permute-start | bytes 1376264 | tf_op jit(solution)/shard_map/ppermute | solution.py:593
  140.8 3.1 %collective-permute-start.7 = (f32[100,8,128]{2,1,0:T(8,128)S(1)}, f32[100,8,128]{2,1,0:T(8,128)S(1)}, u32[]{:S(2)}, u32[]{:S(2)}) collective-permute-start(f32[100,8,128]{2,1,0:T(8,128)S(1)} %get-tuple-element.31), channel_id=1, source_target_pairs={{32,160},{160,32},{64,192},{192,64},{33,161},{161,33},{65,193},{19... | collective-permute-start | bytes 1228808 | tf_op jit(solution)/shard_map/ppermute | solution.py:590
  143.9 0.3 collective-permute-start.6
  144.2 8.5 %collective-permute-done.6.tmc = f32[60,8,128]{2,1,0:T(8,128)S(1)} collective-permute-done((f32[60,8,128]{2,1,0:T(8,128)S(1)}, f32[60,8,128]{2,1,0:T(8,128)S(1)}, u32[]{:S(2)}, u32[]{:S(2)}) %collective-permute-start.6) | collective-permute-done | bytes 245792 | tf_op jit(solution)/shard_map/ppermute | solution.py:591
  152.8 2.4 %shard_map.104 = (f32[64,64,128]{2,1,0:T(8,128)S(1)}, f32[160,8,128]{2,1,0:T(8,128)S(1)}) custom-call(s32[12]{0:T(128)S(1)} %concatenate.8.sc, f32[64,64,128]{2,1,0:T(8,128)S(1)} %get-tuple-element.29.own1, f32[60,8,128]{2,1,0:T(8,128)S(1)} %collective-permute-done.6.tmc, f32[100,8,128]{2,1,0:T(8,128)S(1)} %collective-permute-done.7.tmo, ...), custom_call_target="tpu_custom_call" | custom-call | flops 10000000 | bytes 7000000 | tf_op jit(solution)/shard_map/pallas_call | solution.py:507
  155.2 6.1 %collective-permute-start.10 = (f32[160,8,128]{2,1,0:T(8,128)S(1)}, f32[160,8,128]{2,1,0:T(8,128)S(1)}, u32[]{:S(2)}, u32[]{:S(2)}) collective-permute-start(f32[160,8,128]{2,1,0:T(8,128)S(1)} %get-tuple-element.36), channel_id=1, source_target_pairs={{32,64},{64,32},{33,65},{65,33},{34,66},{66,34},{35,67},{67,35},{3... | collective-permute-start | bytes 1966088 | tf_op jit(solution)/shard_map/ppermute | solution.py:595
  161.3 8.3 %collective-permute-done.10.dmsg = f32[160,8,128]{2,1,0:T(8,128)S(1)} collective-permute-done((f32[160,8,128]{2,1,0:T(8,128)S(1)}, f32[160,8,128]{2,1,0:T(8,128)S(1)}, u32[]{:S(2)}, u32[]{:S(2)}) %collective-permute-start.10) | collective-permute-done | bytes 655392 | tf_op jit(solution)/shard_map/ppermute | solution.py:595
  169.6 3.9 %shard_map.105 = f32[64,64,64]{2,1,0:T(8,128)} custom-call(s32[12]{0:T(128)S(1)} %concatenate.8.sc, f32[64,64,128]{2,1,0:T(8,128)S(1)} %get-tuple-element.35.block, f32[160,8,128]{2,1,0:T(8,128)S(1)} %collective-permute-done.10.dmsg), custom_call_target="tpu_custom_call" | custom-call | flops 1000000 | bytes 5000000 | tf_op jit(solution)/shard_map/pallas_call | solution.py:545
  (21 shorter events, 0.1 us)
Async XLA Ops:
  0.7 1.2 copy-start.3
  2.0 1.2 copy-start.4
  3.2 1.2 copy-start.5
  4.4 0.9 copy-start.6
  5.4 0.9 copy-start.7
  6.3 0.8 copy-start.8
  81.9 9.8 %collective-permute-start = (f32[112,40,128]{2,1,0:T(8,128)}, f32[112,40,128]{2,1,0:T(8,128)S(1)}, u32[]{:S(2)}, u32[]{:S(2)}) collective-permute-start(f32[112,40,128]{2,1,0:T(8,128)} %get-tuple-element.21), channel_id=1, source_target_pairs={{0,32},{32,0},{64,96},{96,64},{1,33},{33,1},{65,97},{97,65},{2,34}... | collective-permute-start | bytes 6881288 | tf_op jit(solution)/shard_map/ppermute | solution.py:578
  82.6 2.9 %copy-start.2 = (bf16[52,256,256]{2,1,0:T(8,128)(2,1)S(1)}, bf16[52,256,256]{2,1,0:T(8,128)(2,1)}, u32[]{:S(2)}) copy-start(bf16[52,256,256]{2,1,0:T(8,128)(2,1)} %get-tuple-element.22.rhs) | copy-start | bytes 20447236
  85.5 7.3 %copy-start.9 = (s32[1,1,1,3]{3,2,1,0:T(1,128)S(1)}, s32[1,1,1,3]{3,2,1,0:T(1,128)}, u32[]{:S(2)}) copy-start(s32[1,1,1,3]{3,2,1,0:T(1,128)} %param.13) | copy-start | bytes 40
  85.5 7.3 %copy-start.10 = (s32[1,1,1,6]{3,2,1,0:T(1,128)S(1)}, s32[1,1,1,6]{3,2,1,0:T(1,128)}, u32[]{:S(2)}) copy-start(s32[1,1,1,6]{3,2,1,0:T(1,128)} %param.12) | copy-start | bytes 76
  89.3 2.4 %copy-start = (f32[104,104,128]{2,1,0:T(8,128)}, f32[104,104,128]{2,1,0:T(8,128)S(1)}, u32[]{:S(2)}) copy-start(f32[104,104,128]{2,1,0:T(8,128)S(1)} %shard_map.101.co) | copy-start | bytes 16613380
  92.9 2.6 %copy-start.1 = (f32[104,104,128]{2,1,0:T(8,128)S(1)}, f32[104,104,128]{2,1,0:T(8,128)}, u32[]{:S(2)}) copy-start(f32[104,104,128]{2,1,0:T(8,128)} %copy-done) | copy-start | bytes 16613380
  99.7 27.5 %collective-permute-start.5 = (f32[240,8,128]{2,1,0:T(8,128)S(1)}, f32[240,8,128]{2,1,0:T(8,128)S(1)}, u32[]{:S(2)}, u32[]{:S(2)}) collective-permute-start(f32[240,8,128]{2,1,0:T(8,128)S(1)} %get-tuple-element.28), channel_id=1, source_target_pairs={{0,128},{128,0},{1,129},{129,1},{2,130},{130,2},{3,131},{131,3},{4... | collective-permute-start | bytes 2949128 | tf_op jit(solution)/shard_map/ppermute | solution.py:584
  100.0 27.2 %collective-permute-start.3 = (f32[182,8,128]{2,1,0:T(8,128)S(1)}, f32[182,8,128]{2,1,0:T(8,128)S(1)}, u32[]{:S(2)}, u32[]{:S(2)}) collective-permute-start(f32[182,8,128]{2,1,0:T(8,128)S(1)} %get-tuple-element.26), channel_id=1, source_target_pairs={{32,33},{33,34},{34,35},{35,36},{36,37},{37,38},{38,39},{39,40},{4... | collective-permute-start | bytes 2236424 | tf_op jit(solution)/shard_map/ppermute | solution.py:585
  103.5 23.7 %collective-permute-start.4 = (f32[182,8,128]{2,1,0:T(8,128)S(1)}, f32[182,8,128]{2,1,0:T(8,128)S(1)}, u32[]{:S(2)}, u32[]{:S(2)}) collective-permute-start(f32[182,8,128]{2,1,0:T(8,128)S(1)} %get-tuple-element.27), channel_id=1, source_target_pairs={{33,32},{34,33},{35,34},{36,35},{37,36},{38,37},{39,38},{40,39},{4... | collective-permute-start | bytes 2236424 | tf_op jit(solution)/shard_map/ppermute | solution.py:586
  109.6 16.1 %collective-permute-start.1 = (f32[104,8,128]{2,1,0:T(8,128)S(1)}, f32[104,8,128]{2,1,0:T(8,128)S(1)}, u32[]{:S(2)}, u32[]{:S(2)}) collective-permute-start(f32[104,8,128]{2,1,0:T(8,128)S(1)} %get-tuple-element.24), channel_id=1, source_target_pairs={{0,1},{1,2},{2,3},{3,4},{4,5},{5,6},{6,7},{7,8},{8,9},{9,10},{10,1... | collective-permute-start | bytes 1277960 | tf_op jit(solution)/shard_map/ppermute | solution.py:587
  111.5 15.7 %collective-permute-start.2 = (f32[104,8,128]{2,1,0:T(8,128)S(1)}, f32[104,8,128]{2,1,0:T(8,128)S(1)}, u32[]{:S(2)}, u32[]{:S(2)}) collective-permute-start(f32[104,8,128]{2,1,0:T(8,128)S(1)} %get-tuple-element.25), channel_id=1, source_target_pairs={{1,0},{2,1},{3,2},{4,3},{5,4},{6,5},{7,6},{8,7},{9,8},{10,9},{11,1... | collective-permute-start | bytes 1277960 | tf_op jit(solution)/shard_map/ppermute | solution.py:588
  132.9 19.9 %collective-permute-start.8 = (f32[112,8,128]{2,1,0:T(8,128)S(1)}, f32[112,8,128]{2,1,0:T(8,128)S(1)}, u32[]{:S(2)}, u32[]{:S(2)}) collective-permute-start(f32[112,8,128]{2,1,0:T(8,128)S(1)} %get-tuple-element.32), channel_id=1, source_target_pairs={{0,1},{1,2},{2,3},{3,4},{4,5},{5,6},{6,7},{7,8},{8,9},{9,10},{10,1... | collective-permute-start | bytes 1376264 | tf_op jit(solution)/shard_map/ppermute | solution.py:592
  134.8 18.0 %collective-permute-start.9 = (f32[112,8,128]{2,1,0:T(8,128)S(1)}, f32[112,8,128]{2,1,0:T(8,128)S(1)}, u32[]{:S(2)}, u32[]{:S(2)}) collective-permute-start(f32[112,8,128]{2,1,0:T(8,128)S(1)} %get-tuple-element.33), channel_id=1, source_target_pairs={{1,0},{2,1},{3,2},{4,3},{5,4},{6,5},{7,6},{8,7},{9,8},{10,9},{11,1... | collective-permute-start | bytes 1376264 | tf_op jit(solution)/shard_map/ppermute | solution.py:593
  140.8 12.0 %collective-permute-start.7 = (f32[100,8,128]{2,1,0:T(8,128)S(1)}, f32[100,8,128]{2,1,0:T(8,128)S(1)}, u32[]{:S(2)}, u32[]{:S(2)}) collective-permute-start(f32[100,8,128]{2,1,0:T(8,128)S(1)} %get-tuple-element.31), channel_id=1, source_target_pairs={{32,160},{160,32},{64,192},{192,64},{33,161},{161,33},{65,193},{19... | collective-permute-start | bytes 1228808 | tf_op jit(solution)/shard_map/ppermute | solution.py:590
  143.9 8.9 %collective-permute-start.6 = (f32[60,8,128]{2,1,0:T(8,128)S(1)}, f32[60,8,128]{2,1,0:T(8,128)S(1)}, u32[]{:S(2)}, u32[]{:S(2)}) collective-permute-start(f32[60,8,128]{2,1,0:T(8,128)S(1)} %get-tuple-element.30), channel_id=1, source_target_pairs={{0,128},{128,0},{1,129},{129,1},{2,130},{130,2},{3,131},{131,3},{4... | collective-permute-start | bytes 737288 | tf_op jit(solution)/shard_map/ppermute | solution.py:591
  155.2 14.4 %collective-permute-start.10 = (f32[160,8,128]{2,1,0:T(8,128)S(1)}, f32[160,8,128]{2,1,0:T(8,128)S(1)}, u32[]{:S(2)}, u32[]{:S(2)}) collective-permute-start(f32[160,8,128]{2,1,0:T(8,128)S(1)} %get-tuple-element.36), channel_id=1, source_target_pairs={{32,64},{64,32},{33,65},{65,33},{34,66},{66,34},{35,67},{67,35},{3... | collective-permute-start | bytes 1966088 | tf_op jit(solution)/shard_map/ppermute | solution.py:595
where the time goes:
time: 175 us; the launch traced here: 173 us
  Pallas kernels  94.7 us (54%)
  starting transfers between devices  35.4 us (20%)
  waiting for transfers between devices  27 us (15%)
  local copies, waits for them, and re-layouts  14.9 us (9%)
    pallas_call x1, Pallas kernels, transform(): pl.pallas_call(transform_kernel, grid=(22,), in_specs=[pl.BlockSpec(memor...  74.7 us
    unnamed x22, local copies, waits for them, and re-layouts  14.3 us
    ppermute x1, waiting for transfers between devices, local(): zhc = lax.ppermute(zhc, 'xline', along)  8.72 us
    ppermute x1, waiting for transfers between devices, local(): tmc = lax.ppermute(tmc, 'tm', times)  8.55 us
    ppermute x1, waiting for transfers between devices, local(): dmsg = lax.ppermute(dmsg, 'inline', outer)  8.25 us
    ppermute x1, starting transfers between devices, local(): dmsg = lax.ppermute(dmsg, 'inline', outer)  6.12 us
    ppermute x1, starting transfers between devices, local(): zlo = lax.ppermute(zlo, ('inline', 'xline'), back_o)  6.04 us
    ppermute x1, starting transfers between devices, local(): zl2 = lax.ppermute(zl2, 'xline', back)  5.92 us
  transfers between devices with their start and end apart: 11, of which 4 were waited for; matrix products, arithmetic and copies ran while one was open for 0% of the time, Pallas kernels for 2%

commit v1 on v0

v1 whole, which is shorter than its diff:
```python
import math

import jax
import jax.numpy as jnp
import numpy as np
from jax import lax
from jax.experimental import pallas as pl
from jax.experimental.pallas import tpu as pltpu
from jax.sharding import PartitionSpec as P

B = 128
NW = 16
F32 = jnp.float32
BF16 = jnp.bfloat16
NTR = 104
VMEM = pltpu.VMEM
SMEM = pltpu.SMEM


def tables():
    f = np.where(np.arange(B) < B // 2, np.arange(B), np.arange(B) - B).astype(np.float64)
    theta = np.mod(np.arctan2(f[None, :], f[:, None]), np.pi)
    delta = np.pi / NW
    dist = np.mod(theta[None] - np.arange(NW)[:, None, None] * delta + np.pi / 2, np.pi) - np.pi / 2
    win = np.where(np.abs(dist) < delta, np.cos(0.5 * np.pi * dist / delta), 0.0)
    rows = np.concatenate([np.arange(0, 32), np.arange(96, 128)])
    radius = np.sqrt(np.arange(32.0)[:, None, None] ** 2 + f[rows][None, :, None] ** 2 + f[None, None, :] ** 2)
    ramp = np.clip((radius - 16.0) / 16.0, 0.0, 1.0)
    wf = np.where(ramp >= 1.0, 1.0, np.sin(0.5 * np.pi * ramp))
    wc = np.where(ramp >= 1.0, 0.0, np.cos(0.5 * np.pi * ramp))
    wf = wf.reshape(32, 2, 32, B).transpose(1, 0, 2, 3)
    wc = wc.reshape(32, 2, 32, B).transpose(1, 0, 2, 3)
    n = np.arange(B)
    p = np.where(n < 64, np.sin(np.pi * (n + 0.5) / B) ** 2, np.sin(np.pi * (B - n - 0.5) / B) ** 2)
    phase = 2 * np.pi * ((n[:, None] * n[None, :]) % B) / B
    c = np.cos(phase) * p[:, None] / math.sqrt(B)
    s = np.sin(phase) * p[:, None] / math.sqrt(B)
    e0 = np.stack([np.concatenate([c, -s], 1), np.concatenate([s, c], 1)])
    w2 = np.stack([np.concatenate([c, -s], 1).T, np.concatenate([s, c], 1).T])
    w1 = np.concatenate([c[:, :64], -s[:, :64]], 1)
    w1[:, 64] = c[:, 64]
    return [np.asarray(t, np.float32) for t in (win, wf, wc, e0, w2, w1)]


def split(x):
    hi = x.astype(BF16)
    return hi, (x - hi.astype(F32)).astype(BF16)


def dot(a, b):
    return lax.dot_general(a, b, (((1,), (0,)), ((), ())), preferred_element_type=F32)


def rows_of(table, offset):
    rolled = pltpu.roll(table, offset, 0)
    row = lax.broadcasted_iota(jnp.int32, (16, table.shape[1]), 0)
    shared = rolled[0:16]
    above = jnp.concatenate([rolled[104:128], jnp.where(row < offset, shared, 0.0)], axis=0)
    below = jnp.concatenate([jnp.where(row >= offset, shared, 0.0), rolled[16:40]], axis=0)
    return rolled[40:104], above, below


def doubled(table):
    hi, lo = split(table)
    hi, lo = hi.astype(F32), lo.astype(F32)
    top, bottom = jnp.concatenate([hi, hi], axis=1), jnp.concatenate([lo, jnp.zeros_like(lo)], axis=1)
    return jnp.concatenate([top, bottom], axis=0).astype(BF16)


def transform_kernel(
    sc, fine, coarse, win, wf, wc, e0t, w2t, w1t, rim_out, outer_out, zho, zlo, rhs_out, wco_out,
    shi, slo, xhi, xlo, pq, ang, e0, w2, wm, gbuf,
):
    step = pl.program_id(0)
    o0, o1, o2, tm, odd = sc[0], sc[1], sc[2], sc[3], sc[4]

    @pl.when(step == 0)
    def _():
        total = win[sc[5]]
        for i in range(1, 6):
            total = total + win[sc[5 + i]]
        ang[...] = total
        parts = []
        for c in range(2):
            own, above, below = rows_of(e0t[c], o0)
            parts += [own, jnp.where(tm == 0, above, below)]
        hi, lo = split(jnp.concatenate(parts, axis=0))
        e0[:, 0:256] = hi
        e0[:, 256:512] = lo
        e0[:, 512:768] = hi
        for c in range(2):
            hi, lo = split(pltpu.roll(w2t[c], o2 + 88, 1))
            w2[c, 0:256] = jnp.concatenate([hi, lo], axis=1)
            w2[c, 256:512] = jnp.concatenate([hi, jnp.zeros_like(hi)], axis=1)
        own, above, below = rows_of(w1t[...], o1)
        mutual = jnp.where(odd == 0, above, below)
        outer = jnp.where(odd == 0, below, above)
        wm[...] = doubled(jnp.concatenate([mutual, outer], axis=0))
        wco_out[...] = doubled(own)

    @pl.when((step == 0) | (step == 3))
    def _():
        a = ang[pl.ds(pl.multiple_of(step * 32, 32), 32), :]
        row = lax.broadcasted_iota(jnp.int32, (32, B), 0)
        a = jnp.where((step == 3) & (row == 0), 1.0, a)

        def put(index, value):
            hi, lo = split(value)
            shi[index] = hi
            slo[index] = lo

        def plane(k0, j0, radial, coarse_w):
            for c in range(2):
                small = coarse[c, j0].astype(F32)
                small = jnp.concatenate([small, small], axis=1)
                put(c * B + k0, radial * fine[c, k0].astype(F32) + coarse_w * small)

        plane(0, 0, a * wf[0, 0], wc[0, 0])

        def low(q, _):
            radial = a * wf[0, q]
            coarse_w = wc[0, q]
            plane(q, q, radial, coarse_w)
            plane(B - q, 64 - q, radial, coarse_w)
            return 0

        lax.fori_loop(1, 32, low, 0, unroll=31)

        def high(i, _):
            for k0 in (32 + 2 * i, 33 + 2 * i):
                for c in range(2):
                    put(c * B + k0, a * fine[c, k0].astype(F32))
            return 0

        lax.fori_loop(0, 32, high, 0, unroll=4)
        for c in range(2):
            put(c * B + 96, a * fine[c, 96].astype(F32))
        xhi[pl.ds(step * 32, 32)] = jnp.swapaxes(shi[...], 0, 1)
        xlo[pl.ds(jnp.where(step == 0, 0, 32), 32)] = jnp.swapaxes(slo[...], 0, 1)

    @pl.when((step == 1) | (step == 2))
    def _():
        xhi[pl.ds(step * 32, 32)] = jnp.swapaxes(fine[...].reshape(256, 32, B), 0, 1)

    def along_xline(j):
        for which in range(2):
            out = dot(gbuf[which], w2[which])
            out = out[:, :B] + out[:, B:]
            pq[which * 64 + j] = out[:NTR]
            pq[which * 64 + j + 1] = out[NTR:]

    def hold(even, odd_part):
        for which, pair in ((0, even), (1, odd_part)):
            wide = [jnp.concatenate([g[:NTR], g[NTR:]], axis=1) for g in pair]
            hi, lo = split(jnp.concatenate(wide, axis=0))
            gbuf[which] = jnp.concatenate([hi, lo], axis=1)

    def first(k, kk, lo_pair):
        hi = jnp.concatenate([xhi[k], xhi[kk]], axis=1)
        if lo_pair is None:
            return dot(e0[:, 0:512], jnp.concatenate([hi, hi], axis=0))
        lo = jnp.concatenate(lo_pair, axis=1)
        return dot(e0[...], jnp.concatenate([hi, hi, lo], axis=0))

    def inner_pair(j):
        out = first(j, B - j, (xlo[j], xlo[64 - j]))
        return out[:, :B] + out[:, B:], out[:, :B] - out[:, B:]

    def outer_pair(j):
        out = first(j, B - j, None)
        a = out[:, :B] * ang[pl.ds(j, 1), :]
        b = out[:, B:] * ang[pl.ds(B - j, 1), :]
        return a + b, a - b

    @pl.when(step == 3)
    def _():
        out = first(0, 64, (xlo[0], jnp.zeros((256, B), BF16)))
        half = out[:, B:] * ang[64:65, :]
        even0 = out[:, :B]
        odd0 = jnp.concatenate([-half[NTR:], half[:NTR]], axis=0)
        even1, odd1 = inner_pair(1)
        hold((even0, even1), (odd0, odd1))

        def near(i, _):
            along_xline(2 * i - 2)
            ea, oa = inner_pair(2 * i)
            eb, ob = inner_pair(2 * i + 1)
            hold((ea, eb), (oa, ob))
            return 0

        lax.fori_loop(1, 16, near, 0, unroll=3)

        def far(i, _):
            along_xline(2 * i - 2)
            ea, oa = outer_pair(2 * i)
            eb, ob = outer_pair(2 * i + 1)
            hold((ea, eb), (oa, ob))
            return 0

        lax.fori_loop(16, 32, far, 0, unroll=2)
        along_xline(62)
        rim_out[13 * 8 : 14 * 8] = jnp.full((8, 40, B), o2.astype(F32), F32)

    @pl.when(step >= 4)
    def _():
        n0 = (step - 4) * 26
        ahead, behind = [], []
        for pair in range(13):
            x = jnp.concatenate([pq[:, n0 + 2 * pair, :], pq[:, n0 + 2 * pair + 1, :]], axis=1)
            hi, lo = split(x)
            rhs = jnp.concatenate([hi, lo], axis=0)
            rhs_out[pair] = rhs
            out = dot(wm[...], rhs)
            out = out[:80] + out[80:]
            for half in range(2):
                part = out[:, half * B : half * B + B]
                rim_out[n0 + 2 * pair + half] = part[:40]
                outer_out[2 * pair + half] = part[40:]
                for b in range(5):
                    near, far = two_sides(part[40 + 8 * b : 48 + 8 * b], o2)
                    ahead.append(near)
                    behind.append(far)
        pack_many(ahead, zho, 64)
        pack_many(behind, zlo, 88)


def transform(scalars, fine, coarse, tabs):
    def edge(s):
        return jnp.minimum(s, 1)

    def late_step(s):
        return (jnp.maximum(s - 4, 0), 0, 0)

    whole = pl.BlockSpec(memory_space=VMEM)
    return pl.pallas_call(
        transform_kernel,
        grid=(8,),
        in_specs=[
            pl.BlockSpec(memory_space=SMEM),
            pl.BlockSpec((2, B, 32, B), lambda s: (0, 0, jnp.minimum(s, 3), 0)),
            pl.BlockSpec((2, 64, 32, 64), lambda s: (0, 0, edge(s), 0)),
            whole,
            pl.BlockSpec((1, 32, 32, B), lambda s: (edge(s), 0, 0, 0)),
            pl.BlockSpec((1, 32, 32, B), lambda s: (edge(s), 0, 0, 0)),
            whole,
            whole,
            whole,
        ],
        out_specs=[
            whole,
            pl.BlockSpec((26, 40, B), late_step),
            pl.BlockSpec((44, 8, B), late_step),
            pl.BlockSpec((44, 8, B), late_step),
            pl.BlockSpec((13, 256, 256), late_step),
            whole,
        ],
        out_shape=[
            jax.ShapeDtypeStruct((NTR + 8, 40, B), F32),
            jax.ShapeDtypeStruct((NTR, 40, B), F32),
            jax.ShapeDtypeStruct((4 * 44, 8, B), F32),
            jax.ShapeDtypeStruct((4 * 44, 8, B), F32),
            jax.ShapeDtypeStruct((NTR // 2, 256, 256), BF16),
            jax.ShapeDtypeStruct((128, 256), BF16),
        ],
        scratch_shapes=[
            VMEM((256, 32, B), BF16),
            VMEM((256, 32, B), BF16),
            VMEM((B, 256, B), BF16),
            VMEM((64, 256, B), BF16),
            VMEM((B, NTR, B), F32),
            VMEM((B, B), F32),
            VMEM((208, 768), BF16),
            VMEM((2, 512, 256), BF16),
            VMEM((160, 256), BF16),
            VMEM((2, 208, 512), BF16),
        ],
        compiler_params=pltpu.CompilerParams(
            dimension_semantics=("arbitrary",), vmem_limit_bytes=63 * 2**20
        ),
        cost_estimate=pl.CostEstimate(flops=2 * 10**10, bytes_accessed=30 * 10**6, transcendentals=0),
    )(scalars, fine, coarse, *tabs)


def own_rows_kernel(rhs, wco, out):
    for pair in range(13):
        x = dot(wco[...], rhs[pair])
        x = x[:64] + x[64:]
        out[2 * pair] = x[:, :B]
        out[2 * pair + 1] = x[:, B:]


def own_rows(rhs, wco):
    return pl.pallas_call(
        own_rows_kernel,
        grid=(4,),
        in_specs=[pl.BlockSpec((13, 256, 256), lambda s: (s, 0, 0)), pl.BlockSpec(memory_space=VMEM)],
        out_specs=pl.BlockSpec((26, 64, B), lambda s: (s, 0, 0)),
        out_shape=jax.ShapeDtypeStruct((NTR, 64, B), F32),
        compiler_params=pltpu.CompilerParams(dimension_semantics=("arbitrary",), vmem_limit_bytes=63 * 2**20),
        cost_estimate=pl.CostEstimate(flops=52 * 2 * 128 * 256 * 256, bytes_accessed=11 * 10**6, transcendentals=0),
    )(rhs, wco)


def lanes():
    return lax.broadcasted_iota(jnp.int32, (8, B), 1)


def two_sides(value, offset):
    lane = lanes()
    return jnp.where(lane < 88 + offset, value, 0.0), jnp.where(lane >= 88 + offset, value, 0.0)


def turn(value, shift):
    shift = shift % B
    return value if shift == 0 else pltpu.roll(value, shift, 1)


def pack3(pieces, start):
    lane = lanes()
    out = turn(pieces[0], -start)
    for i in range(1, len(pieces)):
        out = jnp.where(lane < 40 * i, out, turn(pieces[i], 40 * i - start))
    return out


def unpack3(packed, place, start):
    lane = lanes()
    value = turn(packed, start - 40 * place)
    return jnp.where((lane >= start) & (lane < start + 40), value, 0.0)


def merged(own, rim, mate, t, b, sc):
    near, far = two_sides(own[t, 8 * b : 8 * b + 8, :], sc[2])
    place = b - jnp.where(sc[4] == 0, 3, 0)
    valid = (place >= 0) & (place < 5)
    place = jnp.clip(place, 0, 4)
    other = rim[t, pl.ds(pl.multiple_of(place * 8, 8), 8), :]
    other = jnp.where(valid, other, 0.0)
    upto = lanes().astype(F32) < 88.0 + mate[0, 0:8, :]
    return near + jnp.where(upto, other, 0.0), far + jnp.where(upto, 0.0, other)


def pack_many(pieces, out, start):
    for g in range((len(pieces) + 2) // 3):
        out[g] = pack3(pieces[3 * g : 3 * g + 3], start)


def call(kernel, grid, in_specs, outs, count, *args):
    return pl.pallas_call(
        kernel,
        grid=(grid,),
        in_specs=[pl.BlockSpec(memory_space=SMEM)] + in_specs,
        out_specs=[pl.BlockSpec(block, index) for _, block, index in outs],
        out_shape=[jax.ShapeDtypeStruct(shape, F32) for shape, _, _ in outs],
        compiler_params=pltpu.CompilerParams(dimension_semantics=("arbitrary",), vmem_limit_bytes=63 * 2**20),
        cost_estimate=pl.CostEstimate(flops=10**6, bytes_accessed=count, transcendentals=0),
    )(*args)


def each(s):
    return (s, 0, 0)


def core(s):
    return (jnp.minimum(s, 7), 0, 0)


def edge(s):
    return (jnp.maximum(s - 8, 0), 0, 0)


WHOLE = pl.BlockSpec(memory_space=VMEM)
OWN_SPECS = [
    pl.BlockSpec((8, 64, B), each),
    pl.BlockSpec((8, 40, B), each),
    pl.BlockSpec((8, 40, B), lambda s: (13, 0, 0)),
]


def pack_kernel(sc, own, rim, mate, zhc, zlc, tmsg):
    step = pl.program_id(0)
    ahead, behind = [], []
    for t in range(8):
        for b in range(5):
            near, far = merged(own, rim, mate, t, b, sc)
            ahead.append(near)
            behind.append(far)
    pack_many(ahead, zhc, 64)
    pack_many(behind, zlc, 88)

    @pl.when(step >= 8)
    def _():
        lane = lanes()
        extra = None
        for t in range(8):
            for b in range(3):
                near, far = merged(own, rim, mate, t, b + 5, sc)
                q = t * 3 + b
                tmsg[q] = jnp.where(lane < 104, near, far)
                moved = turn(far, 16 * (q % 8) - 88)
                extra = moved if q % 8 == 0 else jnp.where(lane < 16 * (q % 8), extra, moved)
                if q % 8 == 7:
                    tmsg[24 + q // 8] = extra


def pack(sc, own, rim):
    outs = [
        ((13 * 14, 8, B), (14, 8, B), each),
        ((13 * 14, 8, B), (14, 8, B), each),
        ((5 * 27, 8, B), (27, 8, B), edge),
    ]
    return call(pack_kernel, 13, OWN_SPECS, outs, 9 * 10**6, sc, own, rim, rim)


def outer_middle_kernel(sc, outer, zh, zl, own, msg):
    lane = lanes()

    def summed(t, b):
        q = lax.rem(t, 26) * 5 + b
        g, place = lax.div(t, 26) * 44 + lax.div(q, 3), lax.rem(q, 3)
        low = pltpu.roll(zh[g], lax.rem(B - 40 * place, B), 1)
        high = pltpu.roll(zl[g], lax.rem(B + 24 - 40 * place, B), 1)
        low = jnp.where(lane < 40, low, 0.0)
        high = jnp.where((lane >= 24) & (lane < 64), high, 0.0)
        return outer[t, 8 * b : 8 * b + 8, :] + low + high

    def core_rows(t, _):
        for b in range(5):
            own[t, 8 * b : 8 * b + 8, :] = summed(t, b)
        return 0

    def rim_rows(p, _):
        for b in range(5):
            even, odd = summed(64 + 2 * p, b), summed(65 + 2 * p, b)
            msg[p * 5 + b] = jnp.where(lane < 64, even, pltpu.roll(odd, 64, 1))
        return 0

    lax.fori_loop(0, 20, rim_rows, 0, unroll=2)
    lax.fori_loop(0, 64, core_rows, 0, unroll=4)


def outer_middle(sc, outer, zh, zl):
    outs = [((64, 40, B), (64, 40, B), lambda s: (0, 0, 0)), ((100, 8, B), (100, 8, B), lambda s: (0, 0, 0))]
    return call(outer_middle_kernel, 1, [WHOLE] * 3, outs, 5 * 10**6, sc, outer, zh, zl)


def middle_kernel(sc, own, rim, mate, zhc, zlc, tmsg, own1, tmc, zh2, zl2, own2):
    step = pl.program_id(0)
    lane = lanes()

    def first_rows(t, b):
        near, _ = merged(own, rim, mate, t, b, sc)
        q = t * 5 + b
        return near + unpack3(zhc[q // 3], q % 3, 0) + unpack3(zlc[q // 3], q % 3, 24)

    @pl.when(step >= 8)
    def _():
        for t in range(0, 8, 2):
            for b in range(5):
                tmc[t // 2 * 5 + b] = jnp.where(lane < 64, first_rows(t, b), turn(first_rows(t + 1, b), 64))

    @pl.when(step < 8)
    def _():
        for t in range(8):
            for b in range(5):
                own1[t, 8 * b : 8 * b + 8, :] = first_rows(t, b)
        place = step - jnp.where(sc[3] == 0, 3, 0)
        valid = (place >= 0) & (place < 5)
        base = jnp.clip(place, 0, 4) * 27
        for t in range(8):
            ahead, behind = [], []
            for b in range(3):
                q = t * 3 + b
                near, far = merged(own, rim, mate, t, b + 5, sc)
                main = tmsg[base + q]
                moved = turn(tmsg[base + 24 + q // 8], 88 - 16 * (q % 8))
                near = near + jnp.where(valid & (lane < 104), main, 0.0)
                far2 = jnp.where(lane >= 104, main, jnp.where(lane >= 88, moved, 0.0))
                far = far + jnp.where(valid, far2, 0.0)
                ahead.append(near)
                behind.append(far)
                own2[t, 8 * b : 8 * b + 8, :] = near
            zh2[t] = pack3(ahead, 64)
            zl2[t] = pack3(behind, 88)


def middle(sc, own, rim, zhc, zlc, tmsg):
    outs = [
        ((64, 40, B), (8, 40, B), core),
        ((100, 8, B), (20, 8, B), edge),
        ((64, 8, B), (8, 8, B), core),
        ((64, 8, B), (8, 8, B), core),
        ((64, 24, B), (8, 24, B), core),
    ]
    msgs = [pl.BlockSpec((14, 8, B), each), pl.BlockSpec((14, 8, B), each), WHOLE]
    return call(middle_kernel, 13, OWN_SPECS + msgs, outs, 11 * 10**6, sc, own, rim, rim, zhc, zlc, tmsg)


def time_rows(sc, own, msg, step, t, b):
    place = step - jnp.where(sc[3] == 0, 3, 0)
    valid = (place >= 0) & (place < 5)
    both = msg[(jnp.clip(place, 0, 4) * 4 + t // 2) * 5 + b]
    both = both if t % 2 == 0 else turn(both, 64)
    return own[t, 8 * b : 8 * b + 8, :] + jnp.where(valid, both, 0.0)


def outer_late_kernel(sc, own, msg, dmsg):
    step = pl.program_id(0)
    lane = lanes()
    for t in range(0, 8, 2):
        for b in range(5):
            even, odd = time_rows(sc, own, msg, step, t, b), time_rows(sc, own, msg, step, t + 1, b)
            dmsg[t // 2 * 5 + b] = jnp.where(lane < 64, even, turn(odd, 64))


def outer_late(sc, own, msg):
    outs = [((160, 8, B), (20, 8, B), each)]
    return call(outer_late_kernel, 8, [pl.BlockSpec((8, 40, B), each), WHOLE], outs, 2 * 10**6, sc, own, msg)[0]


def last_kernel(sc, own1, tmc, zh2, zl2, own2, dmsg, out):
    step = pl.program_id(0)
    shift = jnp.where(sc[4] == 0, 0, 3)
    for t in range(8):
        for b in range(8):
            if b < 5:
                value = time_rows(sc, own1, tmc, step, t, b)
            else:
                value = own2[t, 8 * (b - 5) : 8 * (b - 5) + 8, :]
                value = value + unpack3(zh2[t], b - 5, 0) + unpack3(zl2[t], b - 5, 24)
            place = b - shift
            valid = (place >= 0) & (place < 5)
            other = dmsg[t // 2 * 5 + jnp.clip(place, 0, 4)]
            other = other if t % 2 == 0 else turn(other, 64)
            value = value + jnp.where(valid, other, 0.0)
            out[t, 8 * b : 8 * b + 8, :] = value[:, :64]


def last(sc, own1, tmc, zh2, zl2, own2, dmsg):
    specs = [
        pl.BlockSpec((8, 40, B), each),
        WHOLE,
        pl.BlockSpec((8, 8, B), each),
        pl.BlockSpec((8, 8, B), each),
        pl.BlockSpec((8, 24, B), each),
        pl.BlockSpec((20, 8, B), each),
    ]
    outs = [((64, 64, 64), (8, 64, 64), each)]
    return call(last_kernel, 8, specs, outs, 7 * 10**6, sc, own1, tmc, zh2, zl2, own2, dmsg)[0]


def local(coef_fine, coef_coarse, kept, tile_offsets):
    tabs = [jnp.asarray(t) for t in tables()]
    n_tm, n_in, n_x = (lax.axis_size(a) for a in ("tm", "inline", "xline"))
    tm = lax.axis_index("tm").astype(jnp.int32)
    odd = (lax.axis_index("inline") & 1).astype(jnp.int32)
    sc = jnp.concatenate([tile_offsets.reshape(3), jnp.stack([tm, odd]), kept.reshape(6)])

    along = [(i, i + 1) for i in range(n_x - 1)]
    back = [(b, a) for a, b in along]
    inner = range(1, n_in - 1)
    along_o = [(i * n_x + a, i * n_x + b) for i in inner for a, b in along]
    back_o = [(b, a) for a, b in along_o]
    times = [(i, i ^ 1) for i in range(n_tm)]
    times_o = [(a * n_in + i, b * n_in + i) for i in inner for a, b in times]
    mates = [(i, i ^ 1) for i in range(n_in)]
    facing = [p for i in range(1, n_in - 1, 2) for p in ((i, i + 1), (i + 1, i))]

    rim, outer, zho, zlo, rhs, wco = transform(sc, coef_fine, coef_coarse, tabs)
    rim = lax.ppermute(rim, "inline", mates)
    zho = lax.ppermute(zho, ("inline", "xline"), along_o)
    zlo = lax.ppermute(zlo, ("inline", "xline"), back_o)
    own = own_rows(rhs, wco)

    zhc, zlc, tmsg = pack(sc, own, rim)
    tmsg = lax.ppermute(tmsg, "tm", times)
    zhc = lax.ppermute(zhc, "xline", along)
    zlc = lax.ppermute(zlc, "xline", back)
    outer, tmo = outer_middle(sc, outer, zho, zlo)
    tmo = lax.ppermute(tmo, ("tm", "inline"), times_o)
    own1, tmc, zh2, zl2, own2 = middle(sc, own, rim, zhc, zlc, tmsg)
    tmc = lax.ppermute(tmc, "tm", times)
    zh2 = lax.ppermute(zh2, "xline", along)
    zl2 = lax.ppermute(zl2, "xline", back)
    dmsg = outer_late(sc, outer, tmo)
    dmsg = lax.ppermute(dmsg, "inline", facing)
    return last(sc, own1, tmc, zh2, zl2, own2, dmsg)


def solution(mesh):
    in_specs = (
        P(None, "tm", "inline", "xline"),
        P(None, "tm", "inline", "xline"),
        P("tm", "inline", "xline", None),
        P("tm", "inline", "xline", None),
    )
    out_specs = P("tm", "inline", "xline")
    return jax.shard_map(local, mesh=mesh, in_specs=in_specs, out_specs=out_specs, check_vma=False)
```

time: 175 us -> 133 us (0.76)
  waiting for transfers between devices: 27 us -> 11.1 us
  local copies, waits for them, and re-layouts: 14.9 us -> 1.68 us
  Pallas kernels: 94.7 us -> 83.9 us
  starting transfers between devices: 35.4 us -> 33.5 us
    unnamed x22 -> x8, local copies, waits for them, and re-layouts: 14.3 us -> 1.68 us
    pallas_call x6 -> x7, Pallas kernels: 94.7 us -> 83.9 us  [the longest x5 43.8 us: call(): pl.pallas_call(kernel, grid=(grid,), in_specs=[pl.BlockSpec(memory_space=...]
    ppermute x1, waiting for transfers between devices: 8.72 us -> 0.01 us  [local(): zhc = lax.ppermute(zhc, 'xline', along)]
    ppermute x1, waiting for transfers between devices: 8.55 us -> 0.01 us  [local(): tmc = lax.ppermute(tmc, 'tm', times)]
    ppermute x1, waiting for transfers between devices: 8.25 us -> 0.01 us  [local(): dmsg = lax.ppermute(dmsg, 'inline', facing)]
    ppermute x1, waiting for transfers between devices: 0.01 us -> 7.43 us  [local(): tmo = lax.ppermute(tmo, ('tm', 'inline'), times_o)]
    ppermute x1, starting transfers between devices: 6.12 us -> 3.75 us  [local(): dmsg = lax.ppermute(dmsg, 'inline', facing)]
    ppermute x1, waiting for transfers between devices: 0.01 us -> 2.02 us  [local(): zh2 = lax.ppermute(zh2, 'xline', along)]
  transfers between devices with their start and end apart: 11 -> 11, of which waited for: 4 -> 3; matrix products, arithmetic and copies ran while one was open for 0% -> 0% of each run, Pallas kernels for 2% -> 32%
where the time goes in v1:
time: 133 us; the launch traced here: 132 us
  Pallas kernels  83.9 us (63%)
  starting transfers between devices  33.5 us (25%)
  waiting for transfers between devices  11.1 us (8%)
  local copies, waits for them, and re-layouts  1.68 us (1%)
  other arithmetic  1.33 us (1%)
    pallas_call x5, Pallas kernels, call(): pl.pallas_call(kernel, grid=(grid,), in_specs=[pl.BlockSpec(memory_space=...  43.8 us
    pallas_call x1, Pallas kernels, transform(): pl.pallas_call(transform_kernel, grid=(8,), in_specs=[pl.BlockSpec(memory...  34.3 us
    ppermute x1, waiting for transfers between devices, local(): tmo = lax.ppermute(tmo, ('tm', 'inline'), times_o)  7.43 us
    ppermute x1, starting transfers between devices, local(): zlo = lax.ppermute(zlo, ('inline', 'xline'), back_o)  6.02 us
    pallas_call x1, Pallas kernels, own_rows(): pl.pallas_call(own_rows_kernel, grid=(4,), in_specs=[pl.BlockSpec((13, 25...  5.82 us
    ppermute x1, starting transfers between devices, local(): zlc = lax.ppermute(zlc, 'xline', back)  5.47 us
    ppermute x1, starting transfers between devices, local(): zl2 = lax.ppermute(zl2, 'xline', back)  5.47 us
    ppermute x1, starting transfers between devices, local(): dmsg = lax.ppermute(dmsg, 'inline', facing)  3.75 us
  transfers between devices with their start and end apart: 11, of which 3 were waited for; matrix products, arithmetic and copies ran while one was open for 0% of the time, Pallas kernels for 32%

profile of v1, /device:TPU:27, one launch (start us, length us, event | category | flops | bytes accessed | tf_op | source)
XLA Modules:
  0.0 131.6 jit_solution(15623118249235338535)
XLA Ops:
  0.0 1.3 %pad_add_fusion.sc = s32[11]{0:T(128)} fusion(s32[6]{0:T(128)} %bitcast.4, s32[1]{0:T(128)} %bitcast.2, s32[1]{0:T(128)} %bitcast.1, s32[3]{0:T(128)} %bitcast.5), kind=kLoop, calls=%fused_computation | loop fusion | flops 33 | bytes 88 | tf_op jit(solution)/shard_map/concatenate | solution.py:557
  1.3 34.3 %shard_map.100 = (f32[112,40,128]{2,1,0:T(8,128)}, f32[104,40,128]{2,1,0:T(8,128)}, f32[176,8,128]{2,1,0:T(8,128)}, f32[176,8,128]{2,1,0:T(8,128)}, bf16[52,256,...) custom-call(s32[11]{0:T(128)} %pad_add_fusion.sc, bf16[2,128,128,128]{3,2,1,0:T(8,128)(2,1)} %fine.1, ...), custom_call_target="tpu_custom_call" | custom-call | flops 20000000000 | bytes 30000000 | tf_op jit(solution)/shard_map/pallas_call | solution.py:235
  35.6 0.8 collective-permute-start
  36.4 3.5 %collective-permute-start.7 = (f32[176,8,128]{2,1,0:T(8,128)}, f32[176,8,128]{2,1,0:T(8,128)}, u32[]{:S(2)}, u32[]{:S(2)}) collective-permute-start(f32[176,8,128]{2,1,0:T(8,128)} %get-tuple-element.33), channel_id=1, source_target_pairs={{32,33},{33,34},{34,35},{35,36},{36,37},{37,38},{38,39},{39,40},{4... | collective-permute-start | bytes 2162696 | tf_op jit(solution)/shard_map/ppermute | solution.py:571
  39.9 6.0 %collective-permute-start.8 = (f32[176,8,128]{2,1,0:T(8,128)}, f32[176,8,128]{2,1,0:T(8,128)}, u32[]{:S(2)}, u32[]{:S(2)}) collective-permute-start(f32[176,8,128]{2,1,0:T(8,128)} %get-tuple-element.34), channel_id=1, source_target_pairs={{33,32},{34,33},{35,34},{36,35},{37,36},{38,37},{39,38},{40,39},{4... | collective-permute-start | bytes 2162696 | tf_op jit(solution)/shard_map/ppermute | solution.py:572
  45.9 5.8 %shard_map.101.own = f32[104,64,128]{2,1,0:T(8,128)} custom-call(bf16[52,256,256]{2,1,0:T(8,128)(2,1)} %get-tuple-element.21.rhs, bf16[128,256]{1,0:T(8,128)(2,1)} %get-tuple-element.22.wco), custom_call_target="tpu_custom_call" | custom-call | flops 872415232 | bytes 11000000 | tf_op jit(solution)/shard_map/pallas_call | solution.py:293
  51.8 0.0 collective-permute-done.rim.mate
  51.8 9.9 %shard_map.102 = (f32[182,8,128]{2,1,0:T(8,128)}, f32[182,8,128]{2,1,0:T(8,128)}, f32[135,8,128]{2,1,0:T(8,128)}) custom-call(s32[11]{0:T(128)} %pad_add_fusion.sc, f32[104,64,128]{2,1,0:T(8,128)} %shard_map.101.own, f32[112,40,128]{2,1,0:T(8,128)} %collective-permute-done.rim.mate, f32[112,40,128]{2,1,0:T(8,128)} %collective-permute-done.rim.mate), custom_call_target="tpu_custom_call" | custom-call | flops 1000000 | bytes 9000000 | tf_op jit(solution)/shard_map/pallas_call | solution.py:349
  61.6 1.9 %collective-permute-start.1 = (f32[182,8,128]{2,1,0:T(8,128)}, f32[182,8,128]{2,1,0:T(8,128)S(1)}, u32[]{:S(2)}, u32[]{:S(2)}) collective-permute-start(f32[182,8,128]{2,1,0:T(8,128)} %get-tuple-element.24), channel_id=1, source_target_pairs={{0,1},{1,2},{2,3},{3,4},{4,5},{5,6},{6,7},{7,8},{8,9},{9,10},{10,1... | collective-permute-start | bytes 2236424 | tf_op jit(solution)/shard_map/ppermute | solution.py:577
  63.5 5.5 %collective-permute-start.2 = (f32[182,8,128]{2,1,0:T(8,128)}, f32[182,8,128]{2,1,0:T(8,128)}, u32[]{:S(2)}, u32[]{:S(2)}) collective-permute-start(f32[182,8,128]{2,1,0:T(8,128)} %get-tuple-element.25), channel_id=1, source_target_pairs={{1,0},{2,1},{3,2},{4,3},{5,4},{6,5},{7,6},{8,7},{9,8},{10,9},{11,1... | collective-permute-start | bytes 2236424 | tf_op jit(solution)/shard_map/ppermute | solution.py:578
  69.0 0.0 collective-permute-done.7.zh
  69.0 10.1 %shard_map.104 = (f32[64,40,128]{2,1,0:T(8,128)}, f32[100,8,128]{2,1,0:T(8,128)}) custom-call(s32[11]{0:T(128)} %pad_add_fusion.sc, f32[104,40,128]{2,1,0:T(8,128)} %get-tuple-element.32.outer, f32[176,8,128]{2,1,0:T(8,128)} %collective-permute-done.7.zh, f32[176,8,128]{2,1,0:T(8,128)} %collective-permute-done.8.zl), custom_call_target="tpu_custom_call" | custom-call | flops 1000000 | bytes 5000000 | tf_op jit(solution)/shard_map/pallas_call | solution.py:349
  79.2 2.2 %collective-permute-start.9 = (f32[100,8,128]{2,1,0:T(8,128)}, f32[100,8,128]{2,1,0:T(8,128)}, u32[]{:S(2)}, u32[]{:S(2)}) collective-permute-start(f32[100,8,128]{2,1,0:T(8,128)} %get-tuple-element.36), channel_id=1, source_target_pairs={{32,160},{160,32},{64,192},{192,64},{33,161},{161,33},{65,193},{19... | collective-permute-start | bytes 1228808 | tf_op jit(solution)/shard_map/ppermute | solution.py:580
  81.3 1.3 collective-permute-start.3
  82.6 7.4 %collective-permute-done.9.msg = f32[100,8,128]{2,1,0:T(8,128)} collective-permute-done((f32[100,8,128]{2,1,0:T(8,128)}, f32[100,8,128]{2,1,0:T(8,128)}, u32[]{:S(2)}, u32[]{:S(2)}) %collective-permute-start.9) | collective-permute-done | bytes 409632 | tf_op jit(solution)/shard_map/ppermute | solution.py:580
  90.1 5.9 %shard_map.105 = f32[160,8,128]{2,1,0:T(8,128)} custom-call(s32[11]{0:T(128)} %pad_add_fusion.sc, f32[64,40,128]{2,1,0:T(8,128)} %get-tuple-element.35.own, f32[100,8,128]{2,1,0:T(8,128)} %collective-permute-done.9.msg), custom_call_target="tpu_custom_call" | custom-call | flops 1000000 | bytes 2000000 | tf_op jit(solution)/shard_map/pallas_call | solution.py:349
  96.0 3.7 %collective-permute-start.10 = (f32[160,8,128]{2,1,0:T(8,128)}, f32[160,8,128]{2,1,0:T(8,128)}, u32[]{:S(2)}, u32[]{:S(2)}) collective-permute-start(f32[160,8,128]{2,1,0:T(8,128)} %shard_map.105), channel_id=1, source_target_pairs={{32,64},{64,32},{33,65},{65,33},{34,66},{66,34},{35,67},{67,35},{3... | collective-permute-start | bytes 1966088 | tf_op jit(solution)/shard_map/ppermute | solution.py:586
  99.8 0.0 collective-permute-done.1.zhc
  99.8 0.0 copy-start
  99.8 0.0 collective-permute-done.2.zlc
  99.8 0.8 copy-done
  100.7 10.9 %shard_map.103 = (f32[64,40,128]{2,1,0:T(8,128)}, f32[100,8,128]{2,1,0:T(8,128)}, f32[64,8,128]{2,1,0:T(8,128)}, f32[64,8,128]{2,1,0:T(8,128)}, f32[64,24,128]{2,1,0:T(8,128)}) custom-call(s32[11]{0:T(128)} %pad_add_fusion.sc, f32[104,64,128]{2,1,0:T(8,128)} %shard_map.101.own, f32[112,40,128]{2,1,0:T(8,128)} %collective-permute-done.rim.mate, ...), custom_call_target="tpu_custom_call" | custom-call | flops 1000000 | bytes 11000000 | tf_op jit(solution)/shard_map/pallas_call | solution.py:349
  111.6 1.3 collective-permute-start.4
  112.8 1.9 %collective-permute-start.5 = (f32[64,8,128]{2,1,0:T(8,128)}, f32[64,8,128]{2,1,0:T(8,128)S(1)}, u32[]{:S(2)}, u32[]{:S(2)}) collective-permute-start(f32[64,8,128]{2,1,0:T(8,128)} %get-tuple-element.29), channel_id=1, source_target_pairs={{0,1},{1,2},{2,3},{3,4},{4,5},{5,6},{6,7},{7,8},{8,9},{9,10},{10,1... | collective-permute-start | bytes 786440 | tf_op jit(solution)/shard_map/ppermute | solution.py:583
  114.7 5.5 %collective-permute-start.6 = (f32[64,8,128]{2,1,0:T(8,128)}, f32[64,8,128]{2,1,0:T(8,128)S(1)}, u32[]{:S(2)}, u32[]{:S(2)}) collective-permute-start(f32[64,8,128]{2,1,0:T(8,128)} %get-tuple-element.30), channel_id=1, source_target_pairs={{1,0},{2,1},{3,2},{4,3},{5,4},{6,5},{7,6},{8,7},{9,8},{10,9},{11,1... | collective-permute-start | bytes 786440 | tf_op jit(solution)/shard_map/ppermute | solution.py:584
  120.2 0.0 collective-permute-done.10.dmsg
  120.2 2.0 %collective-permute-done.5.zh2 = f32[64,8,128]{2,1,0:T(8,128)S(1)} collective-permute-done((f32[64,8,128]{2,1,0:T(8,128)}, f32[64,8,128]{2,1,0:T(8,128)S(1)}, u32[]{:S(2)}, u32[]{:S(2)}) %collective-permute-start.5) | collective-permute-done | bytes 262176 | tf_op jit(solution)/shard_map/ppermute | solution.py:583
  122.2 1.6 %collective-permute-done.6.zl2 = f32[64,8,128]{2,1,0:T(8,128)S(1)} collective-permute-done((f32[64,8,128]{2,1,0:T(8,128)}, f32[64,8,128]{2,1,0:T(8,128)S(1)}, u32[]{:S(2)}, u32[]{:S(2)}) %collective-permute-start.6) | collective-permute-done | bytes 262176 | tf_op jit(solution)/shard_map/ppermute | solution.py:584
  123.8 0.0 collective-permute-done.4.tmc
  123.8 0.7 copy-done.3
  124.5 0.1 copy-done.1
  124.7 6.9 %shard_map.106 = f32[64,64,64]{2,1,0:T(8,128)} custom-call(s32[11]{0:T(128)} %pad_add_fusion.sc, f32[64,40,128]{2,1,0:T(8,128)} %get-tuple-element.27.own1, f32[100,8,128]{2,1,0:T(8,128)} %copy-done.1, f32[64,8,128]{2,1,0:T(8,128)} %copy-done.2, f32[64,8,128]{2,1,0:T(8,128)} %copy-done.3, f32[64,24,128]{2,1,0:T(8,128)} %get-tuple-element.31.own2, ...), custom_call_target="tpu_custom_call" | custom-call | flops 1000000 | bytes 7000000 | tf_op jit(solution)/shard_map/pallas_call | solution.py:349
  (6 shorter events, 0.0 us)
Async XLA Ops:
  35.6 16.2 %collective-permute-start = (f32[112,40,128]{2,1,0:T(8,128)}, f32[112,40,128]{2,1,0:T(8,128)}, u32[]{:S(2)}, u32[]{:S(2)}) collective-permute-start(f32[112,40,128]{2,1,0:T(8,128)} %get-tuple-element.23), channel_id=1, source_target_pairs={{0,32},{32,0},{64,96},{96,64},{1,33},{33,1},{65,97},{97,65},{2,34}... | collective-permute-start | bytes 6881288 | tf_op jit(solution)/shard_map/ppermute | solution.py:570
  36.4 32.7 %collective-permute-start.7 = (f32[176,8,128]{2,1,0:T(8,128)}, f32[176,8,128]{2,1,0:T(8,128)}, u32[]{:S(2)}, u32[]{:S(2)}) collective-permute-start(f32[176,8,128]{2,1,0:T(8,128)} %get-tuple-element.33), channel_id=1, source_target_pairs={{32,33},{33,34},{34,35},{35,36},{36,37},{37,38},{38,39},{39,40},{4... | collective-permute-start | bytes 2162696 | tf_op jit(solution)/shard_map/ppermute | solution.py:571
  39.9 29.1 %collective-permute-start.8 = (f32[176,8,128]{2,1,0:T(8,128)}, f32[176,8,128]{2,1,0:T(8,128)}, u32[]{:S(2)}, u32[]{:S(2)}) collective-permute-start(f32[176,8,128]{2,1,0:T(8,128)} %get-tuple-element.34), channel_id=1, source_target_pairs={{33,32},{34,33},{35,34},{36,35},{37,36},{38,37},{39,38},{40,39},{4... | collective-permute-start | bytes 2162696 | tf_op jit(solution)/shard_map/ppermute | solution.py:572
  61.6 38.2 %collective-permute-start.1 = (f32[182,8,128]{2,1,0:T(8,128)}, f32[182,8,128]{2,1,0:T(8,128)S(1)}, u32[]{:S(2)}, u32[]{:S(2)}) collective-permute-start(f32[182,8,128]{2,1,0:T(8,128)} %get-tuple-element.24), channel_id=1, source_target_pairs={{0,1},{1,2},{2,3},{3,4},{4,5},{5,6},{6,7},{7,8},{8,9},{9,10},{10,1... | collective-permute-start | bytes 2236424 | tf_op jit(solution)/shard_map/ppermute | solution.py:577
  63.5 36.3 %collective-permute-start.2 = (f32[182,8,128]{2,1,0:T(8,128)}, f32[182,8,128]{2,1,0:T(8,128)}, u32[]{:S(2)}, u32[]{:S(2)}) collective-permute-start(f32[182,8,128]{2,1,0:T(8,128)} %get-tuple-element.25), channel_id=1, source_target_pairs={{1,0},{2,1},{3,2},{4,3},{5,4},{6,5},{7,6},{8,7},{9,8},{10,9},{11,1... | collective-permute-start | bytes 2236424 | tf_op jit(solution)/shard_map/ppermute | solution.py:578
  79.2 10.9 %collective-permute-start.9 = (f32[100,8,128]{2,1,0:T(8,128)}, f32[100,8,128]{2,1,0:T(8,128)}, u32[]{:S(2)}, u32[]{:S(2)}) collective-permute-start(f32[100,8,128]{2,1,0:T(8,128)} %get-tuple-element.36), channel_id=1, source_target_pairs={{32,160},{160,32},{64,192},{192,64},{33,161},{161,33},{65,193},{19... | collective-permute-start | bytes 1228808 | tf_op jit(solution)/shard_map/ppermute | solution.py:580
  81.3 18.4 %collective-permute-start.3 = (f32[135,8,128]{2,1,0:T(8,128)}, f32[135,8,128]{2,1,0:T(8,128)}, u32[]{:S(2)}, u32[]{:S(2)}) collective-permute-start(f32[135,8,128]{2,1,0:T(8,128)} %get-tuple-element.26), channel_id=1, source_target_pairs={{0,128},{128,0},{1,129},{129,1},{2,130},{130,2},{3,131},{131,3},{4... | collective-permute-start | bytes 1658888 | tf_op jit(solution)/shard_map/ppermute | solution.py:576
  96.0 24.2 %collective-permute-start.10 = (f32[160,8,128]{2,1,0:T(8,128)}, f32[160,8,128]{2,1,0:T(8,128)}, u32[]{:S(2)}, u32[]{:S(2)}) collective-permute-start(f32[160,8,128]{2,1,0:T(8,128)} %shard_map.105), channel_id=1, source_target_pairs={{32,64},{64,32},{33,65},{65,33},{34,66},{66,34},{35,67},{67,35},{3... | collective-permute-start | bytes 1966088 | tf_op jit(solution)/shard_map/ppermute | solution.py:586
  99.8 0.9 copy-start
  111.6 12.3 %collective-permute-start.4 = (f32[100,8,128]{2,1,0:T(8,128)}, f32[100,8,128]{2,1,0:T(8,128)S(1)}, u32[]{:S(2)}, u32[]{:S(2)}) collective-permute-start(f32[100,8,128]{2,1,0:T(8,128)} %get-tuple-element.28), channel_id=1, source_target_pairs={{0,128},{128,0},{1,129},{129,1},{2,130},{130,2},{3,131},{131,3},{4... | collective-permute-start | bytes 1228808 | tf_op jit(solution)/shard_map/ppermute | solution.py:582
  112.8 9.4 %collective-permute-start.5 = (f32[64,8,128]{2,1,0:T(8,128)}, f32[64,8,128]{2,1,0:T(8,128)S(1)}, u32[]{:S(2)}, u32[]{:S(2)}) collective-permute-start(f32[64,8,128]{2,1,0:T(8,128)} %get-tuple-element.29), channel_id=1, source_target_pairs={{0,1},{1,2},{2,3},{3,4},{4,5},{5,6},{6,7},{7,8},{8,9},{9,10},{10,1... | collective-permute-start | bytes 786440 | tf_op jit(solution)/shard_map/ppermute | solution.py:583
  114.7 9.1 %collective-permute-start.6 = (f32[64,8,128]{2,1,0:T(8,128)}, f32[64,8,128]{2,1,0:T(8,128)S(1)}, u32[]{:S(2)}, u32[]{:S(2)}) collective-permute-start(f32[64,8,128]{2,1,0:T(8,128)} %get-tuple-element.30), channel_id=1, source_target_pairs={{1,0},{2,1},{3,2},{4,3},{5,4},{6,5},{7,6},{8,7},{9,8},{10,9},{11,1... | collective-permute-start | bytes 786440 | tf_op jit(solution)/shard_map/ppermute | solution.py:584
  122.2 1.6 %copy-start.2 = (f32[64,8,128]{2,1,0:T(8,128)}, f32[64,8,128]{2,1,0:T(8,128)S(1)}, u32[]{:S(2)}) copy-start(f32[64,8,128]{2,1,0:T(8,128)S(1)} %collective-permute-done.5.zh2) | copy-start | bytes 786436
  123.8 0.7 copy-start.3
  123.8 0.8 copy-start.1

commit v2 on v1

--- a/solution.py
+++ b/solution.py
@@ -68,7 +68,7 @@
 
 
 def transform_kernel(
-    sc, fine, coarse, win, wf, wc, e0t, w2t, w1t, rim_out, outer_out, zho, zlo, rhs_out, wco_out,
+    sc, fine, coarse, win, wf, wc, e0t, w2t, w1t, rim_out, outer_out, zho, zlo, own_out,
     shi, slo, xhi, xlo, pq, ang, e0, w2, wm, gbuf,
 ):
     step = pl.program_id(0)
@@ -95,8 +95,7 @@
         own, above, below = rows_of(w1t[...], o1)
         mutual = jnp.where(odd == 0, above, below)
         outer = jnp.where(odd == 0, below, above)
-        wm[...] = doubled(jnp.concatenate([mutual, outer], axis=0))
-        wco_out[...] = doubled(own)
+        wm[...] = doubled(jnp.concatenate([mutual, outer, own], axis=0))
 
     @pl.when((step == 0) | (step == 3))
     def _():
@@ -146,14 +145,14 @@
         for which in range(2):
             out = dot(gbuf[which], w2[which])
             out = out[:, :B] + out[:, B:]
-            pq[which * 64 + j] = out[:NTR]
-            pq[which * 64 + j + 1] = out[NTR:]
-
-    def hold(even, odd_part):
+            for i in range(8):
+                pq[which * 64 + j + i] = out[i * NTR : i * NTR + NTR]
+
+    def hold(slot, even, odd_part):
         for which, pair in ((0, even), (1, odd_part)):
             wide = [jnp.concatenate([g[:NTR], g[NTR:]], axis=1) for g in pair]
             hi, lo = split(jnp.concatenate(wide, axis=0))
-            gbuf[which] = jnp.concatenate([hi, lo], axis=1)
+            gbuf[which, slot * 208 : slot * 208 + 208] = jnp.concatenate([hi, lo], axis=1)
 
     def first(k, kk, lo_pair):
         hi = jnp.concatenate([xhi[k], xhi[kk]], axis=1)
@@ -179,26 +178,25 @@
         even0 = out[:, :B]
         odd0 = jnp.concatenate([-half[NTR:], half[:NTR]], axis=0)
         even1, odd1 = inner_pair(1)
-        hold((even0, even1), (odd0, odd1))
-
-        def near(i, _):
-            along_xline(2 * i - 2)
-            ea, oa = inner_pair(2 * i)
-            eb, ob = inner_pair(2 * i + 1)
-            hold((ea, eb), (oa, ob))
-            return 0
-
-        lax.fori_loop(1, 16, near, 0, unroll=3)
-
-        def far(i, _):
-            along_xline(2 * i - 2)
-            ea, oa = outer_pair(2 * i)
-            eb, ob = outer_pair(2 * i + 1)
-            hold((ea, eb), (oa, ob))
-            return 0
-
-        lax.fori_loop(16, 32, far, 0, unroll=2)
-        along_xline(62)
+        hold(0, (even0, even1), (odd0, odd1))
+
+        def group(pair, i, slots):
+            for slot in slots:
+                (ea, oa), (eb, ob) = pair(8 * i + 2 * slot), pair(8 * i + 2 * slot + 1)
+                hold(slot, (ea, eb), (oa, ob))
+
+        def eight(pair):
+            def body(i, _):
+                along_xline(8 * i - 8)
+                group(pair, i, range(4))
+                return 0
+
+            return body
+
+        group(inner_pair, 0, range(1, 4))
+        lax.fori_loop(1, 4, eight(inner_pair), 0)
+        lax.fori_loop(4, 8, eight(outer_pair), 0)
+        along_xline(56)
         rim_out[13 * 8 : 14 * 8] = jnp.full((8, 40, B), o2.astype(F32), F32)
 
     @pl.when(step >= 4)
@@ -209,13 +207,13 @@
             x = jnp.concatenate([pq[:, n0 + 2 * pair, :], pq[:, n0 + 2 * pair + 1, :]], axis=1)
             hi, lo = split(x)
             rhs = jnp.concatenate([hi, lo], axis=0)
-            rhs_out[pair] = rhs
             out = dot(wm[...], rhs)
-            out = out[:80] + out[80:]
+            out = out[:144] + out[144:]
             for half in range(2):
                 part = out[:, half * B : half * B + B]
                 rim_out[n0 + 2 * pair + half] = part[:40]
-                outer_out[2 * pair + half] = part[40:]
+                outer_out[2 * pair + half] = part[40:80]
+                own_out[2 * pair + half] = part[80:]
                 for b in range(5):
                     near, far = two_sides(part[40 + 8 * b : 48 + 8 * b], o2)
                     ahead.append(near)
@@ -251,16 +249,14 @@
             pl.BlockSpec((26, 40, B), late_step),
             pl.BlockSpec((44, 8, B), late_step),
             pl.BlockSpec((44, 8, B), late_step),
-            pl.BlockSpec((13, 256, 256), late_step),
-            whole,
+            pl.BlockSpec((26, 64, B), late_step),
         ],
         out_shape=[
             jax.ShapeDtypeStruct((NTR + 8, 40, B), F32),
             jax.ShapeDtypeStruct((NTR, 40, B), F32),
             jax.ShapeDtypeStruct((4 * 44, 8, B), F32),
             jax.ShapeDtypeStruct((4 * 44, 8, B), F32),
-            jax.ShapeDtypeStruct((NTR // 2, 256, 256), BF16),
-            jax.ShapeDtypeStruct((128, 256), BF16),
+            jax.ShapeDtypeStruct((NTR, 64, B), F32),
         ],
         scratch_shapes=[
             VMEM((256, 32, B), BF16),
@@ -271,34 +267,14 @@
             VMEM((B, B), F32),
             VMEM((208, 768), BF16),
             VMEM((2, 512, 256), BF16),
-            VMEM((160, 256), BF16),
-            VMEM((2, 208, 512), BF16),
+            VMEM((288, 256), BF16),
+            VMEM((2, 832, 512), BF16),
         ],
         compiler_params=pltpu.CompilerParams(
             dimension_semantics=("arbitrary",), vmem_limit_bytes=63 * 2**20
         ),
         cost_estimate=pl.CostEstimate(flops=2 * 10**10, bytes_accessed=30 * 10**6, transcendentals=0),
     )(scalars, fine, coarse, *tabs)
-
-
-def own_rows_kernel(rhs, wco, out):
-    for pair in range(13):
-        x = dot(wco[...], rhs[pair])
-        x = x[:64] + x[64:]
-        out[2 * pair] = x[:, :B]
-        out[2 * pair + 1] = x[:, B:]
-
-
-def own_rows(rhs, wco):
-    return pl.pallas_call(
-        own_rows_kernel,
-        grid=(4,),
-        in_specs=[pl.BlockSpec((13, 256, 256), lambda s: (s, 0, 0)), pl.BlockSpec(memory_space=VMEM)],
-        out_specs=pl.BlockSpec((26, 64, B), lambda s: (s, 0, 0)),
-        out_shape=jax.ShapeDtypeStruct((NTR, 64, B), F32),
-        compiler_params=pltpu.CompilerParams(dimension_semantics=("arbitrary",), vmem_limit_bytes=63 * 2**20),
-        cost_estimate=pl.CostEstimate(flops=52 * 2 * 128 * 256 * 256, bytes_accessed=11 * 10**6, transcendentals=0),
-    )(rhs, wco)
 
 
 def lanes():
@@ -336,7 +312,7 @@
     place = jnp.clip(place, 0, 4)
     other = rim[t, pl.ds(pl.multiple_of(place * 8, 8), 8), :]
     other = jnp.where(valid, other, 0.0)
-    upto = lanes().astype(F32) < 88.0 + mate[0, 0:8, :]
+    upto = lanes().astype(F32) < 88.0 + mate[NTR, 0:8, :]
     return near + jnp.where(upto, other, 0.0), far + jnp.where(upto, 0.0, other)
 
 
@@ -345,135 +321,143 @@
         out[g] = pack3(pieces[3 * g : 3 * g + 3], start)
 
 
-def call(kernel, grid, in_specs, outs, count, *args):
+def call(kernel, shapes, *args, scratch=(), weight=1000):
     return pl.pallas_call(
         kernel,
-        grid=(grid,),
-        in_specs=[pl.BlockSpec(memory_space=SMEM)] + in_specs,
-        out_specs=[pl.BlockSpec(block, index) for _, block, index in outs],
-        out_shape=[jax.ShapeDtypeStruct(shape, F32) for shape, _, _ in outs],
-        compiler_params=pltpu.CompilerParams(dimension_semantics=("arbitrary",), vmem_limit_bytes=63 * 2**20),
-        cost_estimate=pl.CostEstimate(flops=10**6, bytes_accessed=count, transcendentals=0),
+        in_specs=[pl.BlockSpec(memory_space=SMEM)] + [WHOLE] * (len(args) - 1),
+        out_specs=[WHOLE] * len(shapes),
+        out_shape=[jax.ShapeDtypeStruct(shape, F32) for shape in shapes],
+        scratch_shapes=scratch,
+        compiler_params=pltpu.CompilerParams(vmem_limit_bytes=20 * 2**20),
+        cost_estimate=pl.CostEstimate(flops=1000, bytes_accessed=weight, transcendentals=0),
     )(*args)
 
 
-def each(s):
-    return (s, 0, 0)
-
-
-def core(s):
-    return (jnp.minimum(s, 7), 0, 0)
-
-
-def edge(s):
-    return (jnp.maximum(s - 8, 0), 0, 0)
-
-
 WHOLE = pl.BlockSpec(memory_space=VMEM)
-OWN_SPECS = [
-    pl.BlockSpec((8, 64, B), each),
-    pl.BlockSpec((8, 40, B), each),
-    pl.BlockSpec((8, 40, B), lambda s: (13, 0, 0)),
-]
-
-
-def pack_kernel(sc, own, rim, mate, zhc, zlc, tmsg):
-    step = pl.program_id(0)
-    ahead, behind = [], []
-    for t in range(8):
-        for b in range(5):
-            near, far = merged(own, rim, mate, t, b, sc)
-            ahead.append(near)
-            behind.append(far)
-    pack_many(ahead, zhc, 64)
-    pack_many(behind, zlc, 88)
-
-    @pl.when(step >= 8)
-    def _():
-        lane = lanes()
+
+
+def part(ref, step, size):
+    return ref.at[pl.ds(step * size, size)]
+
+
+def loop(low, high, body):
+    def run(i, _):
+        body(i)
+        return 0
+
+    lax.fori_loop(low, high, run, 0)
+
+
+def pack_time_kernel(sc, own_all, rim_all, tmsg):
+    lane = lanes()
+
+    def rims(step):
+        own, rim, out = part(own_all, step, 8), part(rim_all, step, 8), part(tmsg, step - 8, 27)
         extra = None
         for t in range(8):
             for b in range(3):
-                near, far = merged(own, rim, mate, t, b + 5, sc)
+                near, far = merged(own, rim, rim_all, t, b + 5, sc)
                 q = t * 3 + b
-                tmsg[q] = jnp.where(lane < 104, near, far)
+                out[q] = jnp.where(lane < 104, near, far)
                 moved = turn(far, 16 * (q % 8) - 88)
                 extra = moved if q % 8 == 0 else jnp.where(lane < 16 * (q % 8), extra, moved)
                 if q % 8 == 7:
-                    tmsg[24 + q // 8] = extra
-
-
-def pack(sc, own, rim):
-    outs = [
-        ((13 * 14, 8, B), (14, 8, B), each),
-        ((13 * 14, 8, B), (14, 8, B), each),
-        ((5 * 27, 8, B), (27, 8, B), edge),
-    ]
-    return call(pack_kernel, 13, OWN_SPECS, outs, 9 * 10**6, sc, own, rim, rim)
-
-
-def outer_middle_kernel(sc, outer, zh, zl, own, msg):
+                    out[24 + q // 8] = extra
+
+    loop(8, 13, rims)
+
+
+def pack_xline_kernel(sc, own_all, rim_all, zhc, zlc):
+    def every(step):
+        own, rim = part(own_all, step, 8), part(rim_all, step, 8)
+        ahead, behind = [], []
+        for t in range(8):
+            for b in range(5):
+                near, far = merged(own, rim, rim_all, t, b, sc)
+                ahead.append(near)
+                behind.append(far)
+        pack_many(ahead, part(zhc, step, 14), 64)
+        pack_many(behind, part(zlc, step, 14), 88)
+
+    loop(0, 13, every)
+
+
+def outer_middle_kernel(sc, outer_all, zho_all, zlo_all, tmo, own, held):
     lane = lanes()
 
-    def summed(t, b):
-        q = lax.rem(t, 26) * 5 + b
-        g, place = lax.div(t, 26) * 44 + lax.div(q, 3), lax.rem(q, 3)
-        low = pltpu.roll(zh[g], lax.rem(B - 40 * place, B), 1)
-        high = pltpu.roll(zl[g], lax.rem(B + 24 - 40 * place, B), 1)
-        low = jnp.where(lane < 40, low, 0.0)
-        high = jnp.where((lane >= 24) & (lane < 64), high, 0.0)
-        return outer[t, 8 * b : 8 * b + 8, :] + low + high
-
-    def core_rows(t, _):
+    def outers(step):
+        zh, zl = part(zho_all, step, 44), part(zlo_all, step, 44)
+        outer, out = part(outer_all, step, 26), part(held, step, 26)
+        for t in range(26):
+            for b in range(5):
+                q = t * 5 + b
+                sides = unpack3(zh[q // 3], q % 3, 0) + unpack3(zl[q // 3], q % 3, 24)
+                out[t, 8 * b : 8 * b + 8, :] = outer[t, 8 * b : 8 * b + 8, :] + sides
+
+    def outer_rims(p):
         for b in range(5):
-            own[t, 8 * b : 8 * b + 8, :] = summed(t, b)
-        return 0
-
-    def rim_rows(p, _):
-        for b in range(5):
-            even, odd = summed(64 + 2 * p, b), summed(65 + 2 * p, b)
-            msg[p * 5 + b] = jnp.where(lane < 64, even, pltpu.roll(odd, 64, 1))
-        return 0
-
-    lax.fori_loop(0, 20, rim_rows, 0, unroll=2)
-    lax.fori_loop(0, 64, core_rows, 0, unroll=4)
-
-
-def outer_middle(sc, outer, zh, zl):
-    outs = [((64, 40, B), (64, 40, B), lambda s: (0, 0, 0)), ((100, 8, B), (100, 8, B), lambda s: (0, 0, 0))]
-    return call(outer_middle_kernel, 1, [WHOLE] * 3, outs, 5 * 10**6, sc, outer, zh, zl)
-
-
-def middle_kernel(sc, own, rim, mate, zhc, zlc, tmsg, own1, tmc, zh2, zl2, own2):
-    step = pl.program_id(0)
+            rows = slice(8 * b, 8 * b + 8)
+            tmo[p * 5 + b] = jnp.where(lane < 64, held[64 + 2 * p, rows, :], turn(held[65 + 2 * p, rows, :], 64))
+
+    loop(0, 4, outers)
+    loop(0, 20, outer_rims)
+    own[...] = held[0:64]
+
+
+def pack_time(sc, own, rim):
+    return call(pack_time_kernel, [(5 * 27, 8, B)], sc, own, rim)[0]
+
+
+def pack_xline(sc, own, rim):
+    return call(pack_xline_kernel, [(13 * 14, 8, B), (13 * 14, 8, B)], sc, own, rim, weight=10**8)
+
+
+def outer_middle(sc, outer, zho, zlo):
+    scratch = [VMEM((NTR, 40, B), F32)]
+    return call(outer_middle_kernel, [(100, 8, B), (64, 40, B)], sc, outer, zho, zlo, scratch=scratch, weight=10**8)
+
+
+def middle_kernel(
+    sc, own_all, rim_all, zhc_all, zlc_all, tmsg, outer_all, tmo,
+    own1_all, tmc_all, zh2_all, zl2_all, own2_all, dmsg_all,
+):
     lane = lanes()
 
-    def first_rows(t, b):
-        near, _ = merged(own, rim, mate, t, b, sc)
-        q = t * 5 + b
-        return near + unpack3(zhc[q // 3], q % 3, 0) + unpack3(zlc[q // 3], q % 3, 24)
-
-    @pl.when(step >= 8)
-    def _():
+    def views(step):
+        own, rim = part(own_all, step, 8), part(rim_all, step, 8)
+        zhc, zlc = part(zhc_all, step, 14), part(zlc_all, step, 14)
+
+        def first_rows(t, b):
+            near, _ = merged(own, rim, rim_all, t, b, sc)
+            q = t * 5 + b
+            return near + unpack3(zhc[q // 3], q % 3, 0) + unpack3(zlc[q // 3], q % 3, 24)
+
+        return own, rim, first_rows
+
+    def rims(step):
+        _, _, first_rows = views(step)
+        tmc = part(tmc_all, step - 8, 20)
         for t in range(0, 8, 2):
             for b in range(5):
                 tmc[t // 2 * 5 + b] = jnp.where(lane < 64, first_rows(t, b), turn(first_rows(t + 1, b), 64))
 
-    @pl.when(step < 8)
-    def _():
+    def cores(step):
+        own, rim, first_rows = views(step)
+        own1, own2 = part(own1_all, step, 8), part(own2_all, step, 8)
+        zh2, zl2 = part(zh2_all, step, 8), part(zl2_all, step, 8)
         for t in range(8):
             for b in range(5):
                 own1[t, 8 * b : 8 * b + 8, :] = first_rows(t, b)
         place = step - jnp.where(sc[3] == 0, 3, 0)
         valid = (place >= 0) & (place < 5)
-        base = jnp.clip(place, 0, 4) * 27
+        msg = part(tmsg, jnp.clip(place, 0, 4), 27)
         for t in range(8):
             ahead, behind = [], []
             for b in range(3):
                 q = t * 3 + b
-                near, far = merged(own, rim, mate, t, b + 5, sc)
-                main = tmsg[base + q]
-                moved = turn(tmsg[base + 24 + q // 8], 88 - 16 * (q % 8))
+                near, far = merged(own, rim, rim_all, t, b + 5, sc)
+                main = msg[q]
+                moved = turn(msg[24 + q // 8], 88 - 16 * (q % 8))
                 near = near + jnp.where(valid & (lane < 104), main, 0.0)
                 far2 = jnp.where(lane >= 104, main, jnp.where(lane >= 88, moved, 0.0))
                 far = far + jnp.where(valid, far2, 0.0)
@@ -483,17 +467,21 @@
             zh2[t] = pack3(ahead, 64)
             zl2[t] = pack3(behind, 88)
 
-
-def middle(sc, own, rim, zhc, zlc, tmsg):
-    outs = [
-        ((64, 40, B), (8, 40, B), core),
-        ((100, 8, B), (20, 8, B), edge),
-        ((64, 8, B), (8, 8, B), core),
-        ((64, 8, B), (8, 8, B), core),
-        ((64, 24, B), (8, 24, B), core),
-    ]
-    msgs = [pl.BlockSpec((14, 8, B), each), pl.BlockSpec((14, 8, B), each), WHOLE]
-    return call(middle_kernel, 13, OWN_SPECS + msgs, outs, 11 * 10**6, sc, own, rim, rim, zhc, zlc, tmsg)
+    def outers(step):
+        own, dmsg = part(outer_all, step, 8), part(dmsg_all, step, 20)
+        for t in range(0, 8, 2):
+            for b in range(5):
+                even, odd = time_rows(sc, own, tmo, step, t, b), time_rows(sc, own, tmo, step, t + 1, b)
+                dmsg[t // 2 * 5 + b] = jnp.where(lane < 64, even, turn(odd, 64))
+
+    loop(8, 13, rims)
+    loop(0, 8, outers)
+    loop(0, 8, cores)
+
+
+def middle(sc, *args):
+    shapes = [(64, 40, B), (100, 8, B), (64, 8, B), (64, 8, B), (64, 24, B), (160, 8, B)]
+    return call(middle_kernel, shapes, sc, *args)
 
 
 def time_rows(sc, own, msg, step, t, b):
@@ -504,49 +492,32 @@
     return own[t, 8 * b : 8 * b + 8, :] + jnp.where(valid, both, 0.0)
 
 
-def outer_late_kernel(sc, own, msg, dmsg):
-    step = pl.program_id(0)
-    lane = lanes()
-    for t in range(0, 8, 2):
-        for b in range(5):
-            even, odd = time_rows(sc, own, msg, step, t, b), time_rows(sc, own, msg, step, t + 1, b)
-            dmsg[t // 2 * 5 + b] = jnp.where(lane < 64, even, turn(odd, 64))
-
-
-def outer_late(sc, own, msg):
-    outs = [((160, 8, B), (20, 8, B), each)]
-    return call(outer_late_kernel, 8, [pl.BlockSpec((8, 40, B), each), WHOLE], outs, 2 * 10**6, sc, own, msg)[0]
-
-
-def last_kernel(sc, own1, tmc, zh2, zl2, own2, dmsg, out):
-    step = pl.program_id(0)
+def last_kernel(sc, own1_all, tmc, zh2_all, zl2_all, own2_all, dmsg_all, out_all):
     shift = jnp.where(sc[4] == 0, 0, 3)
-    for t in range(8):
-        for b in range(8):
-            if b < 5:
-                value = time_rows(sc, own1, tmc, step, t, b)
-            else:
-                value = own2[t, 8 * (b - 5) : 8 * (b - 5) + 8, :]
-                value = value + unpack3(zh2[t], b - 5, 0) + unpack3(zl2[t], b - 5, 24)
-            place = b - shift
-            valid = (place >= 0) & (place < 5)
-            other = dmsg[t // 2 * 5 + jnp.clip(place, 0, 4)]
-            other = other if t % 2 == 0 else turn(other, 64)
-            value = value + jnp.where(valid, other, 0.0)
-            out[t, 8 * b : 8 * b + 8, :] = value[:, :64]
+
+    def body(step):
+        own1, own2 = part(own1_all, step, 8), part(own2_all, step, 8)
+        zh2, zl2 = part(zh2_all, step, 8), part(zl2_all, step, 8)
+        dmsg, out = part(dmsg_all, step, 20), part(out_all, step, 8)
+        for t in range(8):
+            for b in range(8):
+                if b < 5:
+                    value = time_rows(sc, own1, tmc, step, t, b)
+                else:
+                    value = own2[t, 8 * (b - 5) : 8 * (b - 5) + 8, :]
+                    value = value + unpack3(zh2[t], b - 5, 0) + unpack3(zl2[t], b - 5, 24)
+                place = b - shift
+                valid = (place >= 0) & (place < 5)
+                other = dmsg[t // 2 * 5 + jnp.clip(place, 0, 4)]
+                other = other if t % 2 == 0 else turn(other, 64)
+                value = value + jnp.where(valid, other, 0.0)
+                out[t, 8 * b : 8 * b + 8, :] = value[:, :64]
+
+    loop(0, 8, body)
 
 
 def last(sc, own1, tmc, zh2, zl2, own2, dmsg):
-    specs = [
-        pl.BlockSpec((8, 40, B), each),
-        WHOLE,
-        pl.BlockSpec((8, 8, B), each),
-        pl.BlockSpec((8, 8, B), each),
-        pl.BlockSpec((8, 24, B), each),
-        pl.BlockSpec((20, 8, B), each),
-    ]
-    outs = [((64, 64, 64), (8, 64, 64), each)]
-    return call(last_kernel, 8, specs, outs, 7 * 10**6, sc, own1, tmc, zh2, zl2, own2, dmsg)[0]
+    return call(last_kernel, [(64, 64, 64)], sc, own1, tmc, zh2, zl2, own2, dmsg)[0]
 
 
 def local(coef_fine, coef_coarse, kept, tile_offsets):
@@ -566,24 +537,22 @@
     mates = [(i, i ^ 1) for i in range(n_in)]
     facing = [p for i in range(1, n_in - 1, 2) for p in ((i, i + 1), (i + 1, i))]
 
-    rim, outer, zho, zlo, rhs, wco = transform(sc, coef_fine, coef_coarse, tabs)
+    rim, outer, zho, zlo, own = transform(sc, coef_fine, coef_coarse, tabs)
     rim = lax.ppermute(rim, "inline", mates)
     zho = lax.ppermute(zho, ("inline", "xline"), along_o)
     zlo = lax.ppermute(zlo, ("inline", "xline"), back_o)
-    own = own_rows(rhs, wco)
-
-    zhc, zlc, tmsg = pack(sc, own, rim)
+    tmsg = pack_time(sc, own, rim)
     tmsg = lax.ppermute(tmsg, "tm", times)
+    zhc, zlc = pack_xline(sc, own, rim)
     zhc = lax.ppermute(zhc, "xline", along)
     zlc = lax.ppermute(zlc, "xline", back)
-    outer, tmo = outer_middle(sc, outer, zho, zlo)
+    tmo, outer = outer_middle(sc, outer, zho, zlo)
     tmo = lax.ppermute(tmo, ("tm", "inline"), times_o)
-    own1, tmc, zh2, zl2, own2 = middle(sc, own, rim, zhc, zlc, tmsg)
+    own1, tmc, zh2, zl2, own2, dmsg = middle(sc, own, rim, zhc, zlc, tmsg, outer, tmo)
+    dmsg = lax.ppermute(dmsg, "inline", facing)
     tmc = lax.ppermute(tmc, "tm", times)
     zh2 = lax.ppermute(zh2, "xline", along)
     zl2 = lax.ppermute(zl2, "xline", back)
-    dmsg = outer_late(sc, outer, tmo)
-    dmsg = lax.ppermute(dmsg, "inline", facing)
     return last(sc, own1, tmc, zh2, zl2, own2, dmsg)
 
 

time: 133 us -> 98.2 us (0.74)
  Pallas kernels: 83.9 us -> 46.2 us
  waiting for transfers between devices: 11.1 us -> 14.9 us
    pallas_call x6 -> x5, Pallas kernels: 49.6 us -> 15.3 us  [call(): pl.pallas_call(kernel, in_specs=[pl.BlockSpec(memory_space=SMEM)] + [WHOL...]
    pallas_call x1, Pallas kernels: 34.3 us -> 30.9 us  [transform(): pl.pallas_call(transform_kernel, grid=(8,), in_specs=[pl.BlockSpec(memory...]
    ppermute x1, waiting for transfers between devices: 7.43 us -> 9.99 us  [local(): tmo = lax.ppermute(tmo, ('tm', 'inline'), times_o)]
    ppermute x1, waiting for transfers between devices: 0.01 us -> 1.56 us  [local(): tmc = lax.ppermute(tmc, 'tm', times)]
  transfers between devices with their start and end apart: 11 -> 11, of which waited for: 3 -> 4; matrix products, arithmetic and copies ran while one was open for 0% -> 0% of each run, Pallas kernels for 32% -> 7%
where the time goes in v2:
time: 98.2 us; the launch traced here: 97.6 us
  Pallas kernels  46.2 us (47%)
  starting transfers between devices  33.2 us (34%)
  waiting for transfers between devices  14.9 us (15%)
  local copies, waits for them, and re-layouts  1.97 us (2%)
  other arithmetic  1.29 us (1%)
    pallas_call x1, Pallas kernels, transform(): pl.pallas_call(transform_kernel, grid=(8,), in_specs=[pl.BlockSpec(memory...  30.9 us
    pallas_call x5, Pallas kernels, call(): pl.pallas_call(kernel, in_specs=[pl.BlockSpec(memory_space=SMEM)] + [WHOL...  15.3 us
    ppermute x1, waiting for transfers between devices, local(): tmo = lax.ppermute(tmo, ('tm', 'inline'), times_o)  9.99 us
    ppermute x1, starting transfers between devices, local(): zlo = lax.ppermute(zlo, ('inline', 'xline'), back_o)  6.06 us
    ppermute x1, starting transfers between devices, local(): zlc = lax.ppermute(zlc, 'xline', back)  5.6 us
    ppermute x1, starting transfers between devices, local(): zl2 = lax.ppermute(zl2, 'xline', back)  5.47 us
    ppermute x1, starting transfers between devices, local(): zho = lax.ppermute(zho, ('inline', 'xline'), along_o)  3.51 us
    ppermute x1, starting transfers between devices, local(): dmsg = lax.ppermute(dmsg, 'inline', facing)  3.21 us
  transfers between devices with their start and end apart: 11, of which 4 were waited for; matrix products, arithmetic and copies ran while one was open for 0% of the time, Pallas kernels for 7%

profile of v2, /device:TPU:27, one launch (start us, length us, event | category | flops | bytes accessed | tf_op | source)
XLA Modules:
  0.0 97.6 jit_solution(13071311589408177143)
XLA Ops:
  0.0 1.3 %pad_add_fusion.sc = s32[11]{0:T(128)} fusion(s32[6]{0:T(128)} %bitcast.4, s32[1]{0:T(128)} %bitcast.2, s32[1]{0:T(128)} %bitcast.1, s32[3]{0:T(128)} %bitcast.5), kind=kLoop, calls=%fused_computation | loop fusion | flops 33 | bytes 88 | tf_op jit(solution)/shard_map/concatenate | solution.py:528
  1.3 30.9 %shard_map.100 = (f32[112,40,128]{2,1,0:T(8,128)}, f32[104,40,128]{2,1,0:T(8,128)}, f32[176,8,128]{2,1,0:T(8,128)}, f32[176,8,128]{2,1,0:T(8,128)}, f32[104,64,128]{2,1,0:T(8,128)}) custom-call(s32[11]{0:T(128)} %pad_add_fusion.sc, bf16[2,128,128,128]{3,2,1,0:T(8,128)(2,1)} %fine.1, bf16[2,64,64,64]{3,2,1,0:T(8,128)(2,1)} %coarse.1, ...), custom_call_target="tpu_custom_call" | custom-call | flops 20000000000 | bytes 30000000 | tf_op jit(solution)/shard_map/pallas_call | solution.py:233
  32.2 0.8 collective-permute-start
  33.0 3.5 %collective-permute-start.4 = (f32[176,8,128]{2,1,0:T(8,128)}, f32[176,8,128]{2,1,0:T(8,128)S(1)}, u32[]{:S(2)}, u32[]{:S(2)}) collective-permute-start(f32[176,8,128]{2,1,0:T(8,128)} %get-tuple-element.25), channel_id=1, source_target_pairs={{32,33},{33,34},{34,35},{35,36},{36,37},{37,38},{38,39},{39,40},{4... | collective-permute-start | bytes 2162696 | tf_op jit(solution)/shard_map/ppermute | solution.py:542
  36.5 6.1 %collective-permute-start.5 = (f32[176,8,128]{2,1,0:T(8,128)}, f32[176,8,128]{2,1,0:T(8,128)S(1)}, u32[]{:S(2)}, u32[]{:S(2)}) collective-permute-start(f32[176,8,128]{2,1,0:T(8,128)} %get-tuple-element.26), channel_id=1, source_target_pairs={{33,32},{34,33},{35,34},{36,35},{37,36},{38,37},{39,38},{40,39},{4... | collective-permute-start | bytes 2162696 | tf_op jit(solution)/shard_map/ppermute | solution.py:543
  42.5 0.0 collective-permute-done.rim_all
  42.6 0.0 copy-done.3
  42.6 2.0 %copy-done = f32[104,64,128]{2,1,0:T(8,128)S(1)} copy-done((f32[104,64,128]{2,1,0:T(8,128)S(1)}, f32[104,64,128]{2,1,0:T(8,128)}, u32[]{:S(2)}) %copy-start) | copy-done | bytes 3407896
  44.5 2.7 %shard_map.101 = (f32[182,8,128]{2,1,0:T(8,128)S(1)}, f32[182,8,128]{2,1,0:T(8,128)S(1)}) custom-call(s32[11]{0:T(128)S(1)} %copy-done.3, f32[104,64,128]{2,1,0:T(8,128)S(1)} %copy-done, f32[112,40,128]{2,1,0:T(8,128)S(1)} %collective-permute-done.rim_all), custom_call_target="tpu_custom_call" | custom-call | flops 1000 | bytes 100000000 | tf_op jit(solution)/shard_map/pallas_call | solution.py:325
  47.2 1.9 %collective-permute-start.1 = (f32[182,8,128]{2,1,0:T(8,128)S(1)}, f32[182,8,128]{2,1,0:T(8,128)S(1)}, u32[]{:S(2)}, u32[]{:S(2)}) collective-permute-start(f32[182,8,128]{2,1,0:T(8,128)S(1)} %get-tuple-element.22), channel_id=1, source_target_pairs={{0,1},{1,2},{2,3},{3,4},{4,5},{5,6},{6,7},{7,8},{8,9},{9,10},{10,1... | collective-permute-start | bytes 2236424 | tf_op jit(solution)/shard_map/ppermute | solution.py:547
  49.1 5.6 %collective-permute-start.2 = (f32[182,8,128]{2,1,0:T(8,128)S(1)}, f32[182,8,128]{2,1,0:T(8,128)S(1)}, u32[]{:S(2)}, u32[]{:S(2)}) collective-permute-start(f32[182,8,128]{2,1,0:T(8,128)S(1)} %get-tuple-element.23), channel_id=1, source_target_pairs={{1,0},{2,1},{3,2},{4,3},{5,4},{6,5},{7,6},{8,7},{9,8},{10,9},{11,1... | collective-permute-start | bytes 2236424 | tf_op jit(solution)/shard_map/ppermute | solution.py:548
  54.7 1.1 %shard_map.102 = f32[135,8,128]{2,1,0:T(8,128)S(1)} custom-call(s32[11]{0:T(128)S(1)} %copy-done.3, f32[104,64,128]{2,1,0:T(8,128)S(1)} %copy-done, f32[112,40,128]{2,1,0:T(8,128)S(1)} %collective-permute-done.rim_all), custom_call_target="tpu_custom_call" | custom-call | flops 1000 | bytes 1000 | tf_op jit(solution)/shard_map/pallas_call | solution.py:325
  55.8 0.3 collective-permute-start.3
  56.1 0.0 collective-permute-done.4.zho_all
  56.2 0.0 collective-permute-done.5.zlo_all
  56.2 0.0 copy-done.2
  56.2 3.2 %shard_map.103 = (f32[100,8,128]{2,1,0:T(8,128)S(1)}, f32[64,40,128]{2,1,0:T(8,128)S(1)}) custom-call(s32[11]{0:T(128)S(1)} %copy-done.3, f32[104,40,128]{2,1,0:T(8,128)S(1)} %copy-done.2, f32[176,8,128]{2,1,0:T(8,128)S(1)} %collective-permute-done.4.zho_all, f32[176,8,128]{2,1,0:T(8,128)S(1)} %collective-permute-done.5.zlo_all), custom_call_target="tpu_custom_call" | custom-call | flops 1000 | bytes 100000000 | tf_op jit(solution)/shard_map/pallas_call | solution.py:325
  59.4 3.1 %collective-permute-start.6 = (f32[100,8,128]{2,1,0:T(8,128)S(1)}, f32[100,8,128]{2,1,0:T(8,128)S(1)}, u32[]{:S(2)}, u32[]{:S(2)}) collective-permute-start(f32[100,8,128]{2,1,0:T(8,128)S(1)} %get-tuple-element.28), channel_id=1, source_target_pairs={{32,160},{160,32},{64,192},{192,64},{33,161},{161,33},{65,193},{19... | collective-permute-start | bytes 1228808 | tf_op jit(solution)/shard_map/ppermute | solution.py:550
  62.5 10.0 %collective-permute-done.6.tmo = f32[100,8,128]{2,1,0:T(8,128)S(1)} collective-permute-done((f32[100,8,128]{2,1,0:T(8,128)S(1)}, f32[100,8,128]{2,1,0:T(8,128)S(1)}, u32[]{:S(2)}, u32[]{:S(2)}) %collective-permute-start.6) | collective-permute-done | bytes 409632 | tf_op jit(solution)/shard_map/ppermute | solution.py:550
  72.5 0.0 collective-permute-done.3.tmsg
  72.5 0.0 collective-permute-done.1.zhc_all
  72.5 0.0 collective-permute-done.2.zlc_all
  72.6 5.1 %shard_map.104 = (f32[64,40,128]{2,1,0:T(8,128)S(1)}, f32[100,8,128]{2,1,0:T(8,128)S(1)}, f32[64,8,128]{2,1,0:T(8,128)S(1)}, f32[64,8,128]{2,1,0:T(8,128)S(1)}, ...) custom-call(s32[11]{0:T(128)S(1)} %copy-done.3, f32[104,64,128]{2,1,0:T(8,128)S(1)} %copy-done.1, ...), custom_call_target="tpu_custom_call" | custom-call | flops 1000 | bytes 1000 | tf_op jit(solution)/shard_map/pallas_call | solution.py:325
  77.7 3.2 %collective-permute-start.10 = (f32[160,8,128]{2,1,0:T(8,128)S(1)}, f32[160,8,128]{2,1,0:T(8,128)S(1)}, u32[]{:S(2)}, u32[]{:S(2)}) collective-permute-start(f32[160,8,128]{2,1,0:T(8,128)S(1)} %get-tuple-element.34), channel_id=1, source_target_pairs={{32,64},{64,32},{33,65},{65,33},{34,66},{66,34},{35,67},{67,35},{3... | collective-permute-start | bytes 1966088 | tf_op jit(solution)/shard_map/ppermute | solution.py:552
  80.9 1.2 %collective-permute-start.7 = (f32[100,8,128]{2,1,0:T(8,128)S(1)}, f32[100,8,128]{2,1,0:T(8,128)S(1)}, u32[]{:S(2)}, u32[]{:S(2)}) collective-permute-start(f32[100,8,128]{2,1,0:T(8,128)S(1)} %get-tuple-element.30), channel_id=1, source_target_pairs={{0,128},{128,0},{1,129},{129,1},{2,130},{130,2},{3,131},{131,3},{4... | collective-permute-start | bytes 1228808 | tf_op jit(solution)/shard_map/ppermute | solution.py:553
  82.2 1.9 %collective-permute-start.8 = (f32[64,8,128]{2,1,0:T(8,128)S(1)}, f32[64,8,128]{2,1,0:T(8,128)S(1)}, u32[]{:S(2)}, u32[]{:S(2)}) collective-permute-start(f32[64,8,128]{2,1,0:T(8,128)S(1)} %get-tuple-element.31), channel_id=1, source_target_pairs={{0,1},{1,2},{2,3},{3,4},{4,5},{5,6},{6,7},{7,8},{8,9},{9,10},{10,1... | collective-permute-start | bytes 786440 | tf_op jit(solution)/shard_map/ppermute | solution.py:554
  84.1 5.5 %collective-permute-start.9 = (f32[64,8,128]{2,1,0:T(8,128)S(1)}, f32[64,8,128]{2,1,0:T(8,128)S(1)}, u32[]{:S(2)}, u32[]{:S(2)}) collective-permute-start(f32[64,8,128]{2,1,0:T(8,128)S(1)} %get-tuple-element.32), channel_id=1, source_target_pairs={{1,0},{2,1},{3,2},{4,3},{5,4},{6,5},{7,6},{8,7},{9,8},{10,9},{11,1... | collective-permute-start | bytes 786440 | tf_op jit(solution)/shard_map/ppermute | solution.py:555
  89.6 1.8 %collective-permute-done.8.zh2_all = f32[64,8,128]{2,1,0:T(8,128)S(1)} collective-permute-done((f32[64,8,128]{2,1,0:T(8,128)S(1)}, f32[64,8,128]{2,1,0:T(8,128)S(1)}, u32[]{:S(2)}, u32[]{:S(2)}) %collective-permute-start.8) | collective-permute-done | bytes 262176 | tf_op jit(solution)/shard_map/ppermute | solution.py:554
  91.4 1.5 %collective-permute-done.9.zl2_all = f32[64,8,128]{2,1,0:T(8,128)S(1)} collective-permute-done((f32[64,8,128]{2,1,0:T(8,128)S(1)}, f32[64,8,128]{2,1,0:T(8,128)S(1)}, u32[]{:S(2)}, u32[]{:S(2)}) %collective-permute-start.9) | collective-permute-done | bytes 262176 | tf_op jit(solution)/shard_map/ppermute | solution.py:555
  92.8 1.6 %collective-permute-done.7.tmc = f32[100,8,128]{2,1,0:T(8,128)S(1)} collective-permute-done((f32[100,8,128]{2,1,0:T(8,128)S(1)}, f32[100,8,128]{2,1,0:T(8,128)S(1)}, u32[]{:S(2)}, u32[]{:S(2)}) %collective-permute-start.7) | collective-permute-done | bytes 409632 | tf_op jit(solution)/shard_map/ppermute | solution.py:553
  94.4 0.0 collective-permute-done.10.dmsg_all
  94.4 3.2 %shard_map.105 = f32[64,64,64]{2,1,0:T(8,128)} custom-call(s32[11]{0:T(128)S(1)} %copy-done.3, f32[64,40,128]{2,1,0:T(8,128)S(1)} %get-tuple-element.29.own1_all, f32[100,8,128]{2,1,0:T(8,128)S(1)} %collective-permute-done.7.tmc, f32[64,8,128]{2,1,0:T(8,128)S(1)} %collective-permute-done.8.zh2_all, f32[64,8,128]{2,1,0:T(8,128)S(1)} %collective-permute-done.9.zl2_all, ...), custom_call_target="tpu_custom_call" | custom-call | flops 1000 | bytes 1000 | tf_op jit(solution)/shard_map/pallas_call | solution.py:325
  (5 shorter events, 0.0 us)
Async XLA Ops:
  1.3 41.3 %copy-start.3 = (s32[11]{0:T(128)S(1)}, s32[11]{0:T(128)}, u32[]{:S(2)}) copy-start(s32[11]{0:T(128)} %pad_add_fusion.sc) | copy-start | bytes 136
  32.2 10.4 %collective-permute-start = (f32[112,40,128]{2,1,0:T(8,128)}, f32[112,40,128]{2,1,0:T(8,128)S(1)}, u32[]{:S(2)}, u32[]{:S(2)}) collective-permute-start(f32[112,40,128]{2,1,0:T(8,128)} %get-tuple-element.21), channel_id=1, source_target_pairs={{0,32},{32,0},{64,96},{96,64},{1,33},{33,1},{65,97},{97,65},{2,34}... | collective-permute-start | bytes 6881288 | tf_op jit(solution)/shard_map/ppermute | solution.py:541
  33.0 23.2 %collective-permute-start.4 = (f32[176,8,128]{2,1,0:T(8,128)}, f32[176,8,128]{2,1,0:T(8,128)S(1)}, u32[]{:S(2)}, u32[]{:S(2)}) collective-permute-start(f32[176,8,128]{2,1,0:T(8,128)} %get-tuple-element.25), channel_id=1, source_target_pairs={{32,33},{33,34},{34,35},{35,36},{36,37},{37,38},{38,39},{39,40},{4... | collective-permute-start | bytes 2162696 | tf_op jit(solution)/shard_map/ppermute | solution.py:542
  36.5 19.7 %collective-permute-start.5 = (f32[176,8,128]{2,1,0:T(8,128)}, f32[176,8,128]{2,1,0:T(8,128)S(1)}, u32[]{:S(2)}, u32[]{:S(2)}) collective-permute-start(f32[176,8,128]{2,1,0:T(8,128)} %get-tuple-element.26), channel_id=1, source_target_pairs={{33,32},{34,33},{35,34},{36,35},{37,36},{38,37},{39,38},{40,39},{4... | collective-permute-start | bytes 2162696 | tf_op jit(solution)/shard_map/ppermute | solution.py:543
  42.6 2.0 %copy-start = (f32[104,64,128]{2,1,0:T(8,128)S(1)}, f32[104,64,128]{2,1,0:T(8,128)}, u32[]{:S(2)}) copy-start(f32[104,64,128]{2,1,0:T(8,128)} %get-tuple-element.20.own_all) | copy-start | bytes 10223620
  47.2 25.3 %collective-permute-start.1 = (f32[182,8,128]{2,1,0:T(8,128)S(1)}, f32[182,8,128]{2,1,0:T(8,128)S(1)}, u32[]{:S(2)}, u32[]{:S(2)}) collective-permute-start(f32[182,8,128]{2,1,0:T(8,128)S(1)} %get-tuple-element.22), channel_id=1, source_target_pairs={{0,1},{1,2},{2,3},{3,4},{4,5},{5,6},{6,7},{7,8},{8,9},{9,10},{10,1... | collective-permute-start | bytes 2236424 | tf_op jit(solution)/shard_map/ppermute | solution.py:547
  49.1 7.0 %copy-start.2 = (f32[104,40,128]{2,1,0:T(8,128)S(1)}, f32[104,40,128]{2,1,0:T(8,128)}, u32[]{:S(2)}) copy-start(f32[104,40,128]{2,1,0:T(8,128)} %get-tuple-element.24.outer_all) | copy-start | bytes 6389764
  49.1 23.4 %collective-permute-start.2 = (f32[182,8,128]{2,1,0:T(8,128)S(1)}, f32[182,8,128]{2,1,0:T(8,128)S(1)}, u32[]{:S(2)}, u32[]{:S(2)}) collective-permute-start(f32[182,8,128]{2,1,0:T(8,128)S(1)} %get-tuple-element.23), channel_id=1, source_target_pairs={{1,0},{2,1},{3,2},{4,3},{5,4},{6,5},{7,6},{8,7},{9,8},{10,9},{11,1... | collective-permute-start | bytes 2236424 | tf_op jit(solution)/shard_map/ppermute | solution.py:548
  55.8 16.7 %copy-start.1 = (f32[104,64,128]{2,1,0:T(8,128)S(1)}, f32[104,64,128]{2,1,0:T(8,128)}, u32[]{:S(2)}) copy-start(f32[104,64,128]{2,1,0:T(8,128)} %get-tuple-element.20.own_all) | copy-start | bytes 10223620
  55.8 16.7 %collective-permute-start.3 = (f32[135,8,128]{2,1,0:T(8,128)S(1)}, f32[135,8,128]{2,1,0:T(8,128)S(1)}, u32[]{:S(2)}, u32[]{:S(2)}) collective-permute-start(f32[135,8,128]{2,1,0:T(8,128)S(1)} %shard_map.102), channel_id=1, source_target_pairs={{0,128},{128,0},{1,129},{129,1},{2,130},{130,2},{3,131},{131,3},{4... | collective-permute-start | bytes 1658888 | tf_op jit(solution)/shard_map/ppermute | solution.py:545
  59.4 13.1 %collective-permute-start.6 = (f32[100,8,128]{2,1,0:T(8,128)S(1)}, f32[100,8,128]{2,1,0:T(8,128)S(1)}, u32[]{:S(2)}, u32[]{:S(2)}) collective-permute-start(f32[100,8,128]{2,1,0:T(8,128)S(1)} %get-tuple-element.28), channel_id=1, source_target_pairs={{32,160},{160,32},{64,192},{192,64},{33,161},{161,33},{65,193},{19... | collective-permute-start | bytes 1228808 | tf_op jit(solution)/shard_map/ppermute | solution.py:550
  77.7 16.7 %collective-permute-start.10 = (f32[160,8,128]{2,1,0:T(8,128)S(1)}, f32[160,8,128]{2,1,0:T(8,128)S(1)}, u32[]{:S(2)}, u32[]{:S(2)}) collective-permute-start(f32[160,8,128]{2,1,0:T(8,128)S(1)} %get-tuple-element.34), channel_id=1, source_target_pairs={{32,64},{64,32},{33,65},{65,33},{34,66},{66,34},{35,67},{67,35},{3... | collective-permute-start | bytes 1966088 | tf_op jit(solution)/shard_map/ppermute | solution.py:552
  80.9 13.5 %collective-permute-start.7 = (f32[100,8,128]{2,1,0:T(8,128)S(1)}, f32[100,8,128]{2,1,0:T(8,128)S(1)}, u32[]{:S(2)}, u32[]{:S(2)}) collective-permute-start(f32[100,8,128]{2,1,0:T(8,128)S(1)} %get-tuple-element.30), channel_id=1, source_target_pairs={{0,128},{128,0},{1,129},{129,1},{2,130},{130,2},{3,131},{131,3},{4... | collective-permute-start | bytes 1228808 | tf_op jit(solution)/shard_map/ppermute | solution.py:553
  82.2 9.2 %collective-permute-start.8 = (f32[64,8,128]{2,1,0:T(8,128)S(1)}, f32[64,8,128]{2,1,0:T(8,128)S(1)}, u32[]{:S(2)}, u32[]{:S(2)}) collective-permute-start(f32[64,8,128]{2,1,0:T(8,128)S(1)} %get-tuple-element.31), channel_id=1, source_target_pairs={{0,1},{1,2},{2,3},{3,4},{4,5},{5,6},{6,7},{7,8},{8,9},{9,10},{10,1... | collective-permute-start | bytes 786440 | tf_op jit(solution)/shard_map/ppermute | solution.py:554
  84.1 8.8 %collective-permute-start.9 = (f32[64,8,128]{2,1,0:T(8,128)S(1)}, f32[64,8,128]{2,1,0:T(8,128)S(1)}, u32[]{:S(2)}, u32[]{:S(2)}) collective-permute-start(f32[64,8,128]{2,1,0:T(8,128)S(1)} %get-tuple-element.32), channel_id=1, source_target_pairs={{1,0},{2,1},{3,2},{4,3},{5,4},{6,5},{7,6},{8,7},{9,8},{10,9},{11,1... | collective-permute-start | bytes 786440 | tf_op jit(solution)/shard_map/ppermute | solution.py:555

commit v3 on v2

--- a/solution.py
+++ b/solution.py
@@ -218,8 +218,7 @@
                     near, far = two_sides(part[40 + 8 * b : 48 + 8 * b], o2)
                     ahead.append(near)
                     behind.append(far)
-        pack_many(ahead, zho, 64)
-        pack_many(behind, zlo, 88)
+        pack_sides(ahead, behind, zho, zlo, sc)
 
 
 def transform(scalars, fine, coarse, tabs):
@@ -316,15 +315,29 @@
     return near + jnp.where(upto, other, 0.0), far + jnp.where(upto, 0.0, other)
 
 
-def pack_many(pieces, out, start):
-    for g in range((len(pieces) + 2) // 3):
-        out[g] = pack3(pieces[3 * g : 3 * g + 3], start)
-
-
-def call(kernel, shapes, *args, scratch=(), weight=1000):
+def pack_sides(ahead, behind, first, second, sc):
+    odd = sc[11] == 1
+    for g in range((len(ahead) + 2) // 3):
+        high = pack3(ahead[3 * g : 3 * g + 3], 64)
+        low = pack3(behind[3 * g : 3 * g + 3], 88)
+        first[g] = jnp.where(odd, low, high)
+        second[g] = jnp.where(odd, high, low)
+
+
+def unpack_sides(first, second, q, sc):
+    odd = sc[11] == 1
+    one, two = first[q // 3], second[q // 3]
+    before, after = jnp.where(odd, one, two), jnp.where(odd, two, one)
+    return unpack3(before, q % 3, 0) + unpack3(after, q % 3, 24)
+
+
+def call(kernel, shapes, *args, scratch=(), weight=1000, token=False):
+    specs = [pl.BlockSpec(memory_space=SMEM)] + [WHOLE] * (len(args) - 1)
+    if token:
+        specs[-1] = pl.BlockSpec(memory_space=pl.ANY)
     return pl.pallas_call(
         kernel,
-        in_specs=[pl.BlockSpec(memory_space=SMEM)] + [WHOLE] * (len(args) - 1),
+        in_specs=specs,
         out_specs=[WHOLE] * len(shapes),
         out_shape=[jax.ShapeDtypeStruct(shape, F32) for shape in shapes],
         scratch_shapes=scratch,
@@ -352,32 +365,31 @@
     lane = lanes()
 
     def rims(step):
-        own, rim, out = part(own_all, step, 8), part(rim_all, step, 8), part(tmsg, step - 8, 27)
+        own, rim, out = part(own_all, step, 8), part(rim_all, step, 8), part(tmsg, step - 8, 36)
         extra = None
         for t in range(8):
-            for b in range(3):
-                near, far = merged(own, rim, rim_all, t, b + 5, sc)
-                q = t * 3 + b
+            for b in range(4):
+                near, far = merged(own, rim, rim_all, t, b + 4, sc)
+                q = t * 4 + b
                 out[q] = jnp.where(lane < 104, near, far)
                 moved = turn(far, 16 * (q % 8) - 88)
                 extra = moved if q % 8 == 0 else jnp.where(lane < 16 * (q % 8), extra, moved)
                 if q % 8 == 7:
-                    out[24 + q // 8] = extra
+                    out[32 + q // 8] = extra
 
     loop(8, 13, rims)
 
 
-def pack_xline_kernel(sc, own_all, rim_all, zhc, zlc):
+def pack_xline_kernel(sc, own_all, rim_all, token, zhc, zlc):
     def every(step):
         own, rim = part(own_all, step, 8), part(rim_all, step, 8)
         ahead, behind = [], []
         for t in range(8):
-            for b in range(5):
+            for b in range(4):
                 near, far = merged(own, rim, rim_all, t, b, sc)
                 ahead.append(near)
                 behind.append(far)
-        pack_many(ahead, part(zhc, step, 14), 64)
-        pack_many(behind, part(zlc, step, 14), 88)
+        pack_sides(ahead, behind, part(zhc, step, 11), part(zlc, step, 11), sc)
 
     loop(0, 13, every)
 
@@ -391,8 +403,7 @@
         for t in range(26):
             for b in range(5):
                 q = t * 5 + b
-                sides = unpack3(zh[q // 3], q % 3, 0) + unpack3(zl[q // 3], q % 3, 24)
-                out[t, 8 * b : 8 * b + 8, :] = outer[t, 8 * b : 8 * b + 8, :] + sides
+                out[t, 8 * b : 8 * b + 8, :] = outer[t, 8 * b : 8 * b + 8, :] + unpack_sides(zh, zl, q, sc)
 
     def outer_rims(p):
         for b in range(5):
@@ -405,11 +416,11 @@
 
 
 def pack_time(sc, own, rim):
-    return call(pack_time_kernel, [(5 * 27, 8, B)], sc, own, rim)[0]
-
-
-def pack_xline(sc, own, rim):
-    return call(pack_xline_kernel, [(13 * 14, 8, B), (13 * 14, 8, B)], sc, own, rim, weight=10**8)
+    return call(pack_time_kernel, [(5 * 36, 8, B)], sc, own, rim)[0]
+
+
+def pack_xline(sc, own, rim, token):
+    return call(pack_xline_kernel, [(13 * 11, 8, B), (13 * 11, 8, B)], sc, own, rim, token, weight=10**8, token=True)
 
 
 def outer_middle(sc, outer, zho, zlo):
@@ -417,61 +428,64 @@
     return call(outer_middle_kernel, [(100, 8, B), (64, 40, B)], sc, outer, zho, zlo, scratch=scratch, weight=10**8)
 
 
-def middle_kernel(
-    sc, own_all, rim_all, zhc_all, zlc_all, tmsg, outer_all, tmo,
-    own1_all, tmc_all, zh2_all, zl2_all, own2_all, dmsg_all,
-):
-    lane = lanes()
-
-    def views(step):
-        own, rim = part(own_all, step, 8), part(rim_all, step, 8)
-        zhc, zlc = part(zhc_all, step, 14), part(zlc_all, step, 14)
-
-        def first_rows(t, b):
-            near, _ = merged(own, rim, rim_all, t, b, sc)
-            q = t * 5 + b
-            return near + unpack3(zhc[q // 3], q % 3, 0) + unpack3(zlc[q // 3], q % 3, 24)
-
-        return own, rim, first_rows
-
-    def rims(step):
-        _, _, first_rows = views(step)
-        tmc = part(tmc_all, step - 8, 20)
-        for t in range(0, 8, 2):
-            for b in range(5):
-                tmc[t // 2 * 5 + b] = jnp.where(lane < 64, first_rows(t, b), turn(first_rows(t + 1, b), 64))
+def middle_xline_kernel(sc, own_all, rim_all, tmsg, zh2_all, zl2_all, own2_all):
+    lane = lanes()
 
     def cores(step):
-        own, rim, first_rows = views(step)
-        own1, own2 = part(own1_all, step, 8), part(own2_all, step, 8)
-        zh2, zl2 = part(zh2_all, step, 8), part(zl2_all, step, 8)
-        for t in range(8):
-            for b in range(5):
-                own1[t, 8 * b : 8 * b + 8, :] = first_rows(t, b)
+        own, rim, own2 = part(own_all, step, 8), part(rim_all, step, 8), part(own2_all, step, 8)
         place = step - jnp.where(sc[3] == 0, 3, 0)
         valid = (place >= 0) & (place < 5)
-        msg = part(tmsg, jnp.clip(place, 0, 4), 27)
+        msg = part(tmsg, jnp.clip(place, 0, 4), 36)
+        ahead, behind = [], []
         for t in range(8):
-            ahead, behind = [], []
-            for b in range(3):
-                q = t * 3 + b
-                near, far = merged(own, rim, rim_all, t, b + 5, sc)
+            for b in range(4):
+                q = t * 4 + b
+                near, far = merged(own, rim, rim_all, t, b + 4, sc)
                 main = msg[q]
-                moved = turn(msg[24 + q // 8], 88 - 16 * (q % 8))
+                moved = turn(msg[32 + q // 8], 88 - 16 * (q % 8))
                 near = near + jnp.where(valid & (lane < 104), main, 0.0)
                 far2 = jnp.where(lane >= 104, main, jnp.where(lane >= 88, moved, 0.0))
                 far = far + jnp.where(valid, far2, 0.0)
                 ahead.append(near)
                 behind.append(far)
                 own2[t, 8 * b : 8 * b + 8, :] = near
-            zh2[t] = pack3(ahead, 64)
-            zl2[t] = pack3(behind, 88)
+        pack_sides(ahead, behind, part(zh2_all, step, 11), part(zl2_all, step, 11), sc)
+
+    loop(0, 8, cores)
+
+
+def middle_time_kernel(sc, own_all, rim_all, zhc_all, zlc_all, outer_all, tmo, token, own1_all, tmc_all, dmsg_all):
+    lane = lanes()
+
+    def views(step):
+        own, rim = part(own_all, step, 8), part(rim_all, step, 8)
+        zhc, zlc = part(zhc_all, step, 11), part(zlc_all, step, 11)
+
+        def first_rows(t, b):
+            near, _ = merged(own, rim, rim_all, t, b, sc)
+            return near + unpack_sides(zhc, zlc, t * 4 + b, sc)
+
+        return first_rows
+
+    def rims(step):
+        first_rows = views(step)
+        tmc = part(tmc_all, step - 8, 16)
+        for t in range(0, 8, 2):
+            for b in range(4):
+                tmc[t // 2 * 4 + b] = jnp.where(lane < 64, first_rows(t, b), turn(first_rows(t + 1, b), 64))
+
+    def cores(step):
+        first_rows = views(step)
+        own1 = part(own1_all, step, 8)
+        for t in range(8):
+            for b in range(4):
+                own1[t, 8 * b : 8 * b + 8, :] = first_rows(t, b)
 
     def outers(step):
         own, dmsg = part(outer_all, step, 8), part(dmsg_all, step, 20)
         for t in range(0, 8, 2):
             for b in range(5):
-                even, odd = time_rows(sc, own, tmo, step, t, b), time_rows(sc, own, tmo, step, t + 1, b)
+                even, odd = time_rows(sc, own, tmo, step, t, b, 5), time_rows(sc, own, tmo, step, t + 1, b, 5)
                 dmsg[t // 2 * 5 + b] = jnp.where(lane < 64, even, turn(odd, 64))
 
     loop(8, 13, rims)
@@ -479,15 +493,18 @@
     loop(0, 8, cores)
 
 
-def middle(sc, *args):
-    shapes = [(64, 40, B), (100, 8, B), (64, 8, B), (64, 8, B), (64, 24, B), (160, 8, B)]
-    return call(middle_kernel, shapes, sc, *args)
-
-
-def time_rows(sc, own, msg, step, t, b):
+def middle_xline(sc, own, rim, tmsg):
+    return call(middle_xline_kernel, [(88, 8, B), (88, 8, B), (64, 32, B)], sc, own, rim, tmsg, weight=10**8)
+
+
+def middle_time(sc, *args):
+    return call(middle_time_kernel, [(64, 32, B), (80, 8, B), (160, 8, B)], sc, *args, weight=10**8, token=True)
+
+
+def time_rows(sc, own, msg, step, t, b, count):
     place = step - jnp.where(sc[3] == 0, 3, 0)
     valid = (place >= 0) & (place < 5)
-    both = msg[(jnp.clip(place, 0, 4) * 4 + t // 2) * 5 + b]
+    both = msg[(jnp.clip(place, 0, 4) * 4 + t // 2) * count + b]
     both = both if t % 2 == 0 else turn(both, 64)
     return own[t, 8 * b : 8 * b + 8, :] + jnp.where(valid, both, 0.0)
 
@@ -497,15 +514,15 @@
 
     def body(step):
         own1, own2 = part(own1_all, step, 8), part(own2_all, step, 8)
-        zh2, zl2 = part(zh2_all, step, 8), part(zl2_all, step, 8)
+        zh2, zl2 = part(zh2_all, step, 11), part(zl2_all, step, 11)
         dmsg, out = part(dmsg_all, step, 20), part(out_all, step, 8)
         for t in range(8):
             for b in range(8):
-                if b < 5:
-                    value = time_rows(sc, own1, tmc, step, t, b)
+                if b < 4:
+                    value = time_rows(sc, own1, tmc, step, t, b, 4)
                 else:
-                    value = own2[t, 8 * (b - 5) : 8 * (b - 5) + 8, :]
-                    value = value + unpack3(zh2[t], b - 5, 0) + unpack3(zl2[t], b - 5, 24)
+                    value = own2[t, 8 * (b - 4) : 8 * (b - 4) + 8, :]
+                    value = value + unpack_sides(zh2, zl2, t * 4 + b - 4, sc)
                 place = b - shift
                 valid = (place >= 0) & (place < 5)
                 other = dmsg[t // 2 * 5 + jnp.clip(place, 0, 4)]
@@ -525,13 +542,14 @@
     n_tm, n_in, n_x = (lax.axis_size(a) for a in ("tm", "inline", "xline"))
     tm = lax.axis_index("tm").astype(jnp.int32)
     odd = (lax.axis_index("inline") & 1).astype(jnp.int32)
-    sc = jnp.concatenate([tile_offsets.reshape(3), jnp.stack([tm, odd]), kept.reshape(6)])
-
-    along = [(i, i + 1) for i in range(n_x - 1)]
-    back = [(b, a) for a, b in along]
+    xodd = (lax.axis_index("xline") & 1).astype(jnp.int32)
+    sc = jnp.concatenate([tile_offsets.reshape(3), jnp.stack([tm, odd]), kept.reshape(6), xodd[None]])
+
+    pairs = [(i, i ^ 1) for i in range(n_x)]
+    between = [p for i in range(1, n_x - 1, 2) for p in ((i, i + 1), (i + 1, i))]
     inner = range(1, n_in - 1)
-    along_o = [(i * n_x + a, i * n_x + b) for i in inner for a, b in along]
-    back_o = [(b, a) for a, b in along_o]
+    pairs_o = [(i * n_x + a, i * n_x + b) for i in inner for a, b in pairs]
+    between_o = [(i * n_x + a, i * n_x + b) for i in inner for a, b in between]
     times = [(i, i ^ 1) for i in range(n_tm)]
     times_o = [(a * n_in + i, b * n_in + i) for i in inner for a, b in times]
     mates = [(i, i ^ 1) for i in range(n_in)]
@@ -539,20 +557,21 @@
 
     rim, outer, zho, zlo, own = transform(sc, coef_fine, coef_coarse, tabs)
     rim = lax.ppermute(rim, "inline", mates)
-    zho = lax.ppermute(zho, ("inline", "xline"), along_o)
-    zlo = lax.ppermute(zlo, ("inline", "xline"), back_o)
-    tmsg = pack_time(sc, own, rim)
-    tmsg = lax.ppermute(tmsg, "tm", times)
-    zhc, zlc = pack_xline(sc, own, rim)
-    zhc = lax.ppermute(zhc, "xline", along)
-    zlc = lax.ppermute(zlc, "xline", back)
+    zho = lax.ppermute(zho, ("inline", "xline"), pairs_o)
+    zlo = lax.ppermute(zlo, ("inline", "xline"), between_o)
+    packed = pack_time(sc, own, rim)
+    tmsg = lax.ppermute(packed, "tm", times)
+    zhc, zlc = pack_xline(sc, own, rim, packed)
+    zhc = lax.ppermute(zhc, "xline", pairs)
+    zlc = lax.ppermute(zlc, "xline", between)
     tmo, outer = outer_middle(sc, outer, zho, zlo)
     tmo = lax.ppermute(tmo, ("tm", "inline"), times_o)
-    own1, tmc, zh2, zl2, own2, dmsg = middle(sc, own, rim, zhc, zlc, tmsg, outer, tmo)
+    packed, zl2, own2 = middle_xline(sc, own, rim, tmsg)
+    zh2 = lax.ppermute(packed, "xline", pairs)
+    zl2 = lax.ppermute(zl2, "xline", between)
+    own1, tmc, dmsg = middle_time(sc, own, rim, zhc, zlc, outer, tmo, packed)
     dmsg = lax.ppermute(dmsg, "inline", facing)
     tmc = lax.ppermute(tmc, "tm", times)
-    zh2 = lax.ppermute(zh2, "xline", along)
-    zl2 = lax.ppermute(zl2, "xline", back)
     return last(sc, own1, tmc, zh2, zl2, own2, dmsg)
 
 

time: 98.2 us -> 94.9 us (0.966)
  starting transfers between devices: 33.2 us -> 28.9 us
  local copies, waits for them, and re-layouts: 1.97 us -> 3.31 us
  other arithmetic: 1.29 us -> 0 us
    ppermute x1, waiting for transfers between devices: 1.56 us -> 10.4 us  [local(): tmc = lax.ppermute(tmc, 'tm', times)]
    ppermute x1, waiting for transfers between devices: 9.99 us -> 2.66 us  [local(): tmo = lax.ppermute(tmo, ('tm', 'inline'), times_o)]
    ppermute x7, starting transfers between devices: 24.8 us -> 18.9 us  [the longest x1 6.75 us: local(): zlo = lax.ppermute(zlo, ('inline', 'xline'), between_o)]
    ppermute x1, starting transfers between devices: 3.21 us -> 4.91 us  [local(): dmsg = lax.ppermute(dmsg, 'inline', facing)]
    concatenate x0 -> x1, local copies, waits for them, and re-layouts: none -> 1.34 us  [local(): jnp.concatenate([tile_offsets.reshape(3), jnp.stack([tm, odd]), kept.resh...]
    concatenate x1 -> x0, other arithmetic: 1.29 us -> none  [local(): jnp.concatenate([tile_offsets.reshape(3), jnp.stack([tm, odd]), kept.resh...]
    pallas_call x5 -> x6, Pallas kernels: 15.3 us -> 16 us  [call(): pl.pallas_call(kernel, in_specs=specs, out_specs=[WHOLE] * len(shapes), o...]
  transfers between devices with their start and end apart: 11 -> 11, of which waited for: 4 -> 4; matrix products, arithmetic and copies ran while one was open for 0% -> 0% of each run, Pallas kernels for 7% -> 9%
where the time goes in v3:
time: 94.9 us; the launch traced here: 94.6 us
  Pallas kernels  46.8 us (49%)
  starting transfers between devices  28.9 us (30%)
  waiting for transfers between devices  15.4 us (16%)
  local copies, waits for them, and re-layouts  3.31 us (3%)
    pallas_call x1, Pallas kernels, transform(): pl.pallas_call(transform_kernel, grid=(8,), in_specs=[pl.BlockSpec(memory...  30.8 us
    pallas_call x6, Pallas kernels, call(): pl.pallas_call(kernel, in_specs=specs, out_specs=[WHOLE] * len(shapes), o...  16 us
    ppermute x1, waiting for transfers between devices, local(): tmc = lax.ppermute(tmc, 'tm', times)  10.4 us
    ppermute x1, starting transfers between devices, local(): zlo = lax.ppermute(zlo, ('inline', 'xline'), between_o)  6.75 us
    ppermute x1, starting transfers between devices, local(): dmsg = lax.ppermute(dmsg, 'inline', facing)  4.91 us
    ppermute x1, starting transfers between devices, local(): zl2 = lax.ppermute(zl2, 'xline', between)  4.74 us
    ppermute x1, starting transfers between devices, local(): zho = lax.ppermute(zho, ('inline', 'xline'), pairs_o)  3.53 us
    ppermute x1, starting transfers between devices, local(): zlc = lax.ppermute(zlc, 'xline', between)  3.34 us
  transfers between devices with their start and end apart: 11, of which 4 were waited for; matrix products, arithmetic and copies ran while one was open for 0% of the time, Pallas kernels for 9%

profile of v3, /device:TPU:27, one launch (start us, length us, event | category | flops | bytes accessed | tf_op | source)
XLA Modules:
  0.0 94.6 jit_solution(13283752210634679381)
XLA Ops:
  0.0 1.3 %concatenate.3.sc = s32[12]{0:T(128)} concatenate(s32[3]{0:T(128)} %bitcast.5, s32[1]{0:T(128)} %bitcast.1, s32[1]{0:T(128)} %bitcast.2, s32[6]{0:T(128)} %bitcast.6, s32[1]{0:T(128)} %bitcast.4), dimensions={0} | concatenate | bytes 96 | tf_op jit(solution)/shard_map/concatenate | solution.py:546
  1.3 30.8 %shard_map.100 = (f32[112,40,128]{2,1,0:T(8,128)}, f32[104,40,128]{2,1,0:T(8,128)}, f32[176,8,128]{2,1,0:T(8,128)}, f32[176,8,128]{2,1,0:T(8,128)}, f32[104,64,128]{2,1,0:T(8,128)}) custom-call(s32[12]{0:T(128)} %concatenate.3.sc, bf16[2,128,128,128]{3,2,1,0:T(8,128)(2,1)} %fine.1, bf16[2,64,64,64]{3,2,1,0:T(8,128)(2,1)} %coarse.1, ...), custom_call_target="tpu_custom_call" | custom-call | flops 20000000000 | bytes 30000000 | tf_op jit(solution)/shard_map/pallas_call | solution.py:232
  32.1 0.8 collective-permute-start
  32.9 3.5 %collective-permute-start.3 = (f32[176,8,128]{2,1,0:T(8,128)}, f32[176,8,128]{2,1,0:T(8,128)S(1)}, u32[]{:S(2)}, u32[]{:S(2)}) collective-permute-start(f32[176,8,128]{2,1,0:T(8,128)} %get-tuple-element.25), channel_id=1, source_target_pairs={{32,33},{33,32},{34,35},{35,34},{36,37},{37,36},{38,39},{39,38},{4... | collective-permute-start | bytes 2162696 | tf_op jit(solution)/shard_map/ppermute | solution.py:560
  36.4 6.8 %collective-permute-start.4 = (f32[176,8,128]{2,1,0:T(8,128)}, f32[176,8,128]{2,1,0:T(8,128)S(1)}, u32[]{:S(2)}, u32[]{:S(2)}) collective-permute-start(f32[176,8,128]{2,1,0:T(8,128)} %get-tuple-element.26), channel_id=1, source_target_pairs={{33,34},{34,33},{35,36},{36,35},{37,38},{38,37},{39,40},{40,39},{4... | collective-permute-start | bytes 2162696 | tf_op jit(solution)/shard_map/ppermute | solution.py:561
  43.2 0.0 collective-permute-done.rim_all
  43.2 2.0 %copy-done = f32[104,64,128]{2,1,0:T(8,128)S(1)} copy-done((f32[104,64,128]{2,1,0:T(8,128)S(1)}, f32[104,64,128]{2,1,0:T(8,128)}, u32[]{:S(2)}) %copy-start) | copy-done | bytes 3407896
  45.2 1.1 %shard_map.101.token = f32[180,8,128]{2,1,0:T(8,128)S(1)} custom-call(s32[12]{0:T(128)S(1)} %copy-done.3, f32[104,64,128]{2,1,0:T(8,128)S(1)} %copy-done, f32[112,40,128]{2,1,0:T(8,128)S(1)} %collective-permute-done.rim_all), custom_call_target="tpu_custom_call" | custom-call | flops 1000 | bytes 1000 | tf_op jit(solution)/shard_map/pallas_call | solution.py:338
  46.2 0.0 copy-start.2
  46.3 0.3 collective-permute-start.6
  46.6 2.4 %shard_map.102 = (f32[143,8,128]{2,1,0:T(8,128)S(1)}, f32[143,8,128]{2,1,0:T(8,128)S(1)}) custom-call(s32[12]{0:T(128)S(1)} %copy-done.3, f32[104,64,128]{2,1,0:T(8,128)S(1)} %copy-done, f32[112,40,128]{2,1,0:T(8,128)S(1)} %collective-permute-done.rim_all, f32[180,8,128]{2,1,0:T(8,128)S(1)} %shard_map.101.token), custom_call_target="tpu_custom_call" | custom-call | flops 1000 | bytes 100000000 | tf_op jit(solution)/shard_map/pallas_call | solution.py:338
  49.0 0.1 collective-permute-start.1
  49.1 3.3 %collective-permute-start.2 = (f32[143,8,128]{2,1,0:T(8,128)S(1)}, f32[143,8,128]{2,1,0:T(8,128)S(1)}, u32[]{:S(2)}, u32[]{:S(2)}) collective-permute-start(f32[143,8,128]{2,1,0:T(8,128)S(1)} %get-tuple-element.23), channel_id=1, source_target_pairs={{1,2},{2,1},{3,4},{4,3},{5,6},{6,5},{7,8},{8,7},{9,10},{10,9},{11,... | collective-permute-start | bytes 1757192 | tf_op jit(solution)/shard_map/ppermute | solution.py:566
  52.5 0.0 collective-permute-done.3.zho_all
  52.5 0.0 collective-permute-done.4.zlo_all
  52.5 3.3 %shard_map.103 = (f32[100,8,128]{2,1,0:T(8,128)S(1)}, f32[64,40,128]{2,1,0:T(8,128)S(1)}) custom-call(s32[12]{0:T(128)S(1)} %copy-done.3, f32[104,40,128]{2,1,0:T(8,128)S(1)} %copy-done.2, f32[176,8,128]{2,1,0:T(8,128)S(1)} %collective-permute-done.3.zho_all, f32[176,8,128]{2,1,0:T(8,128)S(1)} %collective-permute-done.4.zlo_all), custom_call_target="tpu_custom_call" | custom-call | flops 1000 | bytes 100000000 | tf_op jit(solution)/shard_map/pallas_call | solution.py:338
  55.8 3.1 %collective-permute-start.5 = (f32[100,8,128]{2,1,0:T(8,128)S(1)}, f32[100,8,128]{2,1,0:T(8,128)S(1)}, u32[]{:S(2)}, u32[]{:S(2)}) collective-permute-start(f32[100,8,128]{2,1,0:T(8,128)S(1)} %get-tuple-element.28), channel_id=1, source_target_pairs={{32,160},{160,32},{64,192},{192,64},{33,161},{161,33},{65,193},{19... | collective-permute-start | bytes 1228808 | tf_op jit(solution)/shard_map/ppermute | solution.py:568
  58.9 0.7 collective-permute-done.6.tmsg
  59.7 2.2 %shard_map.104 = (f32[88,8,128]{2,1,0:T(8,128)S(1)}, f32[88,8,128]{2,1,0:T(8,128)S(1)}, f32[64,32,128]{2,1,0:T(8,128)S(1)}) custom-call(s32[12]{0:T(128)S(1)} %copy-done.3, f32[104,64,128]{2,1,0:T(8,128)S(1)} %copy-done.1, f32[112,40,128]{2,1,0:T(8,128)S(1)} %collective-permute-done.rim_all, f32[180,8,128]{2,1,0:T(8,128)S(1)} %collective-permute-done.6.tmsg), custom_call_target="tpu_custom_call" | custom-call | flops 1000 | bytes 100000000 | tf_op jit(solution)/shard_map/pallas_call | solution.py:338
  61.8 2.7 %collective-permute-done.5.tmo = f32[100,8,128]{2,1,0:T(8,128)S(1)} collective-permute-done((f32[100,8,128]{2,1,0:T(8,128)S(1)}, f32[100,8,128]{2,1,0:T(8,128)S(1)}, u32[]{:S(2)}, u32[]{:S(2)}) %collective-permute-start.5) | collective-permute-done | bytes 409632 | tf_op jit(solution)/shard_map/ppermute | solution.py:568
  64.5 0.0 collective-permute-done.1.zhc_all
  64.5 1.6 %collective-permute-done.2.zlc_all = f32[143,8,128]{2,1,0:T(8,128)S(1)} collective-permute-done((f32[143,8,128]{2,1,0:T(8,128)S(1)}, f32[143,8,128]{2,1,0:T(8,128)S(1)}, u32[]{:S(2)}, u32[]{:S(2)}) %collective-permute-start.2) | collective-permute-done | bytes 585760 | tf_op jit(solution)/shard_map/ppermute | solution.py:566
  66.1 3.8 %shard_map.105 = (f32[64,32,128]{2,1,0:T(8,128)S(1)}, f32[80,8,128]{2,1,0:T(8,128)S(1)}, f32[160,8,128]{2,1,0:T(8,128)S(1)}) custom-call(s32[12]{0:T(128)S(1)} %copy-done.3, f32[104,64,128]{2,1,0:T(8,128)S(1)} %copy-done.1, f32[112,40,128]{2,1,0:T(8,128)S(1)} %collective-permute-done.rim_all, f32[143,8,128]{2,1,0:T(8,128)S(1)} %collective-permute-done.1.zhc_all, ...), custom_call_target="tpu_custom_call" | custom-call | flops 1000 | bytes 100000000 | tf_op jit(solution)/shard_map/pallas_call | solution.py:338
  69.9 4.9 %collective-permute-start.10 = (f32[160,8,128]{2,1,0:T(8,128)S(1)}, f32[160,8,128]{2,1,0:T(8,128)S(1)}, u32[]{:S(2)}, u32[]{:S(2)}) collective-permute-start(f32[160,8,128]{2,1,0:T(8,128)S(1)} %get-tuple-element.34), channel_id=1, source_target_pairs={{32,64},{64,32},{33,65},{65,33},{34,66},{66,34},{35,67},{67,35},{3... | collective-permute-start | bytes 1966088 | tf_op jit(solution)/shard_map/ppermute | solution.py:573
  74.8 4.7 %collective-permute-start.9 = (f32[88,8,128]{2,1,0:T(8,128)S(1)}, f32[88,8,128]{2,1,0:T(8,128)S(1)}, u32[]{:S(2)}, u32[]{:S(2)}) collective-permute-start(f32[88,8,128]{2,1,0:T(8,128)S(1)} %get-tuple-element.32), channel_id=1, source_target_pairs={{1,2},{2,1},{3,4},{4,3},{5,6},{6,5},{7,8},{8,7},{9,10},{10,9},{11,... | collective-permute-start | bytes 1081352 | tf_op jit(solution)/shard_map/ppermute | solution.py:571
  79.5 0.1 collective-permute-start.8
  79.6 1.2 %collective-permute-start.7 = (f32[80,8,128]{2,1,0:T(8,128)S(1)}, f32[80,8,128]{2,1,0:T(8,128)S(1)}, u32[]{:S(2)}, u32[]{:S(2)}) collective-permute-start(f32[80,8,128]{2,1,0:T(8,128)S(1)} %get-tuple-element.31), channel_id=1, source_target_pairs={{0,128},{128,0},{1,129},{129,1},{2,130},{130,2},{3,131},{131,3},{4... | collective-permute-start | bytes 983048 | tf_op jit(solution)/shard_map/ppermute | solution.py:574
  80.9 10.4 %collective-permute-done.7.tmc = f32[80,8,128]{2,1,0:T(8,128)S(1)} collective-permute-done((f32[80,8,128]{2,1,0:T(8,128)S(1)}, f32[80,8,128]{2,1,0:T(8,128)S(1)}, u32[]{:S(2)}, u32[]{:S(2)}) %collective-permute-start.7) | collective-permute-done | bytes 327712 | tf_op jit(solution)/shard_map/ppermute | solution.py:574
  91.3 0.0 collective-permute-done.9.zl2_all
  91.3 0.0 collective-permute-done.8.zh2_all
  91.3 0.0 collective-permute-done.10.dmsg_all
  91.3 3.3 %shard_map.106 = f32[64,64,64]{2,1,0:T(8,128)} custom-call(s32[12]{0:T(128)S(1)} %copy-done.3, f32[64,32,128]{2,1,0:T(8,128)S(1)} %get-tuple-element.30.own1_all, f32[80,8,128]{2,1,0:T(8,128)S(1)} %collective-permute-done.7.tmc, f32[88,8,128]{2,1,0:T(8,128)S(1)} %collective-permute-done.8.zh2_all, f32[88,8,128]{2,1,0:T(8,128)S(1)} %collective-permute-done.9.zl2_all, ...), custom_call_target="tpu_custom_call" | custom-call | flops 1000 | bytes 1000 | tf_op jit(solution)/shard_map/pallas_call | solution.py:338
  (6 shorter events, 0.0 us)
Async XLA Ops:
  1.3 41.8 %copy-start.3 = (s32[12]{0:T(128)S(1)}, s32[12]{0:T(128)}, u32[]{:S(2)}) copy-start(s32[12]{0:T(128)} %concatenate.3.sc) | copy-start | bytes 148
  32.1 11.1 %collective-permute-start = (f32[112,40,128]{2,1,0:T(8,128)}, f32[112,40,128]{2,1,0:T(8,128)S(1)}, u32[]{:S(2)}, u32[]{:S(2)}) collective-permute-start(f32[112,40,128]{2,1,0:T(8,128)} %get-tuple-element.21), channel_id=1, source_target_pairs={{0,32},{32,0},{64,96},{96,64},{1,33},{33,1},{65,97},{97,65},{2,34}... | collective-permute-start | bytes 6881288 | tf_op jit(solution)/shard_map/ppermute | solution.py:559
  32.9 19.6 %collective-permute-start.3 = (f32[176,8,128]{2,1,0:T(8,128)}, f32[176,8,128]{2,1,0:T(8,128)S(1)}, u32[]{:S(2)}, u32[]{:S(2)}) collective-permute-start(f32[176,8,128]{2,1,0:T(8,128)} %get-tuple-element.25), channel_id=1, source_target_pairs={{32,33},{33,32},{34,35},{35,34},{36,37},{37,36},{38,39},{39,38},{4... | collective-permute-start | bytes 2162696 | tf_op jit(solution)/shard_map/ppermute | solution.py:560
  36.4 16.1 %collective-permute-start.4 = (f32[176,8,128]{2,1,0:T(8,128)}, f32[176,8,128]{2,1,0:T(8,128)S(1)}, u32[]{:S(2)}, u32[]{:S(2)}) collective-permute-start(f32[176,8,128]{2,1,0:T(8,128)} %get-tuple-element.26), channel_id=1, source_target_pairs={{33,34},{34,33},{35,36},{36,35},{37,38},{38,37},{39,40},{40,39},{4... | collective-permute-start | bytes 2162696 | tf_op jit(solution)/shard_map/ppermute | solution.py:561
  43.2 2.0 %copy-start = (f32[104,64,128]{2,1,0:T(8,128)S(1)}, f32[104,64,128]{2,1,0:T(8,128)}, u32[]{:S(2)}) copy-start(f32[104,64,128]{2,1,0:T(8,128)} %get-tuple-element.20.own_all) | copy-start | bytes 10223620
  46.2 6.3 %copy-start.2 = (f32[104,40,128]{2,1,0:T(8,128)S(1)}, f32[104,40,128]{2,1,0:T(8,128)}, u32[]{:S(2)}) copy-start(f32[104,40,128]{2,1,0:T(8,128)} %get-tuple-element.24.outer_all) | copy-start | bytes 6389764
  46.3 13.4 %collective-permute-start.6 = (f32[180,8,128]{2,1,0:T(8,128)S(1)}, f32[180,8,128]{2,1,0:T(8,128)S(1)}, u32[]{:S(2)}, u32[]{:S(2)}) collective-permute-start(f32[180,8,128]{2,1,0:T(8,128)S(1)} %shard_map.101.token), channel_id=1, source_target_pairs={{0,128},{128,0},{1,129},{129,1},{2,130},{130,2},{3,131},{131,3},{4... | collective-permute-start | bytes 2211848 | tf_op jit(solution)/shard_map/ppermute | solution.py:563
  49.0 10.6 %copy-start.1 = (f32[104,64,128]{2,1,0:T(8,128)S(1)}, f32[104,64,128]{2,1,0:T(8,128)}, u32[]{:S(2)}) copy-start(f32[104,64,128]{2,1,0:T(8,128)} %get-tuple-element.20.own_all) | copy-start | bytes 10223620
  49.0 15.4 %collective-permute-start.1 = (f32[143,8,128]{2,1,0:T(8,128)S(1)}, f32[143,8,128]{2,1,0:T(8,128)S(1)}, u32[]{:S(2)}, u32[]{:S(2)}) collective-permute-start(f32[143,8,128]{2,1,0:T(8,128)S(1)} %get-tuple-element.22), channel_id=1, source_target_pairs={{0,1},{1,0},{2,3},{3,2},{4,5},{5,4},{6,7},{7,6},{8,9},{9,8},{10,11... | collective-permute-start | bytes 1757192 | tf_op jit(solution)/shard_map/ppermute | solution.py:565
  49.1 16.9 %collective-permute-start.2 = (f32[143,8,128]{2,1,0:T(8,128)S(1)}, f32[143,8,128]{2,1,0:T(8,128)S(1)}, u32[]{:S(2)}, u32[]{:S(2)}) collective-permute-start(f32[143,8,128]{2,1,0:T(8,128)S(1)} %get-tuple-element.23), channel_id=1, source_target_pairs={{1,2},{2,1},{3,4},{4,3},{5,6},{6,5},{7,8},{8,7},{9,10},{10,9},{11,... | collective-permute-start | bytes 1757192 | tf_op jit(solution)/shard_map/ppermute | solution.py:566
  55.8 8.7 %collective-permute-start.5 = (f32[100,8,128]{2,1,0:T(8,128)S(1)}, f32[100,8,128]{2,1,0:T(8,128)S(1)}, u32[]{:S(2)}, u32[]{:S(2)}) collective-permute-start(f32[100,8,128]{2,1,0:T(8,128)S(1)} %get-tuple-element.28), channel_id=1, source_target_pairs={{32,160},{160,32},{64,192},{192,64},{33,161},{161,33},{65,193},{19... | collective-permute-start | bytes 1228808 | tf_op jit(solution)/shard_map/ppermute | solution.py:568
  69.9 21.4 %collective-permute-start.10 = (f32[160,8,128]{2,1,0:T(8,128)S(1)}, f32[160,8,128]{2,1,0:T(8,128)S(1)}, u32[]{:S(2)}, u32[]{:S(2)}) collective-permute-start(f32[160,8,128]{2,1,0:T(8,128)S(1)} %get-tuple-element.34), channel_id=1, source_target_pairs={{32,64},{64,32},{33,65},{65,33},{34,66},{66,34},{35,67},{67,35},{3... | collective-permute-start | bytes 1966088 | tf_op jit(solution)/shard_map/ppermute | solution.py:573
  74.8 16.5 %collective-permute-start.9 = (f32[88,8,128]{2,1,0:T(8,128)S(1)}, f32[88,8,128]{2,1,0:T(8,128)S(1)}, u32[]{:S(2)}, u32[]{:S(2)}) collective-permute-start(f32[88,8,128]{2,1,0:T(8,128)S(1)} %get-tuple-element.32), channel_id=1, source_target_pairs={{1,2},{2,1},{3,4},{4,3},{5,6},{6,5},{7,8},{8,7},{9,10},{10,9},{11,... | collective-permute-start | bytes 1081352 | tf_op jit(solution)/shard_map/ppermute | solution.py:571
  79.5 11.8 %collective-permute-start.8 = (f32[88,8,128]{2,1,0:T(8,128)S(1)}, f32[88,8,128]{2,1,0:T(8,128)S(1)}, u32[]{:S(2)}, u32[]{:S(2)}) collective-permute-start(f32[88,8,128]{2,1,0:T(8,128)S(1)} %get-tuple-element.29.token), channel_id=1, source_target_pairs={{0,1},{1,0},{2,3},{3,2},{4,5},{5,4},{6,7},{7,6},{8,9},{9,8},{10,11... | collective-permute-start | bytes 1081352 | tf_op jit(solution)/shard_map/ppermute | solution.py:570
  79.6 11.6 %collective-permute-start.7 = (f32[80,8,128]{2,1,0:T(8,128)S(1)}, f32[80,8,128]{2,1,0:T(8,128)S(1)}, u32[]{:S(2)}, u32[]{:S(2)}) collective-permute-start(f32[80,8,128]{2,1,0:T(8,128)S(1)} %get-tuple-element.31), channel_id=1, source_target_pairs={{0,128},{128,0},{1,129},{129,1},{2,130},{130,2},{3,131},{131,3},{4... | collective-permute-start | bytes 983048 | tf_op jit(solution)/shard_map/ppermute | solution.py:574

commit v4 on v3

--- a/solution.py
+++ b/solution.py
@@ -134,12 +134,15 @@
         lax.fori_loop(0, 32, high, 0, unroll=4)
         for c in range(2):
             put(c * B + 96, a * fine[c, 96].astype(F32))
-        xhi[pl.ds(step * 32, 32)] = jnp.swapaxes(shi[...], 0, 1)
-        xlo[pl.ds(jnp.where(step == 0, 0, 32), 32)] = jnp.swapaxes(slo[...], 0, 1)
+        for c in range(0, 256, 16):
+            xhi[pl.ds(step * 32, 32), c : c + 16] = jnp.swapaxes(shi[c : c + 16], 0, 1)
+            xlo[pl.ds(jnp.where(step == 0, 0, 32), 32), c : c + 16] = jnp.swapaxes(slo[c : c + 16], 0, 1)
 
     @pl.when((step == 1) | (step == 2))
     def _():
-        xhi[pl.ds(step * 32, 32)] = jnp.swapaxes(fine[...].reshape(256, 32, B), 0, 1)
+        for c in range(2):
+            for k in range(0, B, 64):
+                xhi[pl.ds(step * 32, 32), c * B + k : c * B + k + 64] = jnp.swapaxes(fine[c, k : k + 64], 0, 1)
 
     def along_xline(j):
         for which in range(2):

time: 94.9 us -> 94 us (level)
  transfers between devices with their start and end apart: 11 -> 11, of which waited for: 4 -> 4; matrix products, arithmetic and copies ran while one was open for 0% -> 0% of each run, Pallas kernels for 9% -> 10%
where the time goes in v4:
time: 94 us; the launch traced here: 93.7 us
  Pallas kernels  45.9 us (49%)
  starting transfers between devices  28.9 us (31%)
  waiting for transfers between devices  15.4 us (16%)
  local copies, waits for them, and re-layouts  3.31 us (4%)
    pallas_call x1, Pallas kernels, transform(): pl.pallas_call(transform_kernel, grid=(8,), in_specs=[pl.BlockSpec(memory...  29.8 us
    pallas_call x6, Pallas kernels, call(): pl.pallas_call(kernel, in_specs=specs, out_specs=[WHOLE] * len(shapes), o...  16 us
    ppermute x1, waiting for transfers between devices, local(): tmc = lax.ppermute(tmc, 'tm', times)  10.4 us
    ppermute x1, starting transfers between devices, local(): zlo = lax.ppermute(zlo, ('inline', 'xline'), between_o)  6.75 us
    ppermute x1, starting transfers between devices, local(): dmsg = lax.ppermute(dmsg, 'inline', facing)  4.91 us
    ppermute x1, starting transfers between devices, local(): zl2 = lax.ppermute(zl2, 'xline', between)  4.73 us
    ppermute x1, starting transfers between devices, local(): zho = lax.ppermute(zho, ('inline', 'xline'), pairs_o)  3.54 us
    ppermute x1, starting transfers between devices, local(): zlc = lax.ppermute(zlc, 'xline', between)  3.33 us
  transfers between devices with their start and end apart: 11, of which 4 were waited for; matrix products, arithmetic and copies ran while one was open for 0% of the time, Pallas kernels for 10%

profile of v4, /device:TPU:27, one launch (start us, length us, event | category | flops | bytes accessed | tf_op | source)
XLA Modules:
  0.0 93.7 jit_solution(55036058220824748)
XLA Ops:
  0.0 1.3 %concatenate.3.sc = s32[12]{0:T(128)} concatenate(s32[3]{0:T(128)} %bitcast.5, s32[1]{0:T(128)} %bitcast.1, s32[1]{0:T(128)} %bitcast.2, s32[6]{0:T(128)} %bitcast.6, s32[1]{0:T(128)} %bitcast.4), dimensions={0} | concatenate | bytes 96 | tf_op jit(solution)/shard_map/concatenate | solution.py:549
  1.3 29.8 %shard_map.100 = (f32[112,40,128]{2,1,0:T(8,128)}, f32[104,40,128]{2,1,0:T(8,128)}, f32[176,8,128]{2,1,0:T(8,128)}, f32[176,8,128]{2,1,0:T(8,128)}, f32[104,64,128]{2,1,0:T(8,128)}) custom-call(s32[12]{0:T(128)} %concatenate.3.sc, bf16[2,128,128,128]{3,2,1,0:T(8,128)(2,1)} %fine.1, bf16[2,64,64,64]{3,2,1,0:T(8,128)(2,1)} %coarse.1, ...), custom_call_target="tpu_custom_call" | custom-call | flops 20000000000 | bytes 30000000 | tf_op jit(solution)/shard_map/pallas_call | solution.py:235
  31.2 0.8 collective-permute-start
  32.0 3.5 %collective-permute-start.3 = (f32[176,8,128]{2,1,0:T(8,128)}, f32[176,8,128]{2,1,0:T(8,128)S(1)}, u32[]{:S(2)}, u32[]{:S(2)}) collective-permute-start(f32[176,8,128]{2,1,0:T(8,128)} %get-tuple-element.25), channel_id=1, source_target_pairs={{32,33},{33,32},{34,35},{35,34},{36,37},{37,36},{38,39},{39,38},{4... | collective-permute-start | bytes 2162696 | tf_op jit(solution)/shard_map/ppermute | solution.py:563
  35.5 6.8 %collective-permute-start.4 = (f32[176,8,128]{2,1,0:T(8,128)}, f32[176,8,128]{2,1,0:T(8,128)S(1)}, u32[]{:S(2)}, u32[]{:S(2)}) collective-permute-start(f32[176,8,128]{2,1,0:T(8,128)} %get-tuple-element.26), channel_id=1, source_target_pairs={{33,34},{34,33},{35,36},{36,35},{37,38},{38,37},{39,40},{40,39},{4... | collective-permute-start | bytes 2162696 | tf_op jit(solution)/shard_map/ppermute | solution.py:564
  42.3 0.0 collective-permute-done.rim_all
  42.3 2.0 %copy-done = f32[104,64,128]{2,1,0:T(8,128)S(1)} copy-done((f32[104,64,128]{2,1,0:T(8,128)S(1)}, f32[104,64,128]{2,1,0:T(8,128)}, u32[]{:S(2)}) %copy-start) | copy-done | bytes 3407896
  44.3 1.1 %shard_map.101.token = f32[180,8,128]{2,1,0:T(8,128)S(1)} custom-call(s32[12]{0:T(128)S(1)} %copy-done.3, f32[104,64,128]{2,1,0:T(8,128)S(1)} %copy-done, f32[112,40,128]{2,1,0:T(8,128)S(1)} %collective-permute-done.rim_all), custom_call_target="tpu_custom_call" | custom-call | flops 1000 | bytes 1000 | tf_op jit(solution)/shard_map/pallas_call | solution.py:341
  45.3 0.3 collective-permute-start.6
  45.7 2.4 %shard_map.102 = (f32[143,8,128]{2,1,0:T(8,128)S(1)}, f32[143,8,128]{2,1,0:T(8,128)S(1)}) custom-call(s32[12]{0:T(128)S(1)} %copy-done.3, f32[104,64,128]{2,1,0:T(8,128)S(1)} %copy-done, f32[112,40,128]{2,1,0:T(8,128)S(1)} %collective-permute-done.rim_all, f32[180,8,128]{2,1,0:T(8,128)S(1)} %shard_map.101.token), custom_call_target="tpu_custom_call" | custom-call | flops 1000 | bytes 100000000 | tf_op jit(solution)/shard_map/pallas_call | solution.py:341
  48.1 0.1 collective-permute-start.1
  48.2 3.3 %collective-permute-start.2 = (f32[143,8,128]{2,1,0:T(8,128)S(1)}, f32[143,8,128]{2,1,0:T(8,128)S(1)}, u32[]{:S(2)}, u32[]{:S(2)}) collective-permute-start(f32[143,8,128]{2,1,0:T(8,128)S(1)} %get-tuple-element.23), channel_id=1, source_target_pairs={{1,2},{2,1},{3,4},{4,3},{5,6},{6,5},{7,8},{8,7},{9,10},{10,9},{11,... | collective-permute-start | bytes 1757192 | tf_op jit(solution)/shard_map/ppermute | solution.py:569
  51.6 0.0 collective-permute-done.3.zho_all
  51.6 0.0 collective-permute-done.4.zlo_all
  51.6 3.3 %shard_map.103 = (f32[100,8,128]{2,1,0:T(8,128)S(1)}, f32[64,40,128]{2,1,0:T(8,128)S(1)}) custom-call(s32[12]{0:T(128)S(1)} %copy-done.3, f32[104,40,128]{2,1,0:T(8,128)S(1)} %copy-done.2, f32[176,8,128]{2,1,0:T(8,128)S(1)} %collective-permute-done.3.zho_all, f32[176,8,128]{2,1,0:T(8,128)S(1)} %collective-permute-done.4.zlo_all), custom_call_target="tpu_custom_call" | custom-call | flops 1000 | bytes 100000000 | tf_op jit(solution)/shard_map/pallas_call | solution.py:341
  54.9 3.1 %collective-permute-start.5 = (f32[100,8,128]{2,1,0:T(8,128)S(1)}, f32[100,8,128]{2,1,0:T(8,128)S(1)}, u32[]{:S(2)}, u32[]{:S(2)}) collective-permute-start(f32[100,8,128]{2,1,0:T(8,128)S(1)} %get-tuple-element.28), channel_id=1, source_target_pairs={{32,160},{160,32},{64,192},{192,64},{33,161},{161,33},{65,193},{19... | collective-permute-start | bytes 1228808 | tf_op jit(solution)/shard_map/ppermute | solution.py:571
  58.0 0.7 collective-permute-done.6.tmsg
  58.7 0.0 copy-done.1
  58.7 2.2 %shard_map.104 = (f32[88,8,128]{2,1,0:T(8,128)S(1)}, f32[88,8,128]{2,1,0:T(8,128)S(1)}, f32[64,32,128]{2,1,0:T(8,128)S(1)}) custom-call(s32[12]{0:T(128)S(1)} %copy-done.3, f32[104,64,128]{2,1,0:T(8,128)S(1)} %copy-done.1, f32[112,40,128]{2,1,0:T(8,128)S(1)} %collective-permute-done.rim_all, f32[180,8,128]{2,1,0:T(8,128)S(1)} %collective-permute-done.6.tmsg), custom_call_target="tpu_custom_call" | custom-call | flops 1000 | bytes 100000000 | tf_op jit(solution)/shard_map/pallas_call | solution.py:341
  60.9 2.7 %collective-permute-done.5.tmo = f32[100,8,128]{2,1,0:T(8,128)S(1)} collective-permute-done((f32[100,8,128]{2,1,0:T(8,128)S(1)}, f32[100,8,128]{2,1,0:T(8,128)S(1)}, u32[]{:S(2)}, u32[]{:S(2)}) %collective-permute-start.5) | collective-permute-done | bytes 409632 | tf_op jit(solution)/shard_map/ppermute | solution.py:571
  63.6 0.0 collective-permute-done.1.zhc_all
  63.6 1.6 %collective-permute-done.2.zlc_all = f32[143,8,128]{2,1,0:T(8,128)S(1)} collective-permute-done((f32[143,8,128]{2,1,0:T(8,128)S(1)}, f32[143,8,128]{2,1,0:T(8,128)S(1)}, u32[]{:S(2)}, u32[]{:S(2)}) %collective-permute-start.2) | collective-permute-done | bytes 585760 | tf_op jit(solution)/shard_map/ppermute | solution.py:569
  65.2 3.8 %shard_map.105 = (f32[64,32,128]{2,1,0:T(8,128)S(1)}, f32[80,8,128]{2,1,0:T(8,128)S(1)}, f32[160,8,128]{2,1,0:T(8,128)S(1)}) custom-call(s32[12]{0:T(128)S(1)} %copy-done.3, f32[104,64,128]{2,1,0:T(8,128)S(1)} %copy-done.1, f32[112,40,128]{2,1,0:T(8,128)S(1)} %collective-permute-done.rim_all, f32[143,8,128]{2,1,0:T(8,128)S(1)} %collective-permute-done.1.zhc_all, ...), custom_call_target="tpu_custom_call" | custom-call | flops 1000 | bytes 100000000 | tf_op jit(solution)/shard_map/pallas_call | solution.py:341
  68.9 4.9 %collective-permute-start.10 = (f32[160,8,128]{2,1,0:T(8,128)S(1)}, f32[160,8,128]{2,1,0:T(8,128)S(1)}, u32[]{:S(2)}, u32[]{:S(2)}) collective-permute-start(f32[160,8,128]{2,1,0:T(8,128)S(1)} %get-tuple-element.34), channel_id=1, source_target_pairs={{32,64},{64,32},{33,65},{65,33},{34,66},{66,34},{35,67},{67,35},{3... | collective-permute-start | bytes 1966088 | tf_op jit(solution)/shard_map/ppermute | solution.py:576
  73.9 4.7 %collective-permute-start.9 = (f32[88,8,128]{2,1,0:T(8,128)S(1)}, f32[88,8,128]{2,1,0:T(8,128)S(1)}, u32[]{:S(2)}, u32[]{:S(2)}) collective-permute-start(f32[88,8,128]{2,1,0:T(8,128)S(1)} %get-tuple-element.32), channel_id=1, source_target_pairs={{1,2},{2,1},{3,4},{4,3},{5,6},{6,5},{7,8},{8,7},{9,10},{10,9},{11,... | collective-permute-start | bytes 1081352 | tf_op jit(solution)/shard_map/ppermute | solution.py:574
  78.6 0.1 collective-permute-start.8
  78.7 1.2 %collective-permute-start.7 = (f32[80,8,128]{2,1,0:T(8,128)S(1)}, f32[80,8,128]{2,1,0:T(8,128)S(1)}, u32[]{:S(2)}, u32[]{:S(2)}) collective-permute-start(f32[80,8,128]{2,1,0:T(8,128)S(1)} %get-tuple-element.31), channel_id=1, source_target_pairs={{0,128},{128,0},{1,129},{129,1},{2,130},{130,2},{3,131},{131,3},{4... | collective-permute-start | bytes 983048 | tf_op jit(solution)/shard_map/ppermute | solution.py:577
  79.9 10.4 %collective-permute-done.7.tmc = f32[80,8,128]{2,1,0:T(8,128)S(1)} collective-permute-done((f32[80,8,128]{2,1,0:T(8,128)S(1)}, f32[80,8,128]{2,1,0:T(8,128)S(1)}, u32[]{:S(2)}, u32[]{:S(2)}) %collective-permute-start.7) | collective-permute-done | bytes 327712 | tf_op jit(solution)/shard_map/ppermute | solution.py:577
  90.3 0.0 collective-permute-done.9.zl2_all
  90.3 0.0 collective-permute-done.8.zh2_all
  90.4 0.0 collective-permute-done.10.dmsg_all
  90.4 3.3 %shard_map.106 = f32[64,64,64]{2,1,0:T(8,128)} custom-call(s32[12]{0:T(128)S(1)} %copy-done.3, f32[64,32,128]{2,1,0:T(8,128)S(1)} %get-tuple-element.30.own1_all, f32[80,8,128]{2,1,0:T(8,128)S(1)} %collective-permute-done.7.tmc, f32[88,8,128]{2,1,0:T(8,128)S(1)} %collective-permute-done.8.zh2_all, f32[88,8,128]{2,1,0:T(8,128)S(1)} %collective-permute-done.9.zl2_all, ...), custom_call_target="tpu_custom_call" | custom-call | flops 1000 | bytes 1000 | tf_op jit(solution)/shard_map/pallas_call | solution.py:341
  (6 shorter events, 0.0 us)
Async XLA Ops:
  1.3 40.9 %copy-start.3 = (s32[12]{0:T(128)S(1)}, s32[12]{0:T(128)}, u32[]{:S(2)}) copy-start(s32[12]{0:T(128)} %concatenate.3.sc) | copy-start | bytes 148
  31.2 11.1 %collective-permute-start = (f32[112,40,128]{2,1,0:T(8,128)}, f32[112,40,128]{2,1,0:T(8,128)S(1)}, u32[]{:S(2)}, u32[]{:S(2)}) collective-permute-start(f32[112,40,128]{2,1,0:T(8,128)} %get-tuple-element.21), channel_id=1, source_target_pairs={{0,32},{32,0},{64,96},{96,64},{1,33},{33,1},{65,97},{97,65},{2,34}... | collective-permute-start | bytes 6881288 | tf_op jit(solution)/shard_map/ppermute | solution.py:562
  32.0 19.6 %collective-permute-start.3 = (f32[176,8,128]{2,1,0:T(8,128)}, f32[176,8,128]{2,1,0:T(8,128)S(1)}, u32[]{:S(2)}, u32[]{:S(2)}) collective-permute-start(f32[176,8,128]{2,1,0:T(8,128)} %get-tuple-element.25), channel_id=1, source_target_pairs={{32,33},{33,32},{34,35},{35,34},{36,37},{37,36},{38,39},{39,38},{4... | collective-permute-start | bytes 2162696 | tf_op jit(solution)/shard_map/ppermute | solution.py:563
  35.5 16.1 %collective-permute-start.4 = (f32[176,8,128]{2,1,0:T(8,128)}, f32[176,8,128]{2,1,0:T(8,128)S(1)}, u32[]{:S(2)}, u32[]{:S(2)}) collective-permute-start(f32[176,8,128]{2,1,0:T(8,128)} %get-tuple-element.26), channel_id=1, source_target_pairs={{33,34},{34,33},{35,36},{36,35},{37,38},{38,37},{39,40},{40,39},{4... | collective-permute-start | bytes 2162696 | tf_op jit(solution)/shard_map/ppermute | solution.py:564
  42.3 2.0 %copy-start = (f32[104,64,128]{2,1,0:T(8,128)S(1)}, f32[104,64,128]{2,1,0:T(8,128)}, u32[]{:S(2)}) copy-start(f32[104,64,128]{2,1,0:T(8,128)} %get-tuple-element.20.own_all) | copy-start | bytes 10223620
  45.3 6.3 %copy-start.2 = (f32[104,40,128]{2,1,0:T(8,128)S(1)}, f32[104,40,128]{2,1,0:T(8,128)}, u32[]{:S(2)}) copy-start(f32[104,40,128]{2,1,0:T(8,128)} %get-tuple-element.24.outer_all) | copy-start | bytes 6389764
  45.3 13.4 %collective-permute-start.6 = (f32[180,8,128]{2,1,0:T(8,128)S(1)}, f32[180,8,128]{2,1,0:T(8,128)S(1)}, u32[]{:S(2)}, u32[]{:S(2)}) collective-permute-start(f32[180,8,128]{2,1,0:T(8,128)S(1)} %shard_map.101.token), channel_id=1, source_target_pairs={{0,128},{128,0},{1,129},{129,1},{2,130},{130,2},{3,131},{131,3},{4... | collective-permute-start | bytes 2211848 | tf_op jit(solution)/shard_map/ppermute | solution.py:566
  48.1 10.6 %copy-start.1 = (f32[104,64,128]{2,1,0:T(8,128)S(1)}, f32[104,64,128]{2,1,0:T(8,128)}, u32[]{:S(2)}) copy-start(f32[104,64,128]{2,1,0:T(8,128)} %get-tuple-element.20.own_all) | copy-start | bytes 10223620
  48.1 15.4 %collective-permute-start.1 = (f32[143,8,128]{2,1,0:T(8,128)S(1)}, f32[143,8,128]{2,1,0:T(8,128)S(1)}, u32[]{:S(2)}, u32[]{:S(2)}) collective-permute-start(f32[143,8,128]{2,1,0:T(8,128)S(1)} %get-tuple-element.22), channel_id=1, source_target_pairs={{0,1},{1,0},{2,3},{3,2},{4,5},{5,4},{6,7},{7,6},{8,9},{9,8},{10,11... | collective-permute-start | bytes 1757192 | tf_op jit(solution)/shard_map/ppermute | solution.py:568
  48.2 16.9 %collective-permute-start.2 = (f32[143,8,128]{2,1,0:T(8,128)S(1)}, f32[143,8,128]{2,1,0:T(8,128)S(1)}, u32[]{:S(2)}, u32[]{:S(2)}) collective-permute-start(f32[143,8,128]{2,1,0:T(8,128)S(1)} %get-tuple-element.23), channel_id=1, source_target_pairs={{1,2},{2,1},{3,4},{4,3},{5,6},{6,5},{7,8},{8,7},{9,10},{10,9},{11,... | collective-permute-start | bytes 1757192 | tf_op jit(solution)/shard_map/ppermute | solution.py:569
  54.9 8.7 %collective-permute-start.5 = (f32[100,8,128]{2,1,0:T(8,128)S(1)}, f32[100,8,128]{2,1,0:T(8,128)S(1)}, u32[]{:S(2)}, u32[]{:S(2)}) collective-permute-start(f32[100,8,128]{2,1,0:T(8,128)S(1)} %get-tuple-element.28), channel_id=1, source_target_pairs={{32,160},{160,32},{64,192},{192,64},{33,161},{161,33},{65,193},{19... | collective-permute-start | bytes 1228808 | tf_op jit(solution)/shard_map/ppermute | solution.py:571
  68.9 21.4 %collective-permute-start.10 = (f32[160,8,128]{2,1,0:T(8,128)S(1)}, f32[160,8,128]{2,1,0:T(8,128)S(1)}, u32[]{:S(2)}, u32[]{:S(2)}) collective-permute-start(f32[160,8,128]{2,1,0:T(8,128)S(1)} %get-tuple-element.34), channel_id=1, source_target_pairs={{32,64},{64,32},{33,65},{65,33},{34,66},{66,34},{35,67},{67,35},{3... | collective-permute-start | bytes 1966088 | tf_op jit(solution)/shard_map/ppermute | solution.py:576
  73.9 16.5 %collective-permute-start.9 = (f32[88,8,128]{2,1,0:T(8,128)S(1)}, f32[88,8,128]{2,1,0:T(8,128)S(1)}, u32[]{:S(2)}, u32[]{:S(2)}) collective-permute-start(f32[88,8,128]{2,1,0:T(8,128)S(1)} %get-tuple-element.32), channel_id=1, source_target_pairs={{1,2},{2,1},{3,4},{4,3},{5,6},{6,5},{7,8},{8,7},{9,10},{10,9},{11,... | collective-permute-start | bytes 1081352 | tf_op jit(solution)/shard_map/ppermute | solution.py:574
  78.6 11.8 %collective-permute-start.8 = (f32[88,8,128]{2,1,0:T(8,128)S(1)}, f32[88,8,128]{2,1,0:T(8,128)S(1)}, u32[]{:S(2)}, u32[]{:S(2)}) collective-permute-start(f32[88,8,128]{2,1,0:T(8,128)S(1)} %get-tuple-element.29.token), channel_id=1, source_target_pairs={{0,1},{1,0},{2,3},{3,2},{4,5},{5,4},{6,7},{7,6},{8,9},{9,8},{10,11... | collective-permute-start | bytes 1081352 | tf_op jit(solution)/shard_map/ppermute | solution.py:573
  78.7 11.6 %collective-permute-start.7 = (f32[80,8,128]{2,1,0:T(8,128)S(1)}, f32[80,8,128]{2,1,0:T(8,128)S(1)}, u32[]{:S(2)}, u32[]{:S(2)}) collective-permute-start(f32[80,8,128]{2,1,0:T(8,128)S(1)} %get-tuple-element.31), channel_id=1, source_target_pairs={{0,128},{128,0},{1,129},{129,1},{2,130},{130,2},{3,131},{131,3},{4... | collective-permute-start | bytes 983048 | tf_op jit(solution)/shard_map/ppermute | solution.py:577
